TPU v7x, 32 devices: a whole 2x2x4 slice. The times are simulated.
32 devices in a mesh: img: 4 (over y, x), sp: 8 (over z, core).
Axes of the slice: x: 2, y: 2, z: 4, core: 2. Of those that a mesh axis runs over, the one named last changes fastest.
Arguments:
- image_in: bfloat16 [4, 64, 64, 512], P('img', 'sp'), may hold values from -16 to 16
- time_embed: bfloat16 [4, 2048], P('img'), may hold values from -6 to 6
- caption: bfloat16 [4, 128, 2048], P('img'), may hold values from -6 to 6
- caption_mask: int32 [4, 128], P('img'), may hold values 0 or 1
- conv_in: bfloat16 [512, 3, 3, 512], P('img', None, None, 'sp'), may hold values from -0.09375 to 0.09375
- conv_out: bfloat16 [512, 3, 3, 512], P('img', None, None, 'sp'), may hold values from -0.09375 to 0.09375
- embed_proj: bfloat16 [2048, 1024], P('img', 'sp'), may hold values from -0.125 to 0.125
- qkv_proj: bfloat16 [512, 1536], P('img', 'sp'), may hold values from -0.25 to 0.25
- caption_proj: bfloat16 [2048, 1024], P('img', 'sp'), may hold values from -0.125 to 0.125
- out_proj: bfloat16 [512, 512], P('img', 'sp'), may hold values from -2 to 2
- norm_gains: bfloat16 [3, 512], P(None, 'img'), may hold values from 0.099609375 to 1.8984375
- norm_biases: bfloat16 [3, 512], P(None, 'img'), may hold values from -3 to 3
- cotangent: bfloat16 [4, 64, 64, 512], P('img', 'sp'), may hold values from -16 to 16
Outputs:
- output: bfloat16 [4, 64, 64, 512], P('img', 'sp')
- grad_image: float32 [4, 64, 64, 512], P('img', 'sp')
- grad_embed: float32 [4, 2048], P('img')
- grad_caption: float32 [4, 128, 2048], P('img', 'sp')
- grad_conv_in: float32 [512, 3, 3, 512], P('img', None, None, 'sp')
- grad_conv_out: float32 [512, 3, 3, 512], P('img', None, None, 'sp')
- grad_embed_proj: float32 [2048, 1024], P('img', 'sp')
- grad_qkv_proj: float32 [512, 1536], P('img', 'sp')
- grad_caption_proj: float32 [2048, 1024], P('img', 'sp')
- grad_out_proj: float32 [512, 512], P('img', 'sp')
- grad_norm_gains: float32 [3, 512], P(None, 'img')
- grad_norm_biases: float32 [3, 512], P(None, 'img')
All inputs are finite; a program needn't handle non-finite values. No bound on the sum of `caption_mask` on one device may be relied on, other than what follows from the above.
Results may differ from a plain program's by a relative error of at most 0.011.
Values may be sent and summed in bfloat16 or wider, within the bound.
A program may use at most 256 MiB of HBM per device.

v0:
```python
import jax
import jax.numpy as jnp
from jax import lax
from jax.sharding import PartitionSpec as P

HEADS = 8
GROUPS = 32


EPSILON = 1e-05
PRECISE = lax.Precision.HIGHEST
MASKED = -1e30


def padded_2(cells, sides, width):
    for axis, dim in sides:
        count = lax.axis_size(axis)
        ends = count - 1
        head = lax.slice_in_dim(cells, 0, width, axis=dim)
        tail = lax.slice_in_dim(cells, cells.shape[dim] - width, cells.shape[dim], axis=dim)
        cells = jnp.concatenate(
            [
                lax.ppermute(tail, axis, [(i, (i + 1) % count) for i in range(ends)]),
                cells,
                lax.ppermute(head, axis, [((i + 1) % count, i) for i in range(ends)]),
            ],
            axis=dim,
        )
    return cells


def sigmoid_linear(values):
    return values * jax.nn.sigmoid(values)


def sigmoid_slope(values):
    gating = jax.nn.sigmoid(values)
    return gating * (1.0 + values * (1.0 - gating))


def grouped_view(tensor):
    return tensor.reshape(tensor.shape[:-1] + (GROUPS, tensor.shape[-1] // GROUPS))


def spread_back(statistic):
    return statistic[:, None, None, :, None]


def norm_forward(tensor, norm_gain, norm_bias):
    grouped = grouped_view(tensor)
    members = grouped.shape[1] * grouped.shape[2] * grouped.shape[4] * lax.axis_size("sp")
    center = lax.psum(jnp.sum(grouped, axis=(1, 2, 4)), "sp") / members
    offset = grouped - spread_back(center)
    spread = lax.psum(jnp.sum(offset * offset, axis=(1, 2, 4)), "sp") / members
    inverse = lax.rsqrt(spread + EPSILON)
    normed = ((grouped - spread_back(center)) * spread_back(inverse)).reshape(tensor.shape)
    return (normed * norm_gain + norm_bias, normed, inverse)


def norm_sums(upstream, normed, norm_gain):
    slope = grouped_view(upstream * norm_gain)
    hat_grouped = grouped_view(normed)
    return (
        slope,
        hat_grouped,
        jnp.sum(slope, axis=(1, 2, 4)),
        jnp.sum(slope * hat_grouped, axis=(1, 2, 4)),
    )


def norm_finish(slope, hat_grouped, inverse, slope_total, cross_total, shape):
    members = slope.shape[1] * slope.shape[2] * slope.shape[4] * lax.axis_size("sp")
    result = spread_back(inverse) * (
        slope
        - spread_back(slope_total) / members
        - hat_grouped * spread_back(cross_total) / members
    )
    return result.reshape(shape)


def param_grads(upstream, normed):
    return (jnp.sum(upstream * normed, axis=(0, 1, 2)), jnp.sum(upstream, axis=(0, 1, 2)))


def norm_back(upstream, normed, inverse, norm_gain):
    slope, hat_grouped, slope_sum, cross_sum = norm_sums(upstream, normed, norm_gain)
    gain_part, bias_part = param_grads(upstream, normed)
    slope_total, cross_total, gain_total, bias_total = lax.psum(
        (slope_sum, cross_sum, gain_part, bias_part), "sp"
    )
    return (
        norm_finish(slope, hat_grouped, inverse, slope_total, cross_total, upstream.shape),
        gain_total,
        bias_total,
    )


def convolve_rows(activation, weight):
    padded = padded_2(activation, (("sp", 1),), 1)
    padded = jnp.pad(padded, ((0, 0), (0, 0), (1, 1), (0, 0)))
    height = activation.shape[1]
    width_len = activation.shape[2]
    summed = None
    for row_off in range(3):
        for col_off in range(3):
            partial_value = jnp.einsum(
                "nrwc,cd->nrwd",
                padded[:, row_off : row_off + height, col_off : col_off + width_len, :],
                weight[:, row_off, col_off, :],
                preferred_element_type=jnp.float32,
            )
            summed = partial_value if summed is None else summed + partial_value
    return (summed, padded)


def convolve_grad(padded, upstream):
    height = upstream.shape[1]
    width_len = upstream.shape[2]
    pieces = []
    for row_off in range(3):
        for col_off in range(3):
            pieces.append(
                jnp.einsum(
                    "nrwc,nrwd->cd",
                    padded[:, row_off : row_off + height, col_off : col_off + width_len, :],
                    upstream,
                    preferred_element_type=jnp.float32,
                )
            )
    stacked = jnp.stack(pieces, axis=1)
    return stacked.reshape(stacked.shape[0], 3, 3, stacked.shape[2])


def flipped(weight):
    return jnp.flip(weight, (1, 2)).transpose(3, 1, 2, 0)


def block_length():
    return 512


def score_block(queries, key_block, scale):
    return (
        jnp.einsum("nqhd,nkhd->nhqk", queries, key_block, preferred_element_type=jnp.float32)
        * scale
    )


def row_logsumexp(queries, image_keys, text_keys, text_keep, scale):
    text_scores = jnp.where(text_keep, score_block(queries, text_keys, scale), MASKED)
    row_peak = jnp.max(text_scores, axis=-1)
    row_mass = jnp.sum(jnp.exp(text_scores - row_peak[..., None]), axis=-1)
    length_all = image_keys.shape[1]
    block_len = block_length()

    def add_block(index, running):
        peak_old, mass_old = running
        key_block = lax.dynamic_slice_in_dim(image_keys, index * block_len, block_len, 1)
        scores = score_block(queries, key_block, scale)
        peak_new = jnp.maximum(peak_old, jnp.max(scores, axis=-1))
        mass_new = mass_old * jnp.exp(peak_old - peak_new) + jnp.sum(
            jnp.exp(scores - peak_new[..., None]), axis=-1
        )
        return (peak_new, mass_new)

    row_peak, row_mass = lax.fori_loop(0, length_all // block_len, add_block, (row_peak, row_mass))
    return row_peak + jnp.log(row_mass)


def attend_rows(
    queries, image_keys, image_values, text_keys, text_values, text_keep, log_mass, scale
):
    text_scores = jnp.where(text_keep, score_block(queries, text_keys, scale), MASKED)
    text_weights = jnp.exp(text_scores - log_mass[..., None]).astype(jnp.bfloat16)
    attended = jnp.einsum(
        "nhqk,nkhd->nqhd", text_weights, text_values, preferred_element_type=jnp.float32
    )
    length_all = image_keys.shape[1]
    block_len = block_length()

    def add_block(index, running):
        key_block = lax.dynamic_slice_in_dim(image_keys, index * block_len, block_len, 1)
        value_block = lax.dynamic_slice_in_dim(image_values, index * block_len, block_len, 1)
        weights = jnp.exp(score_block(queries, key_block, scale) - log_mass[..., None]).astype(
            jnp.bfloat16
        )
        return running + jnp.einsum(
            "nhqk,nkhd->nqhd", weights, value_block, preferred_element_type=jnp.float32
        )

    return lax.fori_loop(0, length_all // block_len, add_block, attended)


def score_grads(log_mass, upstream, row_dot, value_block, scores):
    probs = jnp.exp(scores - log_mass[..., None])
    prob_grad = jnp.einsum(
        "nqhd,nkhd->nhqk", upstream, value_block, preferred_element_type=jnp.float32
    )
    score_grad = (probs * (prob_grad - row_dot[..., None])).astype(jnp.bfloat16)
    return (probs, score_grad)


def attend_back(
    queries,
    image_keys,
    image_values,
    text_keys,
    text_values,
    text_keep,
    log_mass,
    upstream,
    row_dot,
    scale,
):

    def block_grads(key_block, value_block, scores):
        probs, score_grad = score_grads(log_mass, upstream, row_dot, value_block, scores)
        value_grad = jnp.einsum(
            "nhqk,nqhd->nkhd",
            probs.astype(jnp.bfloat16),
            upstream,
            preferred_element_type=jnp.float32,
        )
        query_part = (
            jnp.einsum("nhqk,nkhd->nqhd", score_grad, key_block, preferred_element_type=jnp.float32)
            * scale
        )
        key_grad = (
            jnp.einsum("nhqk,nqhd->nkhd", score_grad, queries, preferred_element_type=jnp.float32)
            * scale
        )
        return (query_part, key_grad, value_grad)

    text_scores = jnp.where(text_keep, score_block(queries, text_keys, scale), MASKED)
    query_grad, text_key_grad, text_value_grad = block_grads(text_keys, text_values, text_scores)
    length_all = image_keys.shape[1]
    block_len = block_length()
    key_buffer = jnp.zeros(image_keys.shape, jnp.float32)
    value_buffer = jnp.zeros(image_values.shape, jnp.float32)

    def add_block(index, running):
        query_acc, key_acc, value_acc = running
        start = index * block_len
        key_block = lax.dynamic_slice_in_dim(image_keys, start, block_len, 1)
        value_block = lax.dynamic_slice_in_dim(image_values, start, block_len, 1)
        query_part, key_grad, value_grad = block_grads(
            key_block, value_block, score_block(queries, key_block, scale)
        )
        return (
            query_acc + query_part,
            lax.dynamic_update_slice_in_dim(key_acc, key_grad, start, 1),
            lax.dynamic_update_slice_in_dim(value_acc, value_grad, start, 1),
        )

    query_grad, key_buffer, value_buffer = lax.fori_loop(
        0, length_all // block_len, add_block, (query_grad, key_buffer, value_buffer)
    )
    return (query_grad, key_buffer, value_buffer, text_key_grad, text_value_grad)


def gather_weights(shards):
    rows = (
        lax.all_gather(shards[0], "img", axis=0, tiled=True),
        lax.all_gather(shards[1], "img", axis=0, tiled=True),
        lax.all_gather(shards[2], "img", axis=0, tiled=True),
        lax.all_gather(shards[3], "img", axis=0, tiled=True),
        lax.all_gather(shards[4], "img", axis=0, tiled=True),
        lax.all_gather(shards[5], "img", axis=0, tiled=True),
        lax.all_gather(shards[6], "img", axis=1, tiled=True),
        lax.all_gather(shards[7], "img", axis=1, tiled=True),
    )
    whole = (
        lax.all_gather(rows[0], "sp", axis=3, tiled=True),
        lax.all_gather(rows[1], "sp", axis=3, tiled=True),
        lax.all_gather(rows[2], "sp", axis=1, tiled=True),
        lax.all_gather(rows[3], "sp", axis=1, tiled=True),
        lax.all_gather(rows[4], "sp", axis=1, tiled=True),
        lax.all_gather(rows[5], "sp", axis=1, tiled=True),
    )
    return (whole[0], whole[1], whole[2], whole[3], whole[4], whole[5], rows[6], rows[7])


def split_heads(tensor):
    return tensor.reshape(tensor.shape[0], tensor.shape[1], HEADS, tensor.shape[2] // HEADS)


def run_forward(image_in, time_embed, caption, caption_mask, weights):
    conv_in, conv_out, embed_proj, qkv_proj, caption_proj, out_proj, norm_gains, norm_biases = (
        weights
    )
    gains = norm_gains.astype(jnp.float32)
    biases = norm_biases.astype(jnp.float32)
    images = image_in.shape[0]
    channels = image_in.shape[3]
    local_len = image_in.shape[1] * image_in.shape[2]
    head_dim = channels // HEADS
    scale = head_dim ** (-0.5)
    image_f = image_in.astype(jnp.float32)
    first_norm, first_hat, first_inv = norm_forward(image_f, gains[0], biases[0])
    first_act = sigmoid_linear(first_norm).astype(jnp.bfloat16)
    hidden_one, first_pad = convolve_rows(first_act, conv_in)
    embedded = sigmoid_linear(time_embed.astype(jnp.float32)).astype(jnp.bfloat16)
    modulation = jnp.dot(embedded, embed_proj, preferred_element_type=jnp.float32)
    scale_term = modulation[:, None, None, :channels]
    shift_term = modulation[:, None, None, channels:]
    second_norm, second_hat, second_inv = norm_forward(hidden_one, gains[1], biases[1])
    second_pre = second_norm * (1.0 + scale_term) + shift_term
    second_act = sigmoid_linear(second_pre).astype(jnp.bfloat16)
    hidden_two, second_pad = convolve_rows(second_act, conv_out)
    residual = image_f + hidden_two
    third_norm, third_hat, third_inv = norm_forward(residual, gains[2], biases[2])
    normed = third_norm.astype(jnp.bfloat16).reshape(images, local_len, channels)
    projected = jnp.einsum(
        "ntc,cd->ntd", normed, qkv_proj, preferred_element_type=jnp.float32
    ).astype(jnp.bfloat16)
    own_keys = projected[..., channels : 2 * channels]
    own_values = projected[..., 2 * channels :]
    caption_kv = jnp.einsum(
        "nlc,cd->nld", caption, caption_proj, preferred_element_type=jnp.float32
    ).astype(jnp.bfloat16)
    image_keys, image_values = (
        lax.all_gather(own_keys, "sp", axis=1, tiled=True),
        lax.all_gather(own_values, "sp", axis=1, tiled=True),
    )
    query_heads = split_heads(projected[..., :channels])
    key_heads = split_heads(image_keys)
    value_heads = split_heads(image_values)
    text_key_heads = split_heads(caption_kv[..., :channels])
    text_value_heads = split_heads(caption_kv[..., channels:])
    text_keep = (caption_mask > 0)[:, None, None, :]
    log_mass = row_logsumexp(query_heads, key_heads, text_key_heads, text_keep, scale)
    attended_f = attend_rows(
        query_heads,
        key_heads,
        value_heads,
        text_key_heads,
        text_value_heads,
        text_keep,
        log_mass,
        scale,
    )
    attended = attended_f.reshape(images, local_len, channels).astype(jnp.bfloat16)
    output = residual + jnp.einsum(
        "ntc,cd->ntd", attended, out_proj, preferred_element_type=jnp.float32
    ).reshape(image_in.shape)
    saved = {
        "gains": gains,
        "first_norm": first_norm,
        "first_hat": first_hat,
        "first_inv": first_inv,
        "first_pad": first_pad,
        "embedded": embedded,
        "scale_term": scale_term,
        "second_norm": second_norm,
        "second_hat": second_hat,
        "second_inv": second_inv,
        "second_pre": second_pre,
        "second_pad": second_pad,
        "third_hat": third_hat,
        "third_inv": third_inv,
        "normed": normed,
        "query_heads": query_heads,
        "key_heads": key_heads,
        "value_heads": value_heads,
        "own_key_heads": split_heads(own_keys),
        "own_value_heads": split_heads(own_values),
        "text_key_heads": text_key_heads,
        "text_value_heads": text_value_heads,
        "text_keep": text_keep,
        "log_mass": log_mass,
        "attended_f": attended_f,
        "attended": attended,
    }
    return (output, saved)


def body(
    image_in,
    time_embed,
    caption,
    caption_mask,
    conv_in,
    conv_out,
    embed_proj,
    qkv_proj,
    caption_proj,
    out_proj,
    norm_gains,
    norm_biases,
    cotangent,
):
    shards = (
        conv_in,
        conv_out,
        embed_proj,
        qkv_proj,
        caption_proj,
        out_proj,
        norm_gains,
        norm_biases,
    )
    weights = gather_weights(shards)
    output, first_pass = run_forward(image_in, time_embed, caption, caption_mask, weights)
    again_weights = gather_weights(shards)
    _, saved = run_forward(image_in, time_embed, caption, caption_mask, again_weights)
    w_in, w_out, w_embed, w_qkv, w_caption, w_proj, unused_gains, unused_biases = again_weights
    gains = saved["gains"]
    images = image_in.shape[0]
    channels = image_in.shape[3]
    local_len = image_in.shape[1] * image_in.shape[2]
    head_dim = channels // HEADS
    scale = head_dim ** (-0.5)
    upstream_flat = cotangent.reshape(images, local_len, channels)
    grad_out = jnp.einsum(
        "ntc,ntd->cd", saved["attended"], upstream_flat, preferred_element_type=jnp.float32
    )
    attended_grad = jnp.einsum(
        "ntd,cd->ntc", upstream_flat, w_proj, preferred_element_type=jnp.float32
    ).astype(jnp.bfloat16)
    grad_heads = attended_grad.reshape(images, local_len, HEADS, head_dim)
    row_dot = jnp.sum(grad_heads.astype(jnp.float32) * saved["attended_f"], axis=-1).transpose(
        0, 2, 1
    )
    query_grad, key_grad, value_grad, text_key_grad, text_value_grad = attend_back(
        saved["query_heads"],
        saved["key_heads"],
        saved["value_heads"],
        saved["text_key_heads"],
        saved["text_value_heads"],
        saved["text_keep"],
        saved["log_mass"],
        grad_heads,
        row_dot,
        scale,
    )
    full_len = key_grad.shape[1]
    text_len = text_key_grad.shape[1]
    own_key_grad, own_value_grad, own_text_key, own_text_value = (
        lax.psum_scatter(
            key_grad.reshape(images, full_len, channels), "sp", scatter_dimension=1, tiled=True
        ),
        lax.psum_scatter(
            value_grad.reshape(images, full_len, channels), "sp", scatter_dimension=1, tiled=True
        ),
        lax.psum_scatter(
            text_key_grad.reshape(images, text_len, channels), "sp", scatter_dimension=1, tiled=True
        ),
        lax.psum_scatter(
            text_value_grad.reshape(images, text_len, channels),
            "sp",
            scatter_dimension=1,
            tiled=True,
        ),
    )
    projected_grad = jnp.concatenate(
        [
            query_grad.reshape(images, local_len, channels).astype(jnp.bfloat16),
            own_key_grad.astype(jnp.bfloat16),
            own_value_grad.astype(jnp.bfloat16),
        ],
        axis=-1,
    )
    grad_qkv = jnp.einsum(
        "ntc,ntd->cd", saved["normed"], projected_grad, preferred_element_type=jnp.float32
    )
    normed_grad = jnp.einsum(
        "ntd,cd->ntc", projected_grad, w_qkv, preferred_element_type=jnp.float32
    ).reshape(image_in.shape)
    caption_grad_kv = jnp.concatenate([own_text_key, own_text_value], axis=-1).astype(jnp.bfloat16)
    text_rows = own_text_key.shape[1]
    own_caption = lax.dynamic_slice_in_dim(caption, lax.axis_index("sp") * text_rows, text_rows, 1)
    grad_caption_proj = jnp.einsum(
        "nlc,nld->cd", own_caption, caption_grad_kv, preferred_element_type=jnp.float32
    )
    grad_caption = jnp.einsum(
        "nld,cd->nlc", caption_grad_kv, w_caption, preferred_element_type=jnp.float32
    )
    third_back, gain_three, bias_three = norm_back(
        normed_grad, saved["third_hat"], saved["third_inv"], gains[2]
    )
    residual_grad = cotangent.astype(jnp.float32) + third_back
    hidden_two_grad = residual_grad.astype(jnp.bfloat16)
    grad_conv_out = convolve_grad(saved["second_pad"], hidden_two_grad)
    second_act_grad, unused_pad = convolve_rows(hidden_two_grad, flipped(w_out))
    second_pre_grad = second_act_grad * sigmoid_slope(saved["second_pre"])
    scale_part = jnp.sum(second_pre_grad * saved["second_norm"], axis=(1, 2))
    shift_part = jnp.sum(second_pre_grad, axis=(1, 2))
    second_norm_grad = second_pre_grad * (1.0 + saved["scale_term"])
    slope, hat_grouped, slope_sum, cross_sum = norm_sums(
        second_norm_grad, saved["second_hat"], gains[1]
    )
    gain_two_part, bias_two_part = param_grads(second_norm_grad, saved["second_hat"])
    slope_total, cross_total, scale_total, shift_total, gain_two, bias_two = lax.psum(
        (slope_sum, cross_sum, scale_part, shift_part, gain_two_part, bias_two_part), "sp"
    )
    hidden_one_f = norm_finish(
        slope, hat_grouped, saved["second_inv"], slope_total, cross_total, image_in.shape
    )
    modulation_part = jnp.concatenate([scale_part, shift_part], axis=-1)
    modulation_grad = jnp.concatenate([scale_total, shift_total], axis=-1)
    grad_embed_proj = jnp.einsum(
        "ne,nd->ed", saved["embedded"].astype(jnp.float32), modulation_part, precision=PRECISE
    )
    embed_f = time_embed.astype(jnp.float32)
    grad_embed = jnp.einsum(
        "nd,ed->ne", modulation_grad, w_embed.astype(jnp.float32), precision=PRECISE
    ) * sigmoid_slope(embed_f)
    hidden_one_grad = hidden_one_f.astype(jnp.bfloat16)
    grad_conv_in = convolve_grad(saved["first_pad"], hidden_one_grad)
    first_act_grad, unused_rims = convolve_rows(hidden_one_grad, flipped(w_in))
    first_norm_grad = first_act_grad * sigmoid_slope(saved["first_norm"])
    first_back, gain_one, bias_one = norm_back(
        first_norm_grad, saved["first_hat"], saved["first_inv"], gains[0]
    )
    grad_image = residual_grad + first_back
    grad_gains = jnp.stack([gain_one, gain_two, gain_three], axis=0)
    grad_biases = jnp.stack([bias_one, bias_two, bias_three], axis=0)
    columns = (
        lax.psum_scatter(grad_conv_in, "sp", scatter_dimension=3, tiled=True),
        lax.psum_scatter(grad_conv_out, "sp", scatter_dimension=3, tiled=True),
        lax.psum_scatter(grad_embed_proj, "sp", scatter_dimension=1, tiled=True),
        lax.psum_scatter(grad_qkv, "sp", scatter_dimension=1, tiled=True),
        lax.psum_scatter(grad_caption_proj, "sp", scatter_dimension=1, tiled=True),
        lax.psum_scatter(grad_out, "sp", scatter_dimension=1, tiled=True),
    )
    sharded = (
        lax.psum_scatter(columns[0], "img", scatter_dimension=0, tiled=True),
        lax.psum_scatter(columns[1], "img", scatter_dimension=0, tiled=True),
        lax.psum_scatter(columns[2], "img", scatter_dimension=0, tiled=True),
        lax.psum_scatter(columns[3], "img", scatter_dimension=0, tiled=True),
        lax.psum_scatter(columns[4], "img", scatter_dimension=0, tiled=True),
        lax.psum_scatter(columns[5], "img", scatter_dimension=0, tiled=True),
        lax.psum_scatter(grad_gains, "img", scatter_dimension=1, tiled=True),
        lax.psum_scatter(grad_biases, "img", scatter_dimension=1, tiled=True),
    )
    return (
        output.astype(jnp.bfloat16),
        grad_image,
        grad_embed,
        grad_caption,
        sharded[0],
        sharded[1],
        sharded[2],
        sharded[3],
        sharded[4],
        sharded[5],
        sharded[6],
        sharded[7],
    )


def solution(mesh):
    placed = (
        P("img", "sp", None, None),
        P("img", None),
        P("img", None, None),
        P("img", None),
        P("img", None, None, "sp"),
        P("img", None, None, "sp"),
        P("img", "sp"),
        P("img", "sp"),
        P("img", "sp"),
        P("img", "sp"),
        P(None, "img"),
        P(None, "img"),
        P("img", "sp", None, None),
    )
    return jax.shard_map(
        body,
        mesh=mesh,
        in_specs=placed,
        out_specs=(
            P("img", "sp", None, None),
            P("img", "sp", None, None),
            P("img", None),
            P("img", "sp", None),
            P("img", None, None, "sp"),
            P("img", None, None, "sp"),
            P("img", "sp"),
            P("img", "sp"),
            P("img", "sp"),
            P("img", "sp"),
            P(None, "img"),
            P(None, "img"),
        ),
        check_vma=False,
    )
```

profile of v0, /device:TPU:0, one launch (start us, length us, event | category | flops | bytes accessed | tf_op | source)
XLA Modules:
  0.0 1456.8 jit_solution(2777755272312460576)
XLA Ops:
  54.6 13.9 psum.158
  69.1 14.1 psum.159
  129.2 14.9 %psum.160 = f32[1,32]{1,0:T(1,128)S(1)} all-reduce(f32[1,32]{1,0:T(1,128)S(1)} %bitcast.905), channel_id=1, replica_groups=mesh['img'=4,'sp'=8] {'sp'}, use_global_device_ids=true, to_apply=%region_8.9 | all-reduce | flops 32 | bytes 256 | tf_op jit(solution)/shard_map/psum | solution.py:52
  144.7 14.2 psum.161
  182.6 15.0 %psum.162 = f32[1,32]{1,0:T(1,128)S(1)} all-reduce(f32[1,32]{1,0:T(1,128)S(1)} %bitcast.907), channel_id=1, replica_groups=mesh['img'=4,'sp'=8] {'sp'}, use_global_device_ids=true, to_apply=%region_14.15 | all-reduce | flops 32 | bytes 256 | tf_op jit(solution)/shard_map/psum | solution.py:52
  224.6 19.2 %all_gather.79 = bf16[512,512]{0,1:T(8,128)(2,1)S(1)} all-gather(bf16[512,64]{0,1:T(8,128)(2,1)S(1)} %all_gather.78), channel_id=1, replica_groups=mesh['img'=4,'sp'=8] {'sp'}, dimensions={1}, use_global_device_ids=true | all-gather | bytes 589824 | tf_op jit(solution)/shard_map/all_gather | solution.py:278
  259.0 41.3 %all-gather.18.cloned.1.call-done = bf16[1,4096,512]{2,1,0:T(8,128)(2,1)} async-done(((bf16[1,512,512]{2,1,0:T(8,128)(2,1)}), bf16[1,4096,512]{2,1,0:T(8,128)(2,1)}) %all-gather.18.cloned.1.call-update) | async-done | bytes 4194320 | tf_op jit(solution)/shard_map/all_gather | solution.py:322
  306.6 30.6 %while.13 = (s32[]{:T(128)}, f32[1,8,512]{2,1,0:T(8,128)S(1)}, f32[1,8,512]{2,1,0:T(8,128)S(1)}, bf16[1,4096,8,64]{1,3,2,0:T(8,128)(2,1)}, bf16[1,512,8,64]{1,3,...) while((s32[]{:T(128)}, f32[1,8,512]{2,1,0:T(8,128)S(1)}, ...), condition=%wide.region_23.24_spmd, body=%wide.region_20.0_spmd.sunk | while | flops 278929408 | bytes 18038928 | solution.py:166
  354.7 28.4 %while.14 = (s32[]{:T(128)}, f32[1,512,8,64]{1,3,2,0:T(8,128)S(1)}, bf16[1,4096,8,64]{1,3,2,0:T(8,128)(2,1)}, bf16[1,4096,8,64]{1,3,2,0:T(8,128)(2,1)}, bf16[1,5...) while((s32[]{:T(128)}, f32[1,512,8,64]{1,3,2,0:T(8,128)S(1)}, ...), condition=%wide.region_25.26_spmd, body=%wide.region_24.25_spmd.sunk | while | flops 543424512 | bytes 3687571 | solution.py:191
  396.0 102.3 %while.58 = (s32[]{:T(128)}, f32[1,512,8,64]{1,3,2,0:T(8,128)S(1)}, f32[1,4096,8,64]{1,3,2,0:T(8,128)}, f32[1,4096,8,64]{1,3,2,0:T(8,128)}, bf16[1,4096,8,64]{1,...) while((s32[]{:T(128)}, f32[1,512,8,64]{1,3,2,0:T(8,128)S(1)}, ...), condition=%wide.region_28.29_spmd, body=%wide.region_27.28_spmd.sunk | while | flops 1359740928 | bytes 45662404 | solution.py:255
  502.6 84.2 %reduce-scatter.23.cloned.1.call-done = f32[1,512,512]{1,2,0:T(8,128)} async-done(((f32[1,4096,512]{1,2,0:T(8,128)}), f32[1,512,512]{1,2,0:T(8,128)}) %reduce-scatter.23.cloned.1.call-update) | async-done | bytes 1048592 | tf_op jit(solution)/shard_map/reduce_scatter | solution.py:442
  588.9 88.2 %reduce-scatter.21.cloned.1.call-done = f32[1,512,512]{1,2,0:T(8,128)} async-done(((f32[1,4096,512]{1,2,0:T(8,128)}), f32[1,512,512]{1,2,0:T(8,128)}) %reduce-scatter.21.cloned.1.call-update) | async-done | bytes 1048592 | tf_op jit(solution)/shard_map/reduce_scatter | solution.py:439
  728.3 15.7 %all-reduce.7 = (f32[32]{0:T(128)S(1)}, f32[1,32]{1,0:T(1,128)S(1)}) all-reduce(f32[32]{0:T(128)S(1)} %reduce_sum.401, f32[1,32]{1,0:T(1,128)S(1)} %bitcast.902), channel_id=1, replica_groups=mesh['img'=4,'sp'=8] {'sp'}, use_global_device_ids=true, to_apply=%region_42.43 | all-reduce | flops 64 | bytes 512 | tf_op jit(solution)/shard_map/psum | solution.py:493
  763.5 158.6 %all-reduce.10 = (f32[32]{0:T(128)}, f32[1,32]{1,0:T(1,128)}, f32[1,512]{1,0:T(1,128)}, f32[1,512]{1,0:T(1,128)}, bf16[1,128,512]{2,0,1:T(2,128)(2,1)S(1)}, /*in...) all-reduce(f32[32]{0:T(128)S(1)} %reduce_sum.409, ...), channel_id=1, replica_groups=mesh['img'=4,'sp'=8] {'sp'}, use_global_device_ids=true, to_apply=%region_48.49 | all-reduce | flops 135232 | bytes 819712 | tf_op jit(solution)/shard_map/psum | solution.py:88
  973.6 41.7 %reduce-scatter.41.cloned.1.call-done = f32[2048,128]{1,0:T(8,128)} async-done(((f32[2048,1024]{1,0:T(8,128)}), f32[2048,128]{1,0:T(8,128)}) %reduce-scatter.41.cloned.1.call-update) | async-done | bytes 1048592 | tf_op jit(solution)/shard_map/reduce_scatter | solution.py:523
  1015.4 100.0 %reduce-scatter.29.cloned.1.call-done = f32[512,3,3,64]{0,3,2,1:T(8,128)} async-done(((f32[512,3,3,512]{0,3,2,1:T(8,128)}), f32[512,3,3,64]{0,3,2,1:T(8,128)}) %reduce-scatter.29.cloned.1.call-update) | async-done | bytes 1179664 | tf_op jit(solution)/shard_map/reduce_scatter | solution.py:520
  1115.7 99.7 %reduce-scatter.25.cloned.1.call-done = f32[512,3,3,64]{0,3,2,1:T(8,128)} async-done(((f32[512,3,3,512]{0,3,2,1:T(8,128)}), f32[512,3,3,64]{0,3,2,1:T(8,128)}) %reduce-scatter.25.cloned.1.call-update) | async-done | bytes 1179664 | tf_op jit(solution)/shard_map/reduce_scatter | solution.py:519
  1242.0 25.5 %reduce-scatter.51.cloned.1.call-done = f32[128,3]{1,0:T(8,128)} async-done(((f32[512,3]{1,0:T(8,128)}), f32[128,3]{1,0:T(8,128)}) %reduce-scatter.51.cloned.1.call-update) | async-done | bytes 1552
  1269.0 25.6 %reduce-scatter.47.cloned.1.call-done = f32[128,64]{0,1:T(8,128)} async-done(((f32[512,64]{0,1:T(8,128)}), f32[128,64]{0,1:T(8,128)}) %reduce-scatter.47.cloned.1.call-update) | async-done | bytes 32784 | tf_op jit(solution)/shard_map/reduce_scatter | solution.py:532
  1294.5 28.0 %reduce-scatter.39.cloned.1.call-done = f32[128,192]{0,1:T(8,128)} async-done(((f32[512,192]{0,1:T(8,128)}), f32[128,192]{0,1:T(8,128)}) %reduce-scatter.39.cloned.1.call-update) | async-done | bytes 98320 | tf_op jit(solution)/shard_map/reduce_scatter | solution.py:530
  1322.6 31.3 %reduce-scatter.35.cloned.1.call-done = f32[512,128]{1,0:T(8,128)} async-done(((f32[2048,128]{1,0:T(8,128)}), f32[512,128]{1,0:T(8,128)}) %reduce-scatter.35.cloned.1.call-update) | async-done | bytes 262160 | tf_op jit(solution)/shard_map/reduce_scatter | solution.py:529
  1353.9 31.2 %reduce-scatter.43.cloned.1.call-done = f32[512,128]{1,0:T(8,128)} async-done(((f32[2048,128]{1,0:T(8,128)}), f32[512,128]{1,0:T(8,128)}) %reduce-scatter.43.cloned.1.call-update) | async-done | bytes 262160 | tf_op jit(solution)/shard_map/reduce_scatter | solution.py:531
  1385.1 32.3 %reduce-scatter.31.cloned.1.call-done = f32[128,3,3,64]{0,3,2,1:T(8,128)} async-done(((f32[512,3,3,64]{0,3,2,1:T(8,128)}), f32[128,3,3,64]{0,3,2,1:T(8,128)}) %reduce-scatter.31.cloned.1.call-update) | async-done | bytes 294928 | tf_op jit(solution)/shard_map/reduce_scatter | solution.py:528
  1417.5 32.3 %reduce-scatter.27.cloned.1.call-done = f32[128,3,3,64]{0,3,2,1:T(8,128)} async-done(((f32[512,3,3,64]{0,3,2,1:T(8,128)}), f32[128,3,3,64]{0,3,2,1:T(8,128)}) %reduce-scatter.27.cloned.1.call-update) | async-done | bytes 294928 | tf_op jit(solution)/shard_map/reduce_scatter | solution.py:527
  (504 shorter events, 511.8 us)
Async XLA Ops:
  7.2 106.0 %all-gather.10.cloned.1.call-start = ((), (), s32[]{:S(2)}) async-start(), calls=%async_computation.17 | async-start | bytes 4718592 | tf_op jit(solution)/shard_map/all_gather | solution.py:275
  20.6 100.8 %all-gather.8.cloned.1.call-start = ((), (), s32[]{:S(2)}) async-start(), calls=%async_computation.16 | async-start | bytes 5308416 | tf_op jit(solution)/shard_map/all_gather | solution.py:273
  32.5 142.1 %all-gather.12.cloned.1.call-start = ((), (), s32[]{:S(2)}) async-start(), calls=%async_computation.18 | async-start | bytes 5308416 | tf_op jit(solution)/shard_map/all_gather | solution.py:274
  43.8 168.3 %all-gather.16.cloned.1.call-start = ((), (), s32[]{:S(2)}) async-start(), calls=%async_computation.20 | async-start | bytes 1769472 | tf_op jit(solution)/shard_map/all_gather | solution.py:276
  53.2 200.2 %all-gather.14.cloned.1.call-start = ((), (), s32[]{:S(2)}) async-start(), calls=%async_computation.19 | async-start | bytes 4718592 | tf_op jit(solution)/shard_map/all_gather | solution.py:277
  98.9 14.0 collective-permute-start
  112.9 187.4 %all-gather.18.cloned.1.call-start = ((), (), s32[]{:S(2)}) async-start(), calls=%async_computation.21 | async-start | bytes 4718592 | tf_op jit(solution)/shard_map/all_gather | solution.py:322
  216.0 132.3 %all-gather.20.cloned.1.call-start = ((), (), s32[]{:S(2)}) async-start(), calls=%async_computation.22 | async-start | bytes 4718592 | tf_op jit(solution)/shard_map/all_gather | solution.py:323
  256.8 330.0 %reduce-scatter.23.cloned.1.call-start = ((), (), s32[]{:S(2)}) async-start(), calls=%async_computation.24 | async-start | bytes 9437184 | tf_op jit(solution)/shard_map/reduce_scatter | solution.py:442
  498.3 178.7 %reduce-scatter.21.cloned.1.call-start = ((), (), s32[]{:S(2)}) async-start(), calls=%async_computation.23 | async-start | bytes 9437184 | tf_op jit(solution)/shard_map/reduce_scatter | solution.py:439
  499.1 472.6 %reduce-scatter.45.cloned.1.call-start = ((), (), s32[]{:S(2)}) async-start(), calls=%async_computation.35 | async-start | bytes 1179648 | tf_op jit(solution)/shard_map/reduce_scatter | solution.py:524
  501.7 470.6 %reduce-scatter.37.cloned.1.call-start = ((), (), s32[]{:S(2)}) async-start(), calls=%async_computation.31 | async-start | bytes 3538944 | tf_op jit(solution)/shard_map/reduce_scatter | solution.py:522
  683.3 289.8 %reduce-scatter.33.cloned.1.call-start = ((), (), s32[]{:S(2)}) async-start(), calls=%async_computation.29 | async-start | bytes 9437184 | tf_op jit(solution)/shard_map/reduce_scatter | solution.py:521
  720.5 294.9 %reduce-scatter.41.cloned.1.call-start = ((), (), s32[]{:S(2)}) async-start(), calls=%async_computation.33 | async-start | bytes 9437184 | tf_op jit(solution)/shard_map/reduce_scatter | solution.py:523
  926.9 188.6 %reduce-scatter.29.cloned.1.call-start = ((), (), s32[]{:S(2)}) async-start(), calls=%async_computation.27 | async-start | bytes 10616832 | tf_op jit(solution)/shard_map/reduce_scatter | solution.py:520
  948.2 267.3 %reduce-scatter.25.cloned.1.call-start = ((), (), s32[]{:S(2)}) async-start(), calls=%async_computation.25 | async-start | bytes 10616832 | tf_op jit(solution)/shard_map/reduce_scatter | solution.py:519
  969.1 271.4 %reduce-scatter.49.cloned.1.call-start = ((), (), s32[]{:S(2)}) async-start(), calls=%async_computation.37 | async-start | bytes 327680
  970.7 296.8 %reduce-scatter.51.cloned.1.call-start = ((), (), s32[]{:S(2)}) async-start(), calls=%async_computation.38 | async-start | bytes 327680
  971.7 322.9 %reduce-scatter.47.cloned.1.call-start = ((), (), s32[]{:S(2)}) async-start(), calls=%async_computation.36 | async-start | bytes 163840 | tf_op jit(solution)/shard_map/reduce_scatter | solution.py:532
  972.2 350.3 %reduce-scatter.39.cloned.1.call-start = ((), (), s32[]{:S(2)}) async-start(), calls=%async_computation.32 | async-start | bytes 491520 | tf_op jit(solution)/shard_map/reduce_scatter | solution.py:530
  973.0 380.9 %reduce-scatter.35.cloned.1.call-start = ((), (), s32[]{:S(2)}) async-start(), calls=%async_computation.30 | async-start | bytes 1310720 | tf_op jit(solution)/shard_map/reduce_scatter | solution.py:529
  973.6 411.6 %reduce-scatter.43.cloned.1.call-start = ((), (), s32[]{:S(2)}) async-start(), calls=%async_computation.34 | async-start | bytes 1310720 | tf_op jit(solution)/shard_map/reduce_scatter | solution.py:531
  1015.4 402.1 %reduce-scatter.31.cloned.1.call-start = ((), (), s32[]{:S(2)}) async-start(), calls=%async_computation.28 | async-start | bytes 1474560 | tf_op jit(solution)/shard_map/reduce_scatter | solution.py:528
  1115.4 334.4 %reduce-scatter.27.cloned.1.call-start = ((), (), s32[]{:S(2)}) async-start(), calls=%async_computation.26 | async-start | bytes 1474560 | tf_op jit(solution)/shard_map/reduce_scatter | solution.py:527
  (81 other events, 2298.4 us)
Sparse Core Ops, SparseCore 0:
  20.7 48.2 all-gather.9
  70.7 50.6 all-gather.7
  123.0 51.5 all-gather.11
  176.1 24.3 all-gather.15
  201.8 51.4 all-gather.13
  254.8 45.4 all-gather.17
  302.4 45.8 all-gather.19
  498.5 88.2 reduce-scatter.22
  589.1 87.9 reduce-scatter.20
  679.2 31.0 reduce-scatter.44
  712.6 38.6 reduce-scatter.36
  753.4 157.1 reduce-scatter.32
  927.0 88.3 reduce-scatter.40
  1017.5 97.8 reduce-scatter.28
  1117.6 97.8 reduce-scatter.24
  1218.1 22.4 reduce-scatter.48
  1243.4 24.0 reduce-scatter.50
  1270.7 23.8 reduce-scatter.46
  1298.1 24.4 reduce-scatter.38
  1326.1 27.7 reduce-scatter.34
  1357.4 27.7 reduce-scatter.42
  1388.9 28.5 reduce-scatter.30
  1421.2 28.5 reduce-scatter.26
where the time goes:
time: 1470 us; the launch traced here: 1460 us
  waiting for transfers between devices  707 us (48%)
  blocking collectives  374 us (25%)
  matrix products  237 us (16%)
  local copies, waits for them, and re-layouts  75.5 us (5%)
  other arithmetic  33.5 us (2%)
  between operations  16.7 us (1%)
    psum x2, blocking collectives, norm_back(): lax.psum((slope_sum, cross_sum, gain_part, bias_part), 'sp')  172 us
    reduce_scatter x1, waiting for transfers between devices, body(): lax.psum_scatter(grad_conv_out, 'sp', scatter_dimension=3, tiled=True)  100 us
    reduce_scatter x1, waiting for transfers between devices, body(): lax.psum_scatter(grad_conv_in, 'sp', scatter_dimension=3, tiled=True)  99.7 us
    reduce_scatter x1, waiting for transfers between devices, body(): lax.psum_scatter(key_grad.reshape(images, full_len, channels), 'sp', scat...  88.2 us
    reduce_scatter x1, waiting for transfers between devices, body(): lax.psum_scatter(value_grad.reshape(images, full_len, channels), 'sp', sc...  84.2 us
    psum x3, blocking collectives, norm_forward(): center = lax.psum(jnp.sum(grouped, axis=(1, 2, 4)), 'sp') / members  43.9 us
    psum x3, blocking collectives, norm_forward(): spread = lax.psum(jnp.sum(offset * offset, axis=(1, 2, 4)), 'sp') / members  41.9 us
    reduce_scatter x1, waiting for transfers between devices, body(): lax.psum_scatter(grad_caption_proj, 'sp', scatter_dimension=1, tiled=True)  41.7 us
  transfers between devices with their start and end apart: 31, of which 20 were waited for; matrix products, arithmetic and copies ran while one was open for 13% of the time, Pallas kernels for 0%

commit v1 on v0

v1 whole, which is shorter than its diff:
```python
import jax
import jax.numpy as jnp
from jax import lax
from jax.sharding import PartitionSpec as P

HEADS = 8
GROUPS = 32
EPSILON = 1e-05
PRECISE = lax.Precision.HIGHEST
MASKED = -1e30
BF16 = jnp.bfloat16
F32 = jnp.float32


def dot(a, b, ca, cb):
    return lax.dot_general(a, b, (((ca,), (cb,)), ((), ())), preferred_element_type=F32)


def silu(v):
    return v * jax.nn.sigmoid(v)


def silu_slope(v):
    s = jax.nn.sigmoid(v)
    return s * (1.0 + v * (1.0 - s))


def gather(x, axis, dim):
    return lax.all_gather(x, axis, axis=dim, tiled=True)


def scatter_sum(x, axis, dim):
    return lax.psum_scatter(x, axis, scatter_dimension=dim, tiled=True)


def swap(x, axis, split, concat):
    return lax.all_to_all(x, axis, split, concat, tiled=True)


def halo(x):
    count = lax.axis_size("sp")
    above = lax.ppermute(x[:, -1:], "sp", [(i, i + 1) for i in range(count - 1)])
    below = lax.ppermute(x[:, :1], "sp", [(i + 1, i) for i in range(count - 1)])
    return above, below


def group_sum(v):
    c = v.shape[-1]
    g = v.reshape(v.shape[:-1] + (GROUPS, c // GROUPS))
    s = jnp.sum(g, axis=-1, keepdims=True)
    return jnp.broadcast_to(s, g.shape).reshape(v.shape)


def norm_stats(x):
    n, r, w, c = x.shape
    cells = r * w * (c // GROUPS)
    parts = lax.axis_size("sp")
    mean = group_sum(jnp.sum(x, axis=(1, 2))) / cells
    dev = group_sum(jnp.sum(jnp.square(x - mean[:, None, None, :]), axis=(1, 2)))
    both = lax.all_gather(jnp.stack([mean, dev]), "sp")
    means, devs = both[:, 0], both[:, 1]
    center = jnp.mean(means, axis=0)
    var = (jnp.sum(devs, axis=0) + cells * jnp.sum(jnp.square(means - center), axis=0)) / (
        cells * parts
    )
    return center, lax.rsqrt(var + EPSILON)


def hat_of(x, center, inverse):
    return (x - center[:, None, None, :]) * inverse[:, None, None, :]


def norm_back(u, hat, inverse, gain, sum_u, sum_uh, members):
    s1 = group_sum(sum_u * gain) / members
    s2 = group_sum(sum_uh * gain) / members
    return inverse[:, None, None, :] * (
        u * gain - s1[:, None, None, :] - hat * s2[:, None, None, :]
    )


def pad_cols(x):
    return jnp.pad(x, ((0, 0), (0, 0), (1, 1), (0, 0)))


def conv(padded, weight_t, transposed):
    n, rp, wp, c = padded.shape
    r, w = rp - 2, wp - 2
    total = None
    for i in range(3):
        for j in range(3):
            a = padded[:, i : i + r, j : j + w].reshape(n * r * w, c)
            part = dot(a, weight_t[2 - i, 2 - j], 1, 0) if transposed else dot(a, weight_t[i, j], 1, 1)
            total = part if total is None else total + part
    return total.reshape(n, r, w, -1)


def conv_grad(padded, g):
    n, r, w, c = g.shape
    gf = g.reshape(n * r * w, c)
    rows = []
    for i in range(3):
        for j in range(3):
            a = padded[:, i : i + r, j : j + w].reshape(n * r * w, -1)
            rows.append(dot(gf, a, 0, 0))
    return jnp.stack(rows).reshape(3, 3, c, -1)


def to_pairs(x, images):
    n, px, h, d = x.shape
    y = x.transpose(0, 2, 1, 3).reshape(n * h, px, d)
    return swap(y, "sp", 0, 1)


def from_pairs(x, images):
    y = swap(x, "sp", 1, 0)
    return y.reshape(images, HEADS, y.shape[1], y.shape[2]).transpose(0, 2, 1, 3)


def attention(q, k, v, g, tk, tv, keep, scale):
    p, length, d = q.shape
    block = min(512, length)
    keys = jnp.concatenate([tk, k], axis=1)
    values = jnp.concatenate([tv, v], axis=1)
    text = tk.shape[1]
    keep_all = jnp.concatenate([keep, jnp.ones((p, length), bool)], axis=1)

    def step(carry, blk):
        dk, dv = carry
        qb, gb = blk
        s = jnp.einsum("pqd,pkd->pqk", qb, keys, preferred_element_type=F32) * scale
        s = jnp.where(keep_all[:, None, :], s, MASKED)
        peak = jnp.max(s, axis=-1, keepdims=True)
        e = jnp.exp(s - peak)
        prob = e / jnp.sum(e, axis=-1, keepdims=True)
        pb = prob.astype(BF16)
        o = jnp.einsum("pqk,pkd->pqd", pb, values, preferred_element_type=F32)
        row = jnp.sum(o * gb.astype(F32), axis=-1, keepdims=True)
        dp = jnp.einsum("pqd,pkd->pqk", gb, values, preferred_element_type=F32)
        ds = (prob * (dp - row)).astype(BF16)
        dq = jnp.einsum("pqk,pkd->pqd", ds, keys, preferred_element_type=F32) * scale
        dk = dk + jnp.einsum("pqk,pqd->pkd", ds, qb, preferred_element_type=F32)
        dv = dv + jnp.einsum("pqk,pqd->pkd", pb, gb, preferred_element_type=F32)
        return (dk, dv), (o.astype(BF16), dq.astype(BF16))

    zeros = jnp.zeros((p, text + length, d), F32)
    cut = lambda t: t.reshape(p, length // block, block, d).swapaxes(0, 1)
    (dk, dv), (o, dq) = lax.scan(step, (zeros, zeros), (cut(q), cut(g)))
    join = lambda t: t.swapaxes(0, 1).reshape(p, length, d)
    dk = (dk * scale).astype(BF16)
    dv = dv.astype(BF16)
    return join(o), join(dq), dk[:, text:], dv[:, text:], dk[:, :text], dv[:, :text]


def body(
    image_in, time_embed, caption, caption_mask, conv_in, conv_out, embed_proj, qkv_proj,
    caption_proj, out_proj, norm_gains, norm_biases, cotangent,
):
    n, rows, width, chans = image_in.shape
    n_img, n_sp = lax.axis_size("img"), lax.axis_size("sp")
    img, sp = lax.axis_index("img"), lax.axis_index("sp")
    px = rows * width
    members = px * n_sp * (chans // GROUPS)
    d = chans // HEADS
    scale = d ** -0.5
    pairs = n * HEADS // n_sp

    def whole(w):
        w = gather(w, "img", w.ndim - 1)
        return gather(w, "sp", w.ndim - 2)

    w_in = whole(conv_in.transpose(1, 2, 3, 0))
    w_out = whole(conv_out.transpose(1, 2, 3, 0))
    w_qkv = whole(qkv_proj.T)
    w_proj = whole(out_proj.T)
    affine = gather(jnp.concatenate([norm_gains, norm_biases]), "img", 1).astype(F32)
    gains, biases = affine[:3], affine[3:]

    embedded = silu(time_embed.astype(F32)).astype(BF16)
    emb_all = swap(embedded, "img", 1, 0)
    mod = scatter_sum(jnp.dot(emb_all, embed_proj, preferred_element_type=F32), "img", 0)
    mod = gather(mod, "sp", 1)
    scale_term, shift_term = mod[:, :chans], mod[:, chans:]
    cap_all = swap(caption, "img", 2, 0)
    cap_flat = cap_all.reshape(-1, cap_all.shape[2])
    kv = jnp.dot(cap_flat, caption_proj, preferred_element_type=F32)
    kv = scatter_sum(kv.reshape(cap_all.shape[0], cap_all.shape[1], -1), "img", 0).astype(BF16)
    kv = gather(kv, "sp", 2)
    text = kv.shape[1]
    kv_heads = kv.reshape(n, text, 2, HEADS, d).transpose(2, 0, 3, 1, 4).reshape(2, n * HEADS, text, d)
    mine = lax.dynamic_slice_in_dim(kv_heads, sp * pairs, pairs, 1)
    keep = jnp.repeat(caption_mask > 0, HEADS, axis=0)
    keep = lax.dynamic_slice_in_dim(keep, sp * pairs, pairs, 0)

    image_f = image_in.astype(F32)
    c0, i0 = norm_stats(image_f)
    hat0 = hat_of(image_f, c0, i0)
    first = hat0 * gains[0] + biases[0]
    act0 = silu(first).astype(BF16)
    above, below = halo(act0)
    pad0 = pad_cols(jnp.concatenate([above, act0, below], axis=1))
    hidden = conv(pad0, w_in, False)
    c1, i1 = norm_stats(hidden)
    hat1 = hat_of(hidden, c1, i1)
    second = hat1 * gains[1] + biases[1]
    pre = second * (1.0 + scale_term[:, None, None, :]) + shift_term[:, None, None, :]
    act1 = silu(pre).astype(BF16)
    above, below = halo(act1)
    pad1 = pad_cols(jnp.concatenate([above, act1, below], axis=1))
    residual = image_f + conv(pad1, w_out, False)
    c2, i2 = norm_stats(residual)
    hat2 = hat_of(residual, c2, i2)
    normed = (hat2 * gains[2] + biases[2]).astype(BF16).reshape(n * px, chans)
    qkv = dot(normed, w_qkv, 1, 1).astype(BF16)
    cot = cotangent.reshape(n * px, chans)
    g_att = dot(cot, w_proj, 1, 0).astype(BF16)
    four = jnp.concatenate([qkv, g_att], axis=1).reshape(n, px, 4, HEADS, d)
    packed = to_pairs(four.transpose(0, 1, 3, 2, 4).reshape(n, px, HEADS, 4 * d), n)
    q, k, v, g = (packed[..., j * d : (j + 1) * d] for j in range(4))
    o, dq, dk, dv, dtk, dtv = attention(q, k, v, g, mine[0], mine[1], keep, scale)
    back = from_pairs(jnp.concatenate([o, dq, dk, dv], axis=-1), n)
    back = back.reshape(n * px, HEADS, 4, d).transpose(0, 2, 1, 3).reshape(n * px, 4 * chans)
    attended, proj_grad = back[:, :chans], back[:, chans:]
    output = residual + dot(attended, w_proj, 1, 1).reshape(image_in.shape)

    grad_out = dot(cot, attended, 0, 0)
    grad_qkv = dot(proj_grad, normed, 0, 0)
    normed_grad = dot(proj_grad, w_qkv, 1, 0).reshape(image_in.shape)

    def sums(u, hat):
        both = jnp.stack([jnp.sum(u, axis=(1, 2)), jnp.sum(u * hat, axis=(1, 2))])
        return lax.psum(both, "sp")

    su2, sh2 = sums(normed_grad, hat2)
    residual_grad = cotangent.astype(F32) + norm_back(
        normed_grad, hat2, i2, gains[2], su2, sh2, members
    )
    g2 = residual_grad.astype(BF16)
    above, below = halo(g2)
    gpad = pad_cols(jnp.concatenate([above, g2, below], axis=1))
    grad_conv_out = conv_grad(pad1, g2)
    pre_grad = conv(gpad, w_out, True) * silu_slope(pre)
    sa, sb = sums(pre_grad, hat1)
    fac = 1.0 + scale_term
    shift_grad = sa
    scale_grad = sb * gains[1] + sa * biases[1]
    u1 = pre_grad * fac[:, None, None, :]
    su1, sh1 = sa * fac, sb * fac
    g1 = norm_back(u1, hat1, i1, gains[1], su1, sh1, members).astype(BF16)
    above, below = halo(g1)
    gpad = pad_cols(jnp.concatenate([above, g1, below], axis=1))
    grad_conv_in = conv_grad(pad0, g1)
    u0 = conv(gpad, w_in, True) * silu_slope(first)
    su0, sh0 = sums(u0, hat0)
    grad_image = residual_grad + norm_back(u0, hat0, i0, gains[0], su0, sh0, members)

    mod_grad = jnp.concatenate([scale_grad, shift_grad], axis=1)
    cols = embed_proj.shape[1]
    mod_all = gather(mod_grad, "img", 0)
    mod_cols = lax.dynamic_slice_in_dim(mod_all, sp * cols, cols, 1)
    grad_embed_proj = jnp.einsum("ne,nd->ed", emb_all.astype(F32), mod_cols, precision=PRECISE)
    part = jnp.einsum("nd,ed->ne", mod_cols, embed_proj.astype(F32), precision=PRECISE)
    part = swap(lax.psum(part, "sp"), "img", 0, 1)
    grad_embed = part * silu_slope(time_embed.astype(F32))

    tg = gather(jnp.stack([dtk, dtv]), "sp", 1).reshape(2, n, HEADS, text, d)
    tg = tg.transpose(1, 3, 0, 2, 4).reshape(n, text, 2 * chans)
    cols = caption_proj.shape[1]
    tg = gather(lax.dynamic_slice_in_dim(tg, sp * cols, cols, 2), "img", 0).reshape(-1, cols)
    grad_caption_proj = dot(cap_flat, tg, 0, 0)
    gc = dot(tg, caption_proj, 1, 1).reshape(cap_all.shape)
    gc = scatter_sum(gc, "sp", 1)
    grad_caption = swap(gc, "img", 0, 2)

    grads = jnp.concatenate(
        [jnp.sum(t, axis=0)[None] for t in (sh0, sh1, sh2, su0, su1, su2)]
    )
    grads = scatter_sum(grads, "img", 1)

    def shared(w):
        w = scatter_sum(w, "sp", w.ndim - 2)
        return scatter_sum(w, "img", w.ndim - 1)

    return (
        output.astype(BF16),
        grad_image,
        grad_embed,
        grad_caption,
        shared(grad_conv_in).transpose(3, 0, 1, 2),
        shared(grad_conv_out).transpose(3, 0, 1, 2),
        grad_embed_proj,
        shared(grad_qkv).T,
        grad_caption_proj,
        shared(grad_out).T,
        grads[:3],
        grads[3:],
    )


def solution(mesh):
    rows = P("img", "sp", None, None)
    kernel = P("img", None, None, "sp")
    flat = P("img", "sp")
    return jax.shard_map(
        body,
        mesh=mesh,
        in_specs=(
            rows, P("img", None), P("img", None, None), P("img", None), kernel, kernel,
            flat, flat, flat, flat, P(None, "img"), P(None, "img"), rows,
        ),
        out_specs=(
            rows, rows, P("img", None), P("img", "sp", None), kernel, kernel,
            flat, flat, flat, flat, P(None, "img"), P(None, "img"),
        ),
        check_vma=False,
    )
```

time: 1470 us -> 1070 us (0.73)
  waiting for transfers between devices: 707 us -> 297 us
  blocking collectives: 374 us -> 307 us
  other arithmetic: 33.5 us -> 87.4 us
  local copies, waits for them, and re-layouts: 75.5 us -> 99.4 us
  matrix products: 237 us -> 216 us
  starting transfers between devices: 12.6 us -> 32.3 us
    reduce_scatter x14 -> x9, waiting for transfers between devices: 595 us -> 269 us  [scatter_sum(): return lax.psum_scatter(x, axis, scatter_dimension=dim, tiled=True)]
    psum x9 -> x3, blocking collectives: 274 us -> 60.8 us  [sums(): return lax.psum(both, 'sp')]
    all_gather x9 -> x14, blocking collectives: 99.7 us -> 181 us  [the longest x11 138 us: gather(): return lax.all_gather(x, axis, axis=dim, tiled=True)]
    all_gather x7 -> x3, waiting for transfers between devices: 73.5 us -> 0.02 us  [gather(): return lax.all_gather(x, axis, axis=dim, tiled=True)]
    all_to_all x0 -> x1, blocking collectives: none -> 53.1 us  [swap(): return lax.all_to_all(x, axis, split, concat, tiled=True)]
    unnamed x0 -> x8, other arithmetic: none -> 34.1 us
    dot_general x127 -> x114, matrix products: 237 us -> 216 us  [the longest x62 56.6 us: dot(): lax.dot_general(a, b, (((ca,), (cb,)), ((), ())), preferred_element_type=...]
    all_to_all x0 -> x5, starting transfers between devices: none -> 19.4 us  [swap(): return lax.all_to_all(x, axis, split, concat, tiled=True)]
  transfers between devices with their start and end apart: 31 -> 27, of which waited for: 20 -> 12; matrix products, arithmetic and copies ran while one was open for 13% -> 12% of each run, Pallas kernels for 0% -> 0%
where the time goes in v1:
time: 1070 us; the launch traced here: 1060 us
  blocking collectives  307 us (29%)
  waiting for transfers between devices  297 us (28%)
  matrix products  216 us (20%)
  local copies, waits for them, and re-layouts  99.4 us (9%)
  other arithmetic  87.4 us (8%)
  starting transfers between devices  32.3 us (3%)
  between operations  17.7 us (2%)
    reduce_scatter x9, waiting for transfers between devices, scatter_sum(): return lax.psum_scatter(x, axis, scatter_dimension=dim, tiled=True)  269 us
    all_gather x11, blocking collectives, gather(): return lax.all_gather(x, axis, axis=dim, tiled=True)  138 us
    psum x3, blocking collectives, sums(): return lax.psum(both, 'sp')  60.8 us
    dot_general x62, matrix products, dot(): lax.dot_general(a, b, (((ca,), (cb,)), ((), ())), preferred_element_type=...  56.6 us
    all_to_all x1, blocking collectives, swap(): return lax.all_to_all(x, axis, split, concat, tiled=True)  53.1 us
    all_gather x3, blocking collectives, norm_stats(): both = lax.all_gather(jnp.stack([mean, dev]), 'sp')  42.9 us
    unnamed x210, local copies, waits for them, and re-layouts  39.1 us
    dot_general x8, matrix products, step(): dp = jnp.einsum('pqd,pkd->pqk', gb, values, preferred_element_type=F32)  38.4 us
  transfers between devices with their start and end apart: 27, of which 12 were waited for; matrix products, arithmetic and copies ran while one was open for 12% of the time, Pallas kernels for 0%

profile of v1, /device:TPU:0, one launch (start us, length us, event | category | flops | bytes accessed | tf_op | source)
XLA Modules:
  0.0 1057.8 jit_solution(2861045531652858509)
XLA Ops:
  8.1 13.6 %all_gather.63 = bf16[3,3,64,512]{3,2,1,0:T(8,128)(2,1)} all-gather(bf16[3,3,64,128]{3,2,1,0:T(8,128)(2,1)} %bitcast.670), channel_id=1, replica_groups=mesh['img'=4,'sp'=8] {'img'}, dimensions={3}, use_global_device_ids=true | all-gather | bytes 737280 | tf_op jit(solution)/shard_map/all_gather | solution.py:29
  21.8 11.8 %all_gather.68 = bf16[3,3,64,512]{3,2,1,0:T(8,128)(2,1)} all-gather(bf16[3,3,64,128]{3,2,1,0:T(8,128)(2,1)} %bitcast.671), channel_id=1, replica_groups=mesh['img'=4,'sp'=8] {'img'}, dimensions={3}, use_global_device_ids=true | all-gather | bytes 737280 | tf_op jit(solution)/shard_map/all_gather | solution.py:29
  44.0 14.6 %all-gather = f32[16,1,512]{2,1,0:T(1,128)S(1)} all-gather(f32[2,1,512]{2,1,0:T(1,128)S(1)} %pad_maximum_fusion.13), channel_id=2, replica_groups=mesh['img'=4,'sp'=8] {'sp'}, dimensions={0}, use_global_device_ids=true | all-gather | bytes 36864 | tf_op jit(solution)/shard_map/all_gather | solution.py:60
  88.0 19.2 %all_gather.75 = bf16[512,512]{1,0:T(8,128)(2,1)S(1)} all-gather(bf16[64,512]{1,0:T(8,128)(2,1)S(1)} %all_gather.74), channel_id=1, replica_groups=mesh['img'=4,'sp'=8] {'sp'}, dimensions={0}, use_global_device_ids=true | all-gather | bytes 589824 | tf_op jit(solution)/shard_map/all_gather | solution.py:29
  127.3 11.7 %all-reduce.5 = f32[4,128]{1,0:T(4,128)S(1)} all-reduce(f32[4,128]{1,0:T(4,128)S(1)} %fusion.129), channel_id=5, replica_groups=mesh['img'=4,'sp'=8] {'img'}, use_global_device_ids=true, to_apply=%region_14.15.clone | all-reduce | flops 512 | bytes 4096
  139.7 11.7 %all_gather.67 = f32[1,1024]{1,0:T(1,128)S(1)} all-gather(f32[1,128]{1,0:T(1,128)S(1)} %constant_dynamic-slice_fusion.3), channel_id=1, replica_groups=mesh['img'=4,'sp'=8] {'sp'}, dimensions={1}, use_global_device_ids=true | all-gather | bytes 4608 | tf_op jit(solution)/shard_map/all_gather | solution.py:29
  164.0 14.0 %all-gather.1 = f32[16,1,512]{2,1,0:T(1,128)S(1)} all-gather(f32[2,1,512]{2,1,0:T(1,128)S(1)} %pad_maximum_fusion.14), channel_id=3, replica_groups=mesh['img'=4,'sp'=8] {'sp'}, dimensions={0}, use_global_device_ids=true | all-gather | bytes 36864 | tf_op jit(solution)/shard_map/all_gather | solution.py:60
  196.7 14.3 %all-gather.2 = f32[16,1,512]{2,1,0:T(1,128)S(1)} all-gather(f32[2,1,512]{2,1,0:T(1,128)S(1)} %pad_maximum_fusion.15), channel_id=4, replica_groups=mesh['img'=4,'sp'=8] {'sp'}, dimensions={0}, use_global_device_ids=true | all-gather | bytes 36864 | tf_op jit(solution)/shard_map/all_gather | solution.py:60
  230.3 24.7 %reduce-scatter.36.cloned.1.call-done = f32[1,128,128]{2,1,0:T(8,128)} async-done(((f32[4,128,128]{2,1,0:T(8,128)}), f32[1,128,128]{2,1,0:T(8,128)}) %reduce-scatter.36.cloned.1.call-update) | async-done | bytes 65552
  255.9 26.5 %all_gather.76 = bf16[1,128,1024]{1,2,0:T(8,128)(2,1)S(1)} all-gather(bf16[1,128,128]{1,2,0:T(8,128)(2,1)S(1)} %copy.91), channel_id=1, replica_groups=mesh['img'=4,'sp'=8] {'sp'}, dimensions={2}, use_global_device_ids=true | all-gather | bytes 294912 | tf_op jit(solution)/shard_map/all_gather | solution.py:29
  292.7 202.8 %while.17 = (s32[]{:T(128)}, f32[1,4224,64]{1,2,0:T(8,128)S(1)}, f32[1,4224,64]{1,2,0:T(8,128)}, bf16[8,1,512,64]{2,3,1,0:T(8,128)(2,1)}, bf16[8,1,512,64]{2,3,1...) while((s32[]{:T(128)}, f32[1,4224,64]{1,2,0:T(8,128)S(1)}, ...), condition=%wide.region_27.28_spmd.clone, body=%wide.region_23.27_spmd.clone.sunk | while | flops 1688173056 | bytes 149976752 | solution.py:147
  505.9 22.0 %reduce.74 = bf16[4096,256]{1,0:T(8,128)(2,1)S(1)} reduce(bf16[4096,1,256]{2,1,0:T(2,128)(2,1)} %bitcast.591, bf16[]{:T(256)} %broadcast.968), dimensions={1}, to_apply=%bitcast.465.reduce_sub_computation | reduce | bytes 4194306
  531.1 53.1 %all_to_all.89 = bf16[8,2,65536]{2,1,0:T(2,128)(2,1)S(1)} all-to-all(bf16[8,2,65536]{2,1,0:T(2,128)(2,1)} %reshape.1274), channel_id=1, replica_groups=mesh['img'=4,'sp'=8] {'sp'}, dimensions={0} | all-to-all | bytes 4194304 | tf_op jit(solution)/shard_map/all_to_all | solution.py:37
  607.3 14.6 %psum.28 = f32[2,1,512]{2,1,0:T(1,128)S(1)} all-reduce(f32[2,1,512]{2,1,0:T(1,128)S(1)} %pad_maximum_fusion.16), channel_id=1, replica_groups=mesh['img'=4,'sp'=8] {'sp'}, use_global_device_ids=true, to_apply=%region_30.31 | all-reduce | flops 1024 | bytes 8192 | tf_op jit(solution)/shard_map/psum | solution.py:231
  635.5 15.2 %all_gather.78 = bf16[2,8,128,64]{2,3,1,0:T(8,128)(2,1)S(1)} all-gather(bf16[2,1,128,64]{2,3,1,0:T(8,128)(2,1)S(1)} %pad_maximum_fusion.12), channel_id=1, replica_groups=mesh['img'=4,'sp'=8] {'sp'}, dimensions={1}, use_global_device_ids=true | all-gather | bytes 294912 | tf_op jit(solution)/shard_map/all_gather | solution.py:29
  672.5 18.0 %psum.29 = f32[2,1,512]{2,1,0:T(1,128)S(1)} all-reduce(f32[2,1,512]{2,1,0:T(1,128)S(1)} %pad_maximum_fusion.17), channel_id=1, replica_groups=mesh['img'=4,'sp'=8] {'sp'}, use_global_device_ids=true, to_apply=%region_35.36 | all-reduce | flops 1024 | bytes 8192 | tf_op jit(solution)/shard_map/psum | solution.py:231
  722.9 28.1 %all-reduce.7 = (f32[2,1,512]{2,1,0:T(1,128)S(1)}, f32[4,1,512]{2,0,1:T(4,128)}) all-reduce(f32[2,1,512]{2,1,0:T(1,128)S(1)} %pad_maximum_fusion.18, f32[4,1,512]{2,0,1:T(4,128)S(1)} %convolution_bitcast_fusion.22), channel_id=1, replica_groups=mesh['img'=4,'sp'=8] {'sp'}, use_global_device_ids=true, to_apply=%region_40.41 | all-reduce | flops 3072 | bytes 24576 | tf_op jit(solution)/shard_map/psum | solution.py:231
  754.4 20.6 %reduce-scatter.22.cloned.1.call-done = f32[3,3,64,512]{3,2,1,0:T(8,128)} async-done(((f32[3,3,512,512]{3,2,1,0:T(8,128)}), f32[3,3,64,512]{3,2,1,0:T(8,128)}) %reduce-scatter.22.cloned.1.call-update) | async-done | bytes 1179664 | tf_op jit(solution)/shard_map/reduce_scatter | solution.py:33
  775.0 32.7 %reduce-scatter.16.cloned.1.call-done = f32[4,16,512]{2,1,0:T(8,128)} async-done(((f32[4,128,512]{2,1,0:T(8,128)}), f32[4,16,512]{2,1,0:T(8,128)}) %reduce-scatter.16.cloned.1.call-update) | async-done | bytes 131088 | tf_op jit(solution)/shard_map/reduce_scatter | solution.py:33
  811.6 96.4 %reduce-scatter.18.cloned.1.call-done = f32[3,3,64,512]{3,2,1,0:T(8,128)} async-done(((f32[3,3,512,512]{3,2,1,0:T(8,128)}), f32[3,3,64,512]{3,2,1,0:T(8,128)}) %reduce-scatter.18.cloned.1.call-update) | async-done | bytes 1179664 | tf_op jit(solution)/shard_map/reduce_scatter | solution.py:33
  933.1 25.6 %reduce-scatter.30.cloned.1.call-done = f32[64,128]{0,1:T(8,128)} async-done(((f32[64,512]{0,1:T(8,128)}), f32[64,128]{0,1:T(8,128)}) %reduce-scatter.30.cloned.1.call-update) | async-done | bytes 32784 | tf_op jit(solution)/shard_map/reduce_scatter | solution.py:33
  960.2 26.3 %reduce-scatter.28.cloned.1.call-done = f32[192,128]{1,0:T(8,128)} async-done(((f32[192,512]{1,0:T(8,128)}), f32[192,128]{1,0:T(8,128)}) %reduce-scatter.28.cloned.1.call-update) | async-done | bytes 98320 | tf_op jit(solution)/shard_map/reduce_scatter | solution.py:33
  986.5 31.9 %reduce-scatter.24.cloned.1.call-done = f32[3,3,64,128]{3,2,1,0:T(8,128)} async-done(((f32[3,3,64,512]{3,2,1,0:T(8,128)}), f32[3,3,64,128]{3,2,1,0:T(8,128)}) %reduce-scatter.24.cloned.1.call-update) | async-done | bytes 294928 | tf_op jit(solution)/shard_map/reduce_scatter | solution.py:33
  1018.4 32.0 %reduce-scatter.20.cloned.1.call-done = f32[3,3,64,128]{3,2,1,0:T(8,128)} async-done(((f32[3,3,64,512]{3,2,1,0:T(8,128)}), f32[3,3,64,128]{3,2,1,0:T(8,128)}) %reduce-scatter.20.cloned.1.call-update) | async-done | bytes 294928 | tf_op jit(solution)/shard_map/reduce_scatter | solution.py:33
  (686 shorter events, 460.9 us)
Async XLA Ops:
  8.1 146.8 %all-gather.8.cloned.1.call-start = ((), (), s32[]{:S(2)}) async-start(), calls=%async_computation.17 | async-start | bytes 5308416 | tf_op jit(solution)/shard_map/all_gather | solution.py:29
  21.7 165.7 %all-gather.10.cloned.1.call-start = ((), (), s32[]{:S(2)}) async-start(), calls=%async_computation.18 | async-start | bytes 5308416 | tf_op jit(solution)/shard_map/all_gather | solution.py:29
  60.5 90.9 %collective-permute-start = (bf16[1,1,64,512]{3,2,1,0:T(8,128)(2,1)}, bf16[1,1,64,512]{3,2,1,0:T(8,128)(2,1)S(1)}, u32[]{:S(2)}, u32[]{:S(2)}) collective-permute-start(bf16[1,1,64,512]{3,2,1,0:T(8,128)(2,1)} %get-tuple-element.298), channel_id=1, source_target_pairs={{0,1},{1,2},{2,3},{3,4},{4,5},{5,6},{6,7},{8,9},{9,10},{10,11},{11... | collective-permute-start | bytes 196616 | tf_op jit(solution)/shard_map/ppermute | solution.py:42
  62.7 88.7 %collective-permute-start.1 = (bf16[1,1,64,512]{3,2,1,0:T(8,128)(2,1)}, bf16[1,1,64,512]{3,2,1,0:T(8,128)(2,1)S(1)}, u32[]{:S(2)}, u32[]{:S(2)}) collective-permute-start(bf16[1,1,64,512]{3,2,1,0:T(8,128)(2,1)} %get-tuple-element.299), channel_id=1, source_target_pairs={{1,0},{2,1},{3,2},{4,3},{5,4},{6,5},{7,6},{9,8},{10,9},{11,10},{12... | collective-permute-start | bytes 196616 | tf_op jit(solution)/shard_map/ppermute | solution.py:43
  66.4 56.5 %all-to-all-start = ((bf16[4,2,256]{2,1,0:T(2,128)(2,1)}), bf16[4,2,256]{2,1,0:T(2,128)(2,1)S(1)}, u32[]{:S(2)}, u32[]{:S(2)}) async-start(bf16[4,2,256]{2,1,0:T(2,128)(2,1)} %reshape.1270), calls=%async_computation | async-start | bytes 8192 | tf_op jit(solution)/shard_map/all_to_all | solution.py:37
  69.7 142.3 %all-gather.12.cloned.1.call-start = ((), (), s32[]{:S(2)}) async-start(), calls=%async_computation.19 | async-start | bytes 1769472 | tf_op jit(solution)/shard_map/all_gather | solution.py:29
  123.0 99.1 %all-to-all-start.2 = ((bf16[4,2,32768]{2,1,0:T(2,128)(2,1)}), bf16[4,2,32768]{2,1,0:T(2,128)(2,1)}, u32[]{:S(2)}, u32[]{:S(2)}) async-start(bf16[4,2,32768]{2,1,0:T(2,128)(2,1)} %reshape.1272), calls=%async_computation.2 | async-start | bytes 1048576 | tf_op jit(solution)/shard_map/all_to_all | solution.py:37
  222.1 60.5 %all-to-all-start.1 = ((bf16[8,512,256]{1,2,0:T(8,128)(2,1)}), bf16[8,512,256]{1,2,0:T(8,128)(2,1)}, u32[]{:S(2)}, u32[]{:S(2)}) async-start(bf16[8,512,256]{1,2,0:T(8,128)(2,1)} %bitcast.62), calls=%async_computation.1 | async-start | bytes 4194304 | tf_op jit(solution)/shard_map/all_to_all | solution.py:37
  226.6 28.4 %reduce-scatter.36.cloned.1.call-start = ((), (), s32[]{:S(2)}) async-start(), calls=%async_computation.30 | async-start | bytes 327680
  230.2 521.6 %reduce-scatter.34.cloned.1.call-start = ((), (), s32[]{:S(2)}) async-start(), calls=%async_computation.29 | async-start | bytes 1179648
  598.5 155.1 %reduce-scatter.26.cloned.1.call-start = ((), (), s32[]{:S(2)}) async-start(), calls=%async_computation.25 | async-start | bytes 3538944 | tf_op jit(solution)/shard_map/reduce_scatter | solution.py:33
  602.4 172.6 %reduce-scatter.22.cloned.1.call-start = ((), (), s32[]{:S(2)}) async-start(), calls=%async_computation.23 | async-start | bytes 10616832 | tf_op jit(solution)/shard_map/reduce_scatter | solution.py:33
  633.9 173.8 %reduce-scatter.16.cloned.1.call-start = ((), (), s32[]{:S(2)}) async-start(), calls=%async_computation.20 | async-start | bytes 1179648 | tf_op jit(solution)/shard_map/reduce_scatter | solution.py:33
  659.6 4.1 collective-permute-start.4
  663.5 244.5 %reduce-scatter.18.cloned.1.call-start = ((), (), s32[]{:S(2)}) async-start(), calls=%async_computation.21 | async-start | bytes 10616832 | tf_op jit(solution)/shard_map/reduce_scatter | solution.py:33
  702.7 229.1 %reduce-scatter.32.cloned.1.call-start = ((), (), s32[]{:S(2)}) async-start(), calls=%async_computation.28 | async-start | bytes 20480 | tf_op jit(solution)/shard_map/reduce_scatter | solution.py:33
  705.3 9.7 collective-permute-start.6
  706.6 8.4 collective-permute-start.7
  751.7 206.9 %reduce-scatter.30.cloned.1.call-start = ((), (), s32[]{:S(2)}) async-start(), calls=%async_computation.27 | async-start | bytes 327680 | tf_op jit(solution)/shard_map/reduce_scatter | solution.py:33
  753.6 232.9 %reduce-scatter.28.cloned.1.call-start = ((), (), s32[]{:S(2)}) async-start(), calls=%async_computation.26 | async-start | bytes 491520 | tf_op jit(solution)/shard_map/reduce_scatter | solution.py:33
  754.3 264.1 %reduce-scatter.24.cloned.1.call-start = ((), (), s32[]{:S(2)}) async-start(), calls=%async_computation.24 | async-start | bytes 1474560 | tf_op jit(solution)/shard_map/reduce_scatter | solution.py:33
  807.7 104.2 %all-to-all-start.5 = ((f32[4,16,512]{2,1,0:T(8,128)}), f32[4,16,512]{2,1,0:T(8,128)S(1)}, u32[]{:S(2)}, u32[]{:S(2)}) async-start(f32[4,16,512]{2,1,0:T(8,128)} %reduce-scatter.16.cloned.1.call-done), calls=%async_computation.6 | async-start | bytes 262144 | tf_op jit(solution)/shard_map/all_to_all | solution.py:37
  811.6 238.8 %reduce-scatter.20.cloned.1.call-start = ((), (), s32[]{:S(2)}) async-start(), calls=%async_computation.22 | async-start | bytes 1474560 | tf_op jit(solution)/shard_map/reduce_scatter | solution.py:33
  919.8 8.3 all-to-all-start.4
  (147 other events, 2884.8 us)
Sparse Core Ops, SparseCore 0:
  21.9 52.8 all-gather.7
  76.3 54.5 all-gather.9
  132.6 23.9 all-gather.11
  598.6 30.3 reduce-scatter.33
  631.2 41.3 reduce-scatter.25
  674.9 100.0 reduce-scatter.21
  777.4 30.2 reduce-scatter.15
  810.1 97.9 reduce-scatter.17
  911.0 20.7 reduce-scatter.31
  934.6 24.0 reduce-scatter.29
  962.0 24.4 reduce-scatter.27
  989.8 28.5 reduce-scatter.23
  1021.9 28.5 reduce-scatter.19
Sparse Core Ops, SparseCore 1:
  230.4 24.6 reduce-scatter.35

commit v2 on v1

--- a/solution.py
+++ b/solution.py
@@ -1,6 +1,10 @@
+import functools
+
 import jax
 import jax.numpy as jnp
 from jax import lax
+from jax.experimental import pallas as pl
+from jax.experimental.pallas import tpu as pltpu
 from jax.sharding import PartitionSpec as P
 
 HEADS = 8
@@ -10,6 +14,8 @@
 MASKED = -1e30
 BF16 = jnp.bfloat16
 F32 = jnp.float32
+MESH = pl.DeviceIdType.MESH
+VMEM_BYTES = 60 * 1024 * 1024
 
 
 def dot(a, b, ca, cb):
@@ -116,7 +122,7 @@
     return y.reshape(images, HEADS, y.shape[1], y.shape[2]).transpose(0, 2, 1, 3)
 
 
-def attention(q, k, v, g, tk, tv, keep, scale):
+def attention_plain(q, k, v, g, tk, tv, keep, scale):
     p, length, d = q.shape
     block = min(512, length)
     keys = jnp.concatenate([tk, k], axis=1)
@@ -151,7 +157,7 @@
     return join(o), join(dq), dk[:, text:], dv[:, text:], dk[:, :text], dv[:, :text]
 
 
-def body(
+def plain_body(
     image_in, time_embed, caption, caption_mask, conv_in, conv_out, embed_proj, qkv_proj,
     caption_proj, out_proj, norm_gains, norm_biases, cotangent,
 ):
@@ -216,7 +222,7 @@
     four = jnp.concatenate([qkv, g_att], axis=1).reshape(n, px, 4, HEADS, d)
     packed = to_pairs(four.transpose(0, 1, 3, 2, 4).reshape(n, px, HEADS, 4 * d), n)
     q, k, v, g = (packed[..., j * d : (j + 1) * d] for j in range(4))
-    o, dq, dk, dv, dtk, dtv = attention(q, k, v, g, mine[0], mine[1], keep, scale)
+    o, dq, dk, dv, dtk, dtv = attention_plain(q, k, v, g, mine[0], mine[1], keep, scale)
     back = from_pairs(jnp.concatenate([o, dq, dk, dv], axis=-1), n)
     back = back.reshape(n * px, HEADS, 4, d).transpose(0, 2, 1, 3).reshape(n * px, 4 * chans)
     attended, proj_grad = back[:, :chans], back[:, chans:]
@@ -296,6 +302,1197 @@
     )
 
 
+class Place:
+    def __init__(self):
+        self.i = lax.axis_index("img")
+        self.s = lax.axis_index("sp")
+        self.z = lax.div(self.s, 2)
+        self.c = lax.rem(self.s, 2)
+        x = lax.rem(self.i, 2)
+        y = lax.div(self.i, 2)
+        self.ix = self.i + 1 - 2 * x
+        self.iy = self.i + 2 - 4 * y
+        self.id = 3 - self.i
+        self.sib = (self.i, self.s + 1 - 2 * self.c)
+        self.xn = (self.ix, self.s)
+        self.yn = (self.iy, self.s)
+
+    def zp(self, k, nz):
+        return (self.i, 2 * lax.rem(self.z + k, nz) + self.c)
+
+    def rp(self, k, n_sp):
+        return (self.i, lax.rem(self.s + k, n_sp))
+
+
+def greet(peers):
+    bar = pltpu.get_barrier_semaphore()
+    for p in peers:
+        pl.semaphore_signal(bar, inc=1, device_id=p, device_id_type=MESH)
+
+
+def greeted(count):
+    pl.semaphore_wait(pltpu.get_barrier_semaphore(), count)
+
+
+def remote(src, dst, ssem, rsem, dev):
+    cp = pltpu.make_async_remote_copy(
+        src_ref=src, dst_ref=dst, send_sem=ssem, recv_sem=rsem, device_id=dev, device_id_type=MESH
+    )
+    cp.start()
+    return cp
+
+
+def params(cid=None, grid=0):
+    extra = {} if cid is None else {"collective_id": cid, "has_side_effects": True}
+    if grid:
+        extra["dimension_semantics"] = ("arbitrary",) * grid
+    return pltpu.CompilerParams(vmem_limit_bytes=VMEM_BYTES, **extra)
+
+
+ANY = pl.BlockSpec(memory_space=pl.ANY)
+VM = pl.BlockSpec(memory_space=pltpu.VMEM)
+def trade_kernel(n_sp, na, *refs):
+    ins, outs = refs[: na + 1], refs[na + 1 : 2 * na + 2]
+    ssem, rsem, lsem = refs[2 * na + 2 :]
+    at = Place()
+    peers = [at.rp(k, n_sp) for k in range(1, n_sp)]
+    greet(peers)
+    local = [pltpu.make_async_copy(ins[a].at[at.s], outs[a].at[at.s], lsem.at[a]) for a in range(na)]
+    local.append(pltpu.make_async_copy(ins[na], outs[na].at[at.s], lsem.at[na]))
+    for cp in local:
+        cp.start()
+    greeted(len(peers))
+    sent = []
+    for k in range(1, n_sp):
+        dev = at.rp(k, n_sp)
+        for a in range(na):
+            sent.append(remote(ins[a].at[dev[1]], outs[a].at[at.s], ssem.at[a, k], rsem.at[a, k], dev))
+        sent.append(remote(ins[na], outs[na].at[at.s], ssem.at[na, k], rsem.at[na, k], dev))
+    for cp in local:
+        cp.wait()
+    for cp in sent:
+        cp.wait()
+
+
+def trade(parts, common, n_sp, cid):
+    na = len(parts)
+    shapes = [p.shape for p in parts] + [(n_sp,) + common.shape]
+    return pl.pallas_call(
+        functools.partial(trade_kernel, n_sp, na),
+        out_shape=[jax.ShapeDtypeStruct(s, BF16) for s in shapes],
+        in_specs=[ANY] * (na + 1),
+        out_specs=[ANY] * (na + 1),
+        scratch_shapes=[
+            pltpu.SemaphoreType.DMA((na + 1, n_sp)),
+            pltpu.SemaphoreType.DMA((na + 1, n_sp)),
+            pltpu.SemaphoreType.DMA((na + 1,)),
+        ],
+        compiler_params=params(cid),
+        name="trade",
+    )(*parts, common)
+
+
+def exchange_scratch(n_sp, width, halo_types, chans):
+    out = [pltpu.VMEM((8, chans), F32), pltpu.VMEM((n_sp, 8, chans), F32)]
+    for ty in halo_types:
+        out += [pltpu.VMEM((width, chans), ty), pltpu.VMEM((width, chans), ty)]
+    count = n_sp - 1 + 2 * len(halo_types)
+    return out + [pltpu.SemaphoreType.DMA((count,)), pltpu.SemaphoreType.DMA((count,))]
+
+
+def exchange_greet(n_sp):
+    at = Place()
+    greet([at.rp(k, n_sp) for k in range(1, n_sp)])
+
+
+def exchange(n_sp, width, scratch, edges):
+    at = Place()
+    mine, every = scratch[0], scratch[1]
+    ssem, rsem = scratch[-2:]
+    greeted(n_sp - 1)
+    sent = []
+    for e, ref in enumerate(edges):
+        above, below = scratch[2 + 2 * e], scratch[3 + 2 * e]
+        px = ref.shape[0]
+        j = n_sp - 1 + 2 * e
+        sent.append(remote(ref.at[px - width :], above, ssem.at[j], rsem.at[j], at.rp(1, n_sp)))
+        sent.append(remote(ref.at[:width], below, ssem.at[j + 1], rsem.at[j + 1], at.rp(n_sp - 1, n_sp)))
+    for k in range(1, n_sp):
+        sent.append(remote(mine, every.at[at.s], ssem.at[k - 1], rsem.at[k - 1], at.rp(k, n_sp)))
+    every[at.s] = mine[...]
+    for cp in sent:
+        cp.wait()
+
+
+def channel_stats(mine, v):
+    mean = jnp.sum(v, axis=0, keepdims=True) / v.shape[0]
+    dev = v - mean
+    mine[0:1, :] = mean
+    mine[1:2, :] = jnp.sum(dev * dev, axis=0, keepdims=True)
+
+
+def group_total(rows):
+    c = rows.shape[1]
+    size = c // GROUPS
+    a = lax.broadcasted_iota(jnp.int32, (c, c), 0)
+    b = lax.broadcasted_iota(jnp.int32, (c, c), 1)
+    same = jnp.where(lax.div(a, size) == lax.div(b, size), 1.0, 0.0)
+    return lax.dot_general(
+        rows, same, (((1,), (0,)), ((), ())), preferred_element_type=F32, precision=PRECISE
+    )
+
+
+def combine_stats(every, px):
+    n_sp, _, c = every.shape
+    size = c // GROUPS
+    means = [every[j, 0:1, :] for j in range(n_sp)]
+    center_c = sum(means) / n_sp
+    dev = sum(every[j, 1:2, :] for j in range(n_sp))
+    dev = dev + px * sum((m - center_c) * (m - center_c) for m in means)
+    center = group_total(jnp.broadcast_to(center_c, (8, c)))[0:1] / size
+    off = center_c - center
+    dev = dev + (px * n_sp) * (off * off)
+    var = group_total(jnp.broadcast_to(dev, (8, c)))[0:1] / (px * n_sp * size)
+    return center, lax.rsqrt(var + EPSILON)
+
+
+def combine_sums(every):
+    n_sp = every.shape[0]
+    total = every[0]
+    for j in range(1, n_sp):
+        total = total + every[j]
+    return total
+
+
+def edge_flags(n_sp, s):
+    return jnp.where(s > 0, 1.0, 0.0), jnp.where(s < n_sp - 1, 1.0, 0.0)
+
+
+def shifted(dst, row, width, block):
+    col = lax.broadcasted_iota(jnp.int32, block.shape, 0)
+    r = slice(row * width, (row + 1) * width)
+    dst[1, r, :] = block.astype(BF16)
+    dst[0, r, :] = jnp.where(col == 0, 0.0, pltpu.roll(block, 1, 0)).astype(BF16)
+    dst[2, r, :] = jnp.where(col == width - 1, 0.0, pltpu.roll(block, width - 1, 0)).astype(BF16)
+
+
+def joined(w_ref, *lead):
+    return jnp.concatenate([w_ref[(j,) + lead] for j in range(4)], axis=-1)
+
+
+def conv_kernel(n_sp, width, refs_in, x, up, dn, every, rows, w, *rest):
+    base = None
+    if refs_in:
+        base, rest = rest[0], rest[1:]
+    out, act, stats, above, below, a3 = rest[:6]
+    scratch = rest[6:]
+    step = pl.program_id(0)
+    px, c = out.shape
+    height = px // width
+
+    @pl.when(step == 0)
+    def _():
+        exchange_greet(n_sp)
+        center, inverse = combine_stats(every, px)
+        mul = inverse * rows[0:1, :] * rows[2:3, :]
+        add = rows[1:2, :] * rows[2:3, :] + rows[3:4, :]
+        has_up, has_dn = edge_flags(n_sp, lax.axis_index("sp"))
+        for r in range(height + 2):
+            if r == 0:
+                v = up[...]
+            elif r == height + 1:
+                v = dn[...]
+            else:
+                v = x[(r - 1) * width : r * width, :]
+            v = silu((v.astype(F32) - center) * mul + add)
+            if r == 0:
+                v = v * has_up
+            elif r == height + 1:
+                v = v * has_dn
+            act[r * width : (r + 1) * width, :] = v.astype(BF16)
+            shifted(a3, r, width, v)
+        if base is None:
+            out[...] = jnp.zeros_like(out)
+        else:
+            out[...] = base[...].astype(F32)
+
+    i, j = lax.div(step, 3), lax.rem(step, 3)
+    lhs = a3[j, pl.ds(pl.multiple_of(i * width, width), px), :]
+    out[...] += dot(lhs, joined(w, 0), 1, 1)
+
+    @pl.when(step == 8)
+    def _():
+        channel_stats(scratch[0], out[...])
+        exchange(n_sp, width, scratch, [out])
+        stats[...] = scratch[1][...]
+        above[...] = scratch[2][...]
+        below[...] = scratch[3][...]
+
+
+def whole_spec(shape):
+    return pl.BlockSpec(shape, lambda t: (0,) * len(shape))
+
+
+def conv_call(x, up, dn, every, rows, w, base, n_sp, width, cid):
+    px, c = x.shape
+    padded = px + 2 * width
+    ins = [x, up, dn, every, rows, w] + ([] if base is None else [base])
+    in_specs = [whole_spec(v.shape) for v in ins]
+    in_specs[5] = pl.BlockSpec((4, 1, c, 128), lambda t: (0, t, 0, 0))
+    outs = [((px, c), F32), ((padded, c), BF16), ((n_sp, 8, c), F32), ((width, c), F32), ((width, c), F32)]
+    return pl.pallas_call(
+        functools.partial(conv_kernel, n_sp, width, base is not None),
+        grid=(9,),
+        in_specs=in_specs,
+        out_specs=[whole_spec(s) for s, _ in outs],
+        out_shape=[jax.ShapeDtypeStruct(s, ty) for s, ty in outs],
+        scratch_shapes=[pltpu.VMEM((3, padded, c), BF16)] + exchange_scratch(n_sp, width, [F32], c),
+        compiler_params=params(cid, 1),
+        name="conv_forward",
+    )(*ins)
+
+
+def qkv_kernel(n_sp, res, every, rows, w_qkv, w_proj, cot, normed, qk, vg, qk_s, vg_s, ssem, rsem, lsem):
+    at = Place()
+    px, c = res.shape
+    d = c // HEADS
+    peers = [at.rp(k, n_sp) for k in range(1, n_sp)]
+    greet(peers)
+    center, inverse = combine_stats(every, px)
+    n = ((res[...] - center) * (inverse * rows[0:1, :]) + rows[1:2, :]).astype(BF16)
+    normed[...] = n
+    wq = joined(w_qkv)
+    wp = joined(w_proj)
+    q = dot(n, wq[:c], 1, 1).astype(BF16)
+    k = dot(n, wq[c : 2 * c], 1, 1).astype(BF16)
+    v = dot(n, wq[2 * c :], 1, 1).astype(BF16)
+    g = dot(cot[...], wp, 1, 0).astype(BF16)
+    for h in range(HEADS):
+        cut = slice(h * d, (h + 1) * d)
+        qk_s[h] = jnp.concatenate([q[:, cut], k[:, cut]], axis=1)
+        vg_s[h] = jnp.concatenate([v[:, cut], g[:, cut]], axis=1)
+    local = []
+    for a, (src, dst) in enumerate(((qk_s, qk), (vg_s, vg))):
+        cp = pltpu.make_async_copy(src.at[at.s], dst.at[at.s], lsem.at[a])
+        cp.start()
+        local.append(cp)
+    greeted(len(peers))
+    sent = []
+    for j in range(1, n_sp):
+        dev = at.rp(j, n_sp)
+        for a, (src, dst) in enumerate(((qk_s, qk), (vg_s, vg))):
+            sent.append(remote(src.at[dev[1]], dst.at[at.s], ssem.at[a, j], rsem.at[a, j], dev))
+    for cp in local:
+        cp.wait()
+    for cp in sent:
+        cp.wait()
+
+
+def qkv_call(res, every, rows, w_qkv, w_proj, cot, n_sp, cid):
+    px, c = res.shape
+    big = jax.ShapeDtypeStruct((n_sp, px, 128), BF16)
+    return pl.pallas_call(
+        functools.partial(qkv_kernel, n_sp),
+        out_shape=[jax.ShapeDtypeStruct((px, c), BF16), big, big],
+        in_specs=[VM] * 6,
+        out_specs=[VM, ANY, ANY],
+        scratch_shapes=[
+            pltpu.VMEM((HEADS, px, 128), BF16),
+            pltpu.VMEM((HEADS, px, 128), BF16),
+            pltpu.SemaphoreType.DMA((2, n_sp)),
+            pltpu.SemaphoreType.DMA((2, n_sp)),
+            pltpu.SemaphoreType.DMA((2,)),
+        ],
+        compiler_params=params(cid),
+        name="project_and_send",
+    )(res, every, rows, w_qkv, w_proj, cot)
+
+
+def post_kernel(
+    n_sp, width, od, dkv, w_qkv, w_proj, res, cot, normed, every, rows,
+    output, g_out, g_qkv, n_grad, stats, above, below, *scratch,
+):
+    exchange_greet(n_sp)
+    px, c = res.shape
+    d = c // HEADS
+    att = jnp.concatenate([od[h][:, :d] for h in range(HEADS)], axis=1)
+    pg = jnp.concatenate(
+        [od[h][:, d:] for h in range(HEADS)]
+        + [dkv[h][:, :d] for h in range(HEADS)]
+        + [dkv[h][:, d:] for h in range(HEADS)],
+        axis=1,
+    )
+    wq = joined(w_qkv)
+    wp = joined(w_proj)
+    ng = dot(pg, wq, 1, 0)
+    n_grad[...] = ng
+    center, inverse = combine_stats(every, px)
+    hat = (res[...] - center) * inverse
+    scratch[0][0:1, :] = jnp.sum(ng, axis=0, keepdims=True)
+    scratch[0][1:2, :] = jnp.sum(ng * hat, axis=0, keepdims=True)
+    output[...] = (res[...] + dot(att, wp, 1, 1)).astype(BF16)
+    go = dot(cot[...], att, 0, 0).astype(BF16)
+    gq = dot(pg, normed[...], 0, 0).astype(BF16)
+    for j in range(4):
+        g_out[j] = go[:, j * 128 : (j + 1) * 128]
+        g_qkv[j] = gq[:, j * 128 : (j + 1) * 128]
+    exchange(n_sp, width, scratch, [n_grad])
+    stats[...] = scratch[1][...]
+    above[...] = scratch[2][...]
+    below[...] = scratch[3][...]
+
+
+def post_call(od, dkv, w_qkv, w_proj, res, cot, normed, every, rows, n_sp, width, cid):
+    px, c = res.shape
+    outs = [
+        ((px, c), BF16), ((4, c, 128), BF16), ((4, 3 * c, 128), BF16), ((px, c), F32),
+        ((n_sp, 8, c), F32), ((width, c), F32), ((width, c), F32),
+    ]
+    return pl.pallas_call(
+        functools.partial(post_kernel, n_sp, width),
+        out_shape=[jax.ShapeDtypeStruct(s, ty) for s, ty in outs],
+        in_specs=[VM] * 9,
+        out_specs=[VM] * len(outs),
+        scratch_shapes=exchange_scratch(n_sp, width, [F32], c),
+        compiler_params=params(cid),
+        name="project_back",
+    )(od, dkv, w_qkv, w_proj, res, cot, normed, every, rows)
+
+
+def back_kernel(n_sp, width, has_base, x, every, rows, act, u, ua, ub, sums, every2, rows2, y, ya, yb, *rest):
+    if has_base:
+        cot, cota, cotb = rest[:3]
+        rest = rest[3:]
+    w = rest[0]
+    rest = rest[1:]
+    if has_base:
+        dw, out, stats, above, below, res_grad = rest[:6]
+        rest = rest[6:]
+    else:
+        dw, out, stats, above, below = rest[:5]
+        rest = rest[5:]
+    a3, g3, gt = rest[:3]
+    scratch = rest[3:]
+    step = pl.program_id(0)
+    px, c = u.shape
+    height = px // width
+    members = px * n_sp * (c // GROUPS)
+
+    @pl.when(step == 0)
+    def _():
+        exchange_greet(n_sp)
+        center, inverse = combine_stats(every2, px)
+        gain, fac = rows2[0:1, :], rows2[2:3, :]
+        total = combine_sums(sums) * (gain * fac)
+        total = group_total(total) / members
+        s1, s2 = total[0:1, :], total[1:2, :]
+        mul = gain * fac
+        has_up, has_dn = edge_flags(n_sp, lax.axis_index("sp"))
+        for r in range(height + 2):
+            if r == 0:
+                uu, yy, flag = ua[...], ya[...], has_up
+            elif r == height + 1:
+                uu, yy, flag = ub[...], yb[...], has_dn
+            else:
+                cut = slice((r - 1) * width, r * width)
+                uu, yy, flag = u[cut, :], y[cut, :], None
+            hat = (yy - center) * inverse
+            g = inverse * (uu * mul - s1 - hat * s2)
+            if has_base:
+                cc = cota[...] if r == 0 else cotb[...] if r == height + 1 else cot[cut, :]
+                g = g + cc.astype(F32)
+            if flag is not None:
+                g = g * flag
+            elif has_base:
+                res_grad[cut, :] = g
+            g = g.astype(BF16).astype(F32)
+            shifted(g3, r, width, g)
+            shifted(a3, r, width, act[r * width : (r + 1) * width, :].astype(F32))
+        gt[...] = g3[1, width : width + px, :].T
+        out[...] = jnp.zeros_like(out)
+
+    i, j = lax.div(step, 3), lax.rem(step, 3)
+    lhs = g3[2 - j, pl.ds(pl.multiple_of((2 - i) * width, width), px), :]
+    out[...] += dot(lhs, joined(w, 0), 1, 0)
+    part = dot(gt[...], a3[j, pl.ds(pl.multiple_of(i * width, width), px), :], 1, 0).astype(BF16)
+    for b in range(4):
+        dw[b, 0] = part[:, b * 128 : (b + 1) * 128]
+
+    @pl.when(step == 8)
+    def _():
+        center, inverse = combine_stats(every, px)
+        hat = (x[...].astype(F32) - center) * inverse
+        pre = hat * (rows[0:1, :] * rows[2:3, :]) + (rows[1:2, :] * rows[2:3, :] + rows[3:4, :])
+        v = out[...] * silu_slope(pre)
+        out[...] = v
+        scratch[0][0:1, :] = jnp.sum(v, axis=0, keepdims=True)
+        scratch[0][1:2, :] = jnp.sum(v * hat, axis=0, keepdims=True)
+        exchange(n_sp, width, scratch, [out])
+        stats[...] = scratch[1][...]
+        above[...] = scratch[2][...]
+        below[...] = scratch[3][...]
+
+
+def back_call(x, every, rows, act, u, ua, ub, sums, every2, rows2, y, ya, yb, base, w, n_sp, width, cid):
+    px, c = u.shape
+    padded = px + 2 * width
+    ins = [x, every, rows, act, u, ua, ub, sums, every2, rows2, y, ya, yb] + list(base or ()) + [w]
+    in_specs = [whole_spec(v.shape) for v in ins]
+    in_specs[-1] = pl.BlockSpec((4, 1, c, 128), lambda t: (0, t, 0, 0))
+    outs = [((4, 9, c, 128), BF16), ((px, c), F32), ((n_sp, 8, c), F32), ((width, c), F32), ((width, c), F32)]
+    out_specs = [whole_spec(s) for s, _ in outs]
+    out_specs[0] = pl.BlockSpec((4, 1, c, 128), lambda t: (0, t, 0, 0))
+    if base:
+        outs.append(((px, c), F32))
+        out_specs.append(whole_spec((px, c)))
+    return pl.pallas_call(
+        functools.partial(back_kernel, n_sp, width, bool(base)),
+        grid=(9,),
+        in_specs=in_specs,
+        out_specs=out_specs,
+        out_shape=[jax.ShapeDtypeStruct(s, ty) for s, ty in outs],
+        scratch_shapes=[
+            pltpu.VMEM((3, padded, c), BF16), pltpu.VMEM((3, padded, c), BF16), pltpu.VMEM((c, px), BF16),
+        ]
+        + exchange_scratch(n_sp, width, [F32], c),
+        compiler_params=params(cid, 1),
+        name="conv_backward",
+    )(*ins)
+
+
+def attention_kernel(L, T, BQ, BK, qk, vg, text, bias, od, dkv, dt, k_s, v_s, s_s, e_s, dk_s, dv_s):
+    d = qk.shape[1] // 2
+    step = pl.program_id(0)
+
+    @pl.when(step == 0)
+    def _():
+        ones = (lax.broadcasted_iota(jnp.int32, (1, d), 1) == 0).astype(BF16)
+        head = lax.axis_index("sp")
+        pair, odd = lax.div(head, 2), lax.rem(head, 2)
+        picked = []
+        for j in (pair, HEADS // 2 + pair):
+            blk = text[j].astype(F32)
+            picked.append(jnp.where(odd > 0, blk[:, d:], blk[:, :d]).astype(BF16))
+        k_s[0:T, :] = picked[0]
+        v_s[0:T, :] = jnp.concatenate([picked[1], jnp.broadcast_to(ones, (T, d))], axis=1)
+        k_s[T:, :] = qk[:, d:]
+        v_s[T:, :] = jnp.concatenate([vg[:, :d], jnp.broadcast_to(ones, (L, d))], axis=1)
+        dk_s[...] = jnp.zeros_like(dk_s)
+        dv_s[...] = jnp.zeros_like(dv_s)
+
+    r = pl.ds(pl.multiple_of(step * BQ, BQ), BQ)
+    scale = d ** -0.5
+    q = (qk[r, :][:, :d].astype(F32) * scale).astype(BF16)
+    g = vg[r, :][:, d:]
+    blocks = [(0, T)] + [(T + j * BK, BK) for j in range(L // BK)]
+    peak = None
+    for at, n in blocks:
+        s = dot(q, k_s[at : at + n, :], 1, 1)
+        if at == 0:
+            s = s + bias[...]
+        s_s[:, at : at + n] = s
+        for j in range(n // 128):
+            part = s[:, 128 * j : 128 * j + 128]
+            peak = part if peak is None else jnp.maximum(peak, part)
+    peak = jnp.max(peak, axis=1, keepdims=True)
+    o = jnp.zeros((BQ, 2 * d), F32)
+    for at, n in blocks:
+        e = jnp.exp(s_s[:, at : at + n] - peak).astype(BF16)
+        e_s[:, at : at + n] = e
+        o = o + dot(e, v_s[at : at + n, :], 1, 0)
+    inverse = 1.0 / o[:, d : d + 1]
+    o = o[:, :d] * inverse
+    g = g.astype(F32) * inverse
+    row = jnp.sum(o * g, axis=1, keepdims=True)
+    g = g.astype(BF16)
+    gt, qt = g.T, q.T
+    dq = jnp.zeros((BQ, d), F32)
+    for at, n in blocks:
+        e = e_s[:, at : at + n]
+        dp = dot(g, v_s[at : at + n, :d], 1, 1)
+        ds = (e.astype(F32) * (dp - row)).astype(BF16)
+        dq = dq + dot(ds, k_s[at : at + n, :], 1, 0)
+        dv_s[:, at : at + n] += dot(gt, e, 1, 0)
+        dk_s[:, at : at + n] += dot(qt, ds, 1, 0)
+    od[...] = jnp.concatenate([o, dq * scale], axis=1).astype(BF16)
+
+    @pl.when(step == pl.num_programs(0) - 1)
+    def _():
+        both = jnp.concatenate([dk_s[...], dv_s[...]], axis=0).astype(BF16).T
+        dt[...] = both[:T]
+        dkv[...] = both[T:]
+
+
+def attention_call(qk, vg, text, bias):
+    (L, d2), T = qk.shape, text.shape[1]
+    BQ, BK = 256, 1024
+    full = lambda shape: pl.BlockSpec(shape, lambda t: (0, 0))
+    return pl.pallas_call(
+        functools.partial(attention_kernel, L, T, BQ, BK),
+        grid=(L // BQ,),
+        in_specs=[full((L, d2)), full((L, d2)), pl.BlockSpec(text.shape, lambda t: (0, 0, 0)), full((1, T))],
+        out_specs=[pl.BlockSpec((BQ, d2), lambda t: (t, 0)), full((L, d2)), full((T, d2))],
+        out_shape=[jax.ShapeDtypeStruct(s, BF16) for s in ((L, d2), (L, d2), (T, d2))],
+        scratch_shapes=[
+            pltpu.VMEM((T + L, d2 // 2), BF16),
+            pltpu.VMEM((T + L, d2), BF16),
+            pltpu.VMEM((BQ, T + L), F32),
+            pltpu.VMEM((BQ, T + L), BF16),
+            pltpu.VMEM((d2 // 2, T + L), F32),
+            pltpu.VMEM((d2 // 2, T + L), F32),
+        ],
+        compiler_params=params(None, 1),
+        name="attention",
+    )(qk, vg, text, bias)
+
+
+class Mail:
+    def __init__(self, ssem, rsem):
+        self.ssem, self.rsem, self.sent = ssem, rsem, []
+
+    def send(self, src, dst, dev):
+        j = len(self.sent)
+        cp = remote(src, dst, self.ssem.at[j], self.rsem.at[j], dev)
+        self.sent.append(cp)
+        return cp
+
+
+def img_peers(at):
+    return [(lax.rem(at.i + k, 4), at.s) for k in range(1, 4)]
+
+
+HEAD_MAIL = 3 * 3 + 3 + 2 * 7 + 7 + 4
+
+
+def head_kernel(nz, width, dims, *refs):
+    na = len(dims)
+    ins, refs = refs[:na], refs[na:]
+    x, cot, emb, cap, w_emb, w_cap, affine = refs[:7]
+    outs, refs = refs[7 : 7 + na], refs[7 + na :]
+    st0, xa, xb, ca, cb, rows, kv_all, cap_all, emb_all = refs[:9]
+    (ssem, rsem, lsem, mine, every, h0, h1, h2, h3, aff_s, emb_s, cap_s, part, part_r, kv_s, kv_r, mod_s, mod_r,
+     msend, mrecv) = refs[9:]
+    n_sp = 2 * nz
+    at = Place()
+    line = [at.rp(k, n_sp) for k in range(1, n_sp)]
+    grid = img_peers(at)
+    greet(line + grid)
+    mail = Mail(msend, mrecv)
+    local = []
+    sent = {}
+    kinds = {}
+
+    def view(a, ii, k, core, half=None):
+        r = dims[a][1]
+        sp = 2 * lax.rem(at.z - k + nz, nz) + core
+        if half is None:
+            return outs[a].at[ii, :, pl.ds(pl.multiple_of(sp * r, r), r), :]
+        h = r // 2
+        return outs[a].at[ii, :, pl.ds(pl.multiple_of(sp * r + half * h, h), h), :]
+
+    def send(a, kind, src, dst, dev):
+        j = kinds.setdefault(kind, len(kinds))
+        sent[a, kind] = remote(src, dst, ssem.at[a, j], rsem.at[a, j], dev)
+
+    def forward(a, kind, ref, dev):
+        send(a, kind, ref, ref, dev)
+
+    def first(a):
+        own = view(a, at.i, 0, at.c)
+        for k in range(1, nz):
+            send(a, ("z", k), ins[a], own, at.zp(k, nz))
+        send(a, ("x", 0), ins[a], own, at.xn)
+        send(a, ("y", 0), ins[a], own, at.yn)
+        send(a, ("s", 0), ins[a], own, at.sib)
+
+    def second(a):
+        for k in range(1, nz):
+            sent[a, ("z", k)].wait_recv()
+            got = view(a, at.i, k, at.c)
+            forward(a, ("x", k), got, at.xn)
+            forward(a, ("y", k), got, at.yn)
+            forward(a, ("s", k), got, at.sib)
+
+    def third(a):
+        for k in range(nz):
+            sent[a, ("x", k)].wait_recv()
+            forward(a, ("da", k), view(a, at.ix, k, at.c, 0), at.yn)
+            forward(a, ("sx", k), view(a, at.ix, k, at.c), at.sib)
+            sent[a, ("y", k)].wait_recv()
+            forward(a, ("db", k), view(a, at.iy, k, at.c, 1), at.xn)
+            forward(a, ("sy", k), view(a, at.iy, k, at.c), at.sib)
+
+    def fourth(a):
+        for k in range(nz):
+            sent[a, ("da", k)].wait_recv()
+            forward(a, ("sa", k), view(a, at.id, k, at.c, 0), at.sib)
+            sent[a, ("db", k)].wait_recv()
+            forward(a, ("sb", k), view(a, at.id, k, at.c, 1), at.sib)
+
+    channel_stats(mine, x[...].astype(F32))
+    greeted(n_sp + 2)
+    first(0)
+    e = cap.shape[1] // 4
+    round1 = []
+    for dev in grid:
+        round1.append(mail.send(affine, aff_s.at[at.i], dev))
+        round1.append(mail.send(emb.at[dev[0]], emb_s.at[at.i], dev))
+        round1.append(mail.send(cap.at[:, pl.ds(pl.multiple_of(dev[0] * e, e), e)], cap_s.at[at.i], dev))
+    own_cap = pltpu.make_async_copy(cap.at[:, pl.ds(pl.multiple_of(at.i * e, e), e)], cap_s.at[at.i], lsem.at[na])
+    own_cap.start()
+    aff_s[at.i] = affine[...]
+    emb_s[at.i] = emb[at.i]
+    px = x.shape[0]
+    stat = []
+    for ref, above, below in ((x, h0, h1), (cot, h2, h3)):
+        stat.append(mail.send(ref.at[px - width :], above, line[0]))
+        stat.append(mail.send(ref.at[:width], below, line[-1]))
+    for dev in line:
+        stat.append(mail.send(mine, every.at[at.s], dev))
+    every[at.s] = mine[...]
+    for a in range(na):
+        cp = pltpu.make_async_copy(ins[a], view(a, at.i, 0, at.c), lsem.at[a])
+        cp.start()
+        local.append(cp)
+    tokens = cap.shape[0]
+    round2, round3 = [], []
+
+    def extras(tick):
+        if tick == 1:
+            own_cap.wait()
+            for cp in round1:
+                cp.wait_recv()
+            for j in range(4):
+                part[j, :tokens] = dot(cap_s[j], w_cap[...], 1, 0)
+                part[j, tokens:] = dot(emb_s[j].astype(BF16), w_emb[...], 1, 0)
+            for dev in grid:
+                round2.append(mail.send(part.at[dev[0]], part_r.at[at.i], dev))
+            part_r[at.i] = part[at.i]
+        if tick == 2:
+            for cp in round2:
+                cp.wait_recv()
+            total = part_r[0] + part_r[1] + part_r[2] + part_r[3]
+            kv_s[...] = total[:tokens].astype(BF16)
+            mod_s[...] = total[tokens:]
+            for dev in line:
+                round3.append(mail.send(kv_s, kv_r.at[at.s], dev))
+                round3.append(mail.send(mod_s, mod_r.at[at.s], dev))
+            kv_r[at.s] = kv_s[...]
+            mod_r[at.s] = mod_s[...]
+        if tick == 4:
+            for cp in round3 + stat:
+                cp.wait_recv()
+            kv_all[...] = kv_r[...]
+            cap_all[...] = cap_s[...]
+            emb_all[...] = jnp.concatenate([emb_s[j][0:1] for j in range(4)] + [jnp.zeros((4, e), F32)])
+            st0[...] = every[...]
+            for dst, src in ((xa, h0), (xb, h1), (ca, h2), (cb, h3)):
+                dst[...] = src[...]
+            aff = jnp.concatenate([aff_s[j] for j in range(4)], axis=1)
+            mod = jnp.concatenate([mod_r[j][0:1] for j in range(n_sp)], axis=1)
+            c = aff.shape[1]
+            rows[...] = jnp.zeros_like(rows)
+            for j in range(3):
+                rows[j, 0:1] = aff[j : j + 1]
+                rows[j, 1:2] = aff[3 + j : 4 + j]
+                rows[j, 2:3] = 1.0 + mod[:, :c] if j == 1 else jnp.ones((1, c), F32)
+            rows[1, 3:4] = mod[:, c:]
+
+    stages = (first, second, third, fourth)
+    for tick in range(1, na + 3):
+        for a in range(na):
+            stage = tick - a
+            if 0 <= stage < 4 and (stage, a) != (0, 0):
+                stages[stage](a)
+        extras(tick)
+    for cp in local:
+        cp.wait()
+    for (a, kind), cp in sent.items():
+        if kind[0] in ("s", "sx", "sy", "sa", "sb"):
+            cp.wait_recv()
+        cp.wait_send()
+    for cp in mail.sent:
+        cp.wait_send()
+
+
+def head_call(chunks, x, cot, emb, cap, w_emb, w_cap, affine, nz, width, cid):
+    dims = [c.shape[:2] for c in chunks]
+    na = len(chunks)
+    n_sp = 2 * nz
+    copies = 3 * nz - 1 + 7 * nz
+    px, c = x.shape
+    tokens, wide = cap.shape
+    e = wide // 4
+    edge = ((width, c), BF16)
+    outs = [
+        ((n_sp, 8, c), F32), edge, edge, edge, edge, ((3, 8, c), F32), ((n_sp, tokens, 128), BF16),
+        ((4, tokens, e), BF16), ((8, e), F32),
+    ]
+    return pl.pallas_call(
+        functools.partial(head_kernel, nz, width, dims),
+        out_shape=[jax.ShapeDtypeStruct((4, t, n_sp * r, 128), BF16) for t, r in dims]
+        + [jax.ShapeDtypeStruct(s, ty) for s, ty in outs],
+        in_specs=[ANY] * na + [VM, VM, VM, ANY, VM, VM, VM],
+        out_specs=[ANY] * na + [VM] * len(outs),
+        scratch_shapes=[
+            pltpu.SemaphoreType.DMA((na, copies)),
+            pltpu.SemaphoreType.DMA((na, copies)),
+            pltpu.SemaphoreType.DMA((na + 1,)),
+            pltpu.VMEM((8, c), F32),
+            pltpu.VMEM((n_sp, 8, c), F32),
+            pltpu.VMEM((width, c), BF16), pltpu.VMEM((width, c), BF16),
+            pltpu.VMEM((width, c), BF16), pltpu.VMEM((width, c), BF16),
+            pltpu.VMEM((4, 8, 128), F32),
+            pltpu.VMEM((4, 8, e), F32),
+            pltpu.VMEM((4, tokens, e), BF16),
+            pltpu.VMEM((4, tokens + 8, 128), F32),
+            pltpu.VMEM((4, tokens + 8, 128), F32),
+            pltpu.VMEM((tokens, 128), BF16),
+            pltpu.VMEM((n_sp, tokens, 128), BF16),
+            pltpu.VMEM((8, 128), F32),
+            pltpu.VMEM((n_sp, 8, 128), F32),
+            pltpu.SemaphoreType.DMA((HEAD_MAIL,)),
+            pltpu.SemaphoreType.DMA((HEAD_MAIL,)),
+        ],
+        compiler_params=params(cid),
+        name="gather_weights",
+    )(*chunks, x, cot, emb, cap, w_emb, w_cap, affine)
+
+
+class Reducer:
+    NAMES = ("q", "sb", "da", "db", "rx", "ry", "r", "zr")
+
+    def __init__(self, at, nz, arrays, ssem, rsem, lsem):
+        self.at, self.nz, self.arrays = at, nz, arrays
+        self.ssem, self.rsem, self.lsem = ssem, rsem, lsem
+        self.sent, self.local, self.groups = {}, {}, []
+
+    @staticmethod
+    def buffers(nz, t, r):
+        return [
+            pltpu.VMEM((4, t, nz, r, 128), BF16),
+            pltpu.VMEM((4, t, nz, r, 128), BF16),
+            pltpu.VMEM((t, nz, r // 2, 128), BF16),
+            pltpu.VMEM((t, nz, r // 2, 128), BF16),
+            pltpu.VMEM((t, nz, r, 128), BF16),
+            pltpu.VMEM((t, nz, r, 128), BF16),
+            pltpu.VMEM((t, nz, r, 128), BF16),
+            pltpu.VMEM((nz - 1, t, r, 128), BF16),
+        ]
+
+    def send(self, g, j, src, dst, dev):
+        self.sent[g, j] = remote(src, dst, self.ssem.at[g, j], self.rsem.at[g, j], dev)
+
+    def load(self, a, t0, t1):
+        g = len(self.groups)
+        self.groups.append((a, t0, t1))
+        src, hbm, _, b = self.arrays[a]
+        if hbm:
+            cp = pltpu.make_async_copy(src.at[:, t0:t1, :, self.at.c], b["q"].at[:, t0:t1], self.lsem.at[g])
+            cp.start()
+            self.local[g] = cp
+        return g
+
+    def start(self, g):
+        a, t0, t1 = self.groups[g]
+        src, _, _, b = self.arrays[a]
+        self.send(g, 0, src.at[:, t0:t1, :, 1 - self.at.c], b["sb"].at[:, t0:t1], self.at.sib)
+
+    def stage1(self, g):
+        a, t0, t1 = self.groups[g]
+        src, hbm, _, b = self.arrays[a]
+        q, sb, at = b["q"], b["sb"], self.at
+        if hbm:
+            self.local[g].wait()
+        self.sent[g, 0].wait_recv()
+        n = t1 - t0
+
+        def add(j, _):
+            ii, tt = lax.div(j, n), t0 + lax.rem(j, n)
+            own = q[ii, tt] if hbm else src[ii, tt, :, at.c]
+            q[ii, tt] = (own.astype(F32) + sb[ii, tt].astype(F32)).astype(BF16)
+            return 0
+
+        lax.fori_loop(0, 4 * n, add, 0)
+        h = q.shape[3] // 2
+        self.send(g, 1, q.at[at.id, t0:t1, :, :h], b["da"].at[t0:t1], at.yn)
+        self.send(g, 2, q.at[at.id, t0:t1, :, h:], b["db"].at[t0:t1], at.xn)
+
+    def stage2(self, g):
+        a, t0, t1 = self.groups[g]
+        b, at = self.arrays[a][3], self.at
+        q = b["q"]
+        h = q.shape[3] // 2
+        self.sent[g, 1].wait_recv()
+        self.sent[g, 2].wait_recv()
+
+        def add(tt, _):
+            q[at.ix, tt, :, :h] = (q[at.ix, tt, :, :h].astype(F32) + b["da"][tt].astype(F32)).astype(BF16)
+            q[at.iy, tt, :, h:] = (q[at.iy, tt, :, h:].astype(F32) + b["db"][tt].astype(F32)).astype(BF16)
+            return 0
+
+        lax.fori_loop(t0, t1, add, 0)
+        self.send(g, 3, q.at[at.ix, t0:t1], b["rx"].at[t0:t1], at.xn)
+        self.send(g, 4, q.at[at.iy, t0:t1], b["ry"].at[t0:t1], at.yn)
+
+    def stage3(self, g):
+        a, t0, t1 = self.groups[g]
+        b, at = self.arrays[a][3], self.at
+        self.sent[g, 3].wait_recv()
+        self.sent[g, 4].wait_recv()
+
+        def add(tt, _):
+            total = b["q"][at.i, tt].astype(F32) + b["rx"][tt].astype(F32) + b["ry"][tt].astype(F32)
+            b["r"][tt] = total.astype(BF16)
+            return 0
+
+        lax.fori_loop(t0, t1, add, 0)
+        for k in range(1, self.nz):
+            dev = at.zp(k, self.nz)
+            there = lax.rem(at.z + k, self.nz)
+            self.send(g, 4 + k, b["r"].at[t0:t1, there], b["zr"].at[k - 1, t0:t1], dev)
+
+    def stage4(self, g):
+        a, t0, t1 = self.groups[g]
+        _, _, out, b = self.arrays[a]
+        at = self.at
+        for k in range(1, self.nz):
+            self.sent[g, 4 + k].wait_recv()
+
+        def add(tt, _):
+            total = (
+                b["q"][at.i, tt, at.z].astype(F32) + b["rx"][tt, at.z].astype(F32) + b["ry"][tt, at.z].astype(F32)
+            )
+            for k in range(1, self.nz):
+                total = total + b["zr"][k - 1, tt].astype(F32)
+            out[tt] = total
+            return 0
+
+        lax.fori_loop(t0, t1, add, 0)
+
+    def finish(self):
+        for cp in self.sent.values():
+            cp.wait_send()
+
+
+class Pipeline:
+    def __init__(self, red):
+        self.red, self.queue = red, []
+
+    def add(self, g):
+        self.red.start(g)
+        self.queue.append([g, 1])
+
+    def tick(self):
+        for item in list(self.queue):
+            g, stage = item
+            getattr(self.red, "stage%d" % stage)(g)
+            item[1] += 1
+            if stage == 4:
+                self.queue.remove(item)
+
+    def drain(self):
+        while self.queue:
+            self.tick()
+
+
+TAIL_MAIL = 6 + 14 + 6 + 3 + 7
+TAIL_GROUPS = 7
+
+
+def tail_kernel(nz, width, *refs):
+    (g_out, g_small, x, st0, rows, act, u, ua, ub, su1, su2, st1, y, ya, yb, w, res_grad,
+     dt_all, cap_all, emb_all, w_emb, w_cap, temb) = refs[:23]
+    image_grad, s_in, s_out, s_small, g_temb, g_cap, g_wemb, g_wcap, g_aff = refs[23:32]
+    refs = refs[32:]
+    names = Reducer.NAMES
+    bufs = [dict(zip(names, refs[8 * a : 8 * a + 8])) for a in range(3)]
+    (ssem, rsem, lsem, msend, mrecv, dw, a3, g3, gt, acc, mine, every, tg_s, tg_r, mod_s, mod_r,
+     gc_s, gc_r, pe_s, pe_r, gs_s, gs_r, ps_s, ps_r, aff_s, aff_r) = refs[24:]
+    n_sp = 2 * nz
+    at = Place()
+    line = [at.rp(k, n_sp) for k in range(1, n_sp)]
+    grid = img_peers(at)
+    greet(line + grid)
+    mail = Mail(msend, mrecv)
+    red = Reducer(
+        at, nz,
+        [(g_out, True, s_out, bufs[0]), (g_small, True, s_small, bufs[1]), (dw, False, s_in, bufs[2])],
+        ssem, rsem, lsem,
+    )
+    pipe = Pipeline(red)
+    early = [red.load(0, 0, 3), red.load(0, 3, 6), red.load(0, 6, 9), red.load(1, 0, 1)]
+    px, c = u.shape
+    height = px // width
+    members = px * n_sp * (c // GROUPS)
+    d = c // HEADS
+    rows0, rows1 = rows[0], rows[1]
+    gain1, bias1, fac1 = rows1[0:1], rows1[1:2], rows1[2:3]
+
+    t1 = combine_sums(su1)
+    t2 = combine_sums(su2)
+    mod = jnp.concatenate([t1[1:2] * gain1 + t1[0:1] * bias1, t1[0:1]], axis=1)
+    for j in range(n_sp):
+        mod_s[j] = jnp.broadcast_to(mod[:, j * 128 : (j + 1) * 128], (8, 128))
+    first = 2 * lax.rem(at.s, nz)
+    value = lax.div(at.s, nz)
+    halves = []
+    for j in range(2):
+        blk = dt_all[first + j].astype(F32)
+        halves.append(jnp.where(value > 0, blk[:, d:], blk[:, :d]))
+    tg_s[...] = jnp.concatenate(halves, axis=1).astype(BF16)
+    greeted(n_sp + 2)
+    for g in early:
+        pipe.add(g)
+    round_a = []
+    for dev in grid:
+        round_a.append(mail.send(tg_s, tg_r.at[at.i], dev))
+        round_a.append(mail.send(mod_s.at[at.s], mod_r.at[at.i], dev))
+    tg_r[at.i] = tg_s[...]
+    mod_r[at.i] = mod_s[at.s]
+
+    center, inverse = combine_stats(st1, px)
+    total = group_total(t1 * (gain1 * fac1)) / members
+    s1, s2 = total[0:1, :], total[1:2, :]
+    mul = gain1 * fac1
+    has_up, has_dn = edge_flags(n_sp, at.s)
+    for r in range(height + 2):
+        cut = slice((r - 1) * width, r * width)
+        if r == 0:
+            uu, yy = ua[...], ya[...]
+        elif r == height + 1:
+            uu, yy = ub[...], yb[...]
+        else:
+            uu, yy = u[cut, :], y[cut, :]
+        g = inverse * (uu * mul - s1 - (yy - center) * inverse * s2)
+        if r == 0:
+            g = g * has_up
+        elif r == height + 1:
+            g = g * has_dn
+        shifted(g3, r, width, g.astype(BF16).astype(F32))
+        shifted(a3, r, width, act[r * width : (r + 1) * width, :].astype(F32))
+    gt[...] = g3[1, width : width + px, :].T
+    pipe.tick()
+
+    def weight_taps(t0, t1):
+        def one(tap, _):
+            i, j = lax.div(tap, 3), lax.rem(tap, 3)
+            part = dot(gt[...], a3[j, pl.ds(pl.multiple_of(i * width, width), px), :], 1, 0).astype(BF16)
+            for b in range(4):
+                dw[b, tap] = part[:, b * 128 : (b + 1) * 128].reshape(nz, 2, c // n_sp, 128)
+            return 0
+
+        lax.fori_loop(t0, t1, one, 0)
+        pipe.add(red.load(2, t0, t1))
+
+    def input_taps(t0, t1):
+        def one(tap, _):
+            i, j = lax.div(tap, 3), lax.rem(tap, 3)
+            lhs = g3[2 - j, pl.ds(pl.multiple_of((2 - i) * width, width), px), :]
+            part = dot(lhs, joined(w, tap), 1, 0)
+            acc[...] = part + jnp.where(tap > 0, acc[...], 0.0)
+            return 0
+
+        lax.fori_loop(t0, t1, one, 0)
+
+    weight_taps(0, 3)
+    pipe.tick()
+    weight_taps(3, 6)
+    for cp in round_a:
+        cp.wait_recv()
+    tokens = tg_s.shape[0]
+    flat_tg = tg_r[...].reshape(4 * tokens, 128)
+    g_wcap[...] = dot(cap_all[...].reshape(4 * tokens, cap_all.shape[2]), flat_tg, 0, 0)
+    gc_s[...] = dot(flat_tg, w_cap[...], 1, 1).astype(BF16).reshape(gc_s.shape)
+    mods = jnp.concatenate([mod_r[j][0:1] for j in range(4)] + [jnp.zeros((4, 128), F32)])
+    exact = lambda a, b, ca, cb: lax.dot_general(
+        a, b, (((ca,), (cb,)), ((), ())), preferred_element_type=F32, precision=PRECISE
+    )
+    emb_t = emb_all[...].T
+    g_wemb[...] = sum(emb_t[:, j : j + 1] * mods[j : j + 1] for j in range(4))
+    pe_s[...] = exact(mods, w_emb[...].astype(F32), 1, 1)
+    share = tokens // n_sp
+    round_b = []
+    for dev in line:
+        cut = pl.ds(pl.multiple_of(dev[1] * share, share), share)
+        round_b.append(mail.send(gc_s.at[:, cut, :], gc_r.at[at.s], dev))
+        round_b.append(mail.send(pe_s, pe_r.at[at.s], dev))
+    gc_r[at.s] = gc_s[:, pl.ds(pl.multiple_of(at.s * share, share), share), :]
+    pe_r[at.s] = pe_s[...]
+    pipe.tick()
+    weight_taps(6, 9)
+    pipe.tick()
+    input_taps(0, 3)
+    pipe.tick()
+    for cp in round_b:
+        cp.wait_recv()
+    gc = gc_r[0].astype(F32)
+    pe = pe_r[0]
+    for j in range(1, n_sp):
+        gc = gc + gc_r[j].astype(F32)
+        pe = pe + pe_r[j]
+    gs_s[...] = gc
+    for j in range(4):
+        ps_s[j] = jnp.broadcast_to(pe[j : j + 1], pe.shape)
+    round_c = []
+    for dev in grid:
+        round_c.append(mail.send(gs_s.at[dev[0]], gs_r.at[at.i], dev))
+        round_c.append(mail.send(ps_s.at[dev[0]], ps_r.at[at.i], dev))
+    gs_r[at.i] = gs_s[at.i]
+    ps_r[at.i] = ps_s[at.i]
+    input_taps(3, 6)
+    pipe.tick()
+    input_taps(6, 9)
+    pipe.tick()
+
+    center, inverse = combine_stats(st0, px)
+    hat = (x[...].astype(F32) - center) * inverse
+    gain0 = rows0[0:1]
+    v = acc[...] * silu_slope(hat * gain0 + rows0[1:2])
+    acc[...] = v
+    mine[...] = jnp.zeros_like(mine)
+    mine[0:1, :] = jnp.sum(v, axis=0, keepdims=True)
+    mine[1:2, :] = jnp.sum(v * hat, axis=0, keepdims=True)
+    round_d = [mail.send(mine, every.at[at.s], dev) for dev in line]
+    every[at.s] = mine[...]
+    pipe.tick()
+    for cp in round_d:
+        cp.wait_recv()
+    t0 = combine_sums(every)
+    zero = jnp.zeros((2, c), F32)
+    aff = jnp.concatenate([t0[1:2], t1[1:2] * fac1, t2[1:2], t0[0:1], t1[0:1] * fac1, t2[0:1], zero])
+    for j in range(4):
+        aff_s[j] = aff[:, j * 128 : (j + 1) * 128]
+    round_e = [mail.send(aff_s.at[dev[0]], aff_r.at[at.i], dev) for dev in grid]
+    aff_r[at.i] = aff_s[at.i]
+    total = group_total(t0 * gain0) / members
+    image_grad[...] = res_grad[...] + inverse * (acc[...] * gain0 - total[0:1] - hat * total[1:2])
+    pipe.drain()
+    for cp in round_c + round_e:
+        cp.wait_recv()
+    g_cap[...] = jnp.concatenate([gs_r[j] for j in range(4)], axis=1)
+    g_temb[...] = jnp.concatenate([ps_r[j] for j in range(4)], axis=1) * silu_slope(temb[...])
+    g_aff[...] = aff_r[0] + aff_r[1] + aff_r[2] + aff_r[3]
+    red.finish()
+    for cp in mail.sent:
+        cp.wait_send()
+
+
+def tail_call(g_out, g_small, x, st0, rows, act, u, ua, ub, su1, su2, st1, y, ya, yb, w, res_grad,
+              dt_all, cap_all, emb_all, w_emb, w_cap, temb, nz, width, cid):
+    px, c = u.shape
+    n_sp = 2 * nz
+    padded = px + 2 * width
+    r = c // n_sp
+    rs = g_small.shape[4]
+    tokens = dt_all.shape[1]
+    e = cap_all.shape[2]
+    share = tokens // n_sp
+    ins = [g_out, g_small, x, st0, rows, act, u, ua, ub, su1, su2, st1, y, ya, yb, w, res_grad,
+           dt_all, cap_all, emb_all, w_emb, w_cap, temb]
+    outs = [(px, c), (9, r, 128), (9, r, 128), (1, rs, 128), (8, 4 * e), (share, 4 * e), (e, 128), (e, 128), (8, 128)]
+    vm = pltpu.VMEM
+    return pl.pallas_call(
+        functools.partial(tail_kernel, nz, width),
+        out_shape=[jax.ShapeDtypeStruct(s, F32) for s in outs],
+        in_specs=[ANY, ANY] + [VM] * (len(ins) - 2),
+        out_specs=[VM] * len(outs),
+        scratch_shapes=Reducer.buffers(nz, 9, r) + Reducer.buffers(nz, 1, rs) + Reducer.buffers(nz, 9, r)
+        + [
+            pltpu.SemaphoreType.DMA((TAIL_GROUPS, 4 + nz)),
+            pltpu.SemaphoreType.DMA((TAIL_GROUPS, 4 + nz)),
+            pltpu.SemaphoreType.DMA((TAIL_GROUPS,)),
+            pltpu.SemaphoreType.DMA((TAIL_MAIL,)),
+            pltpu.SemaphoreType.DMA((TAIL_MAIL,)),
+            vm((4, 9, nz, 2, r, 128), BF16),
+            vm((3, padded, c), BF16), vm((3, padded, c), BF16), vm((c, px), BF16), vm((px, c), F32),
+            vm((8, c), F32), vm((n_sp, 8, c), F32),
+            vm((tokens, 128), BF16), vm((4, tokens, 128), BF16),
+            vm((n_sp, 8, 128), F32), vm((4, 8, 128), F32),
+            vm((4, tokens, e), BF16), vm((n_sp, 4, share, e), BF16),
+            vm((8, e), F32), vm((n_sp, 8, e), F32),
+            vm((4, share, e), F32), vm((4, share, e), F32),
+            vm((4, 8, e), F32), vm((4, 8, e), F32),
+            vm((4, 8, 128), F32), vm((4, 8, 128), F32),
+        ],
+        compiler_params=params(cid),
+        name="first_backward_and_sums",
+    )(*ins)
+
+
+def fast_body(
+    image_in, time_embed, caption, caption_mask, conv_in, conv_out, embed_proj, qkv_proj,
+    caption_proj, out_proj, norm_gains, norm_biases, cotangent,
+):
+    n, height, width, c = image_in.shape
+    n_img, n_sp = lax.axis_size("img"), lax.axis_size("sp")
+    sp = lax.axis_index("sp")
+    nz = n_sp // 2
+    px = height * width
+    d = c // HEADS
+    x = image_in.reshape(px, c)
+    cot = cotangent.reshape(px, c)
+
+    flat = lambda w: w.transpose(1, 2, 3, 0).reshape(9, w.shape[3], w.shape[0])
+    small = jnp.concatenate([qkv_proj.T, out_proj.T], axis=0)[None]
+    affine = jnp.concatenate([norm_gains, norm_biases, jnp.zeros_like(norm_gains[:2])]).astype(F32)
+    temb = jnp.broadcast_to(time_embed.astype(F32), (8, time_embed.shape[1]))
+    emb = silu(temb).astype(BF16).astype(F32).reshape(8, 4, -1).transpose(1, 0, 2)
+    (w_in, w_out, w_small, st0, xa, xb, ca, cb, rows, kv_all, cap_all, emb_all) = head_call(
+        [flat(conv_in), flat(conv_out), small], x, cot, emb, caption[0], embed_proj, caption_proj, affine, nz, width, 0
+    )
+    cut = qkv_proj.shape[1]
+    w_small = w_small.reshape(4, n_sp, -1, 128)
+    w_qkv = w_small[:, :, :cut].reshape(4, 3 * c, 128)
+    w_proj = w_small[:, :, cut:].reshape(4, c, 128)
+    bias = jnp.where(caption_mask > 0, 0.0, MASKED).astype(F32)
+
+    hidden, act0, st1, ha, hb = conv_call(x, xa, xb, st0, rows[0], w_in, None, n_sp, width, 1)
+    res, act1, st2, ra, rb = conv_call(hidden, ha, hb, st1, rows[1], w_out, x, n_sp, width, 2)
+    normed, qk, vg = qkv_call(res, st2, rows[2], w_qkv, w_proj, cot, n_sp, 3)
+    od, dkv, dt = attention_call(qk.reshape(-1, 2 * d), vg.reshape(-1, 2 * d), kv_all, bias)
+    od, dkv, dt_all = trade([od.reshape(n_sp, px, 2 * d), dkv.reshape(n_sp, px, 2 * d)], dt, n_sp, 4)
+
+    output, g_out, g_qkv, ng, su2, na, nb = post_call(
+        od, dkv, w_qkv, w_proj, res, cot, normed, st2, rows[2], n_sp, width, 5
+    )
+    g_conv_out, pre_grad, su1, pa, pb, res_grad = back_call(
+        hidden, st1, rows[1], act1, ng, na, nb, su2, st2, rows[2], res, ra, rb,
+        (cot, ca, cb), w_out, n_sp, width, 6,
+    )
+    g_small = jnp.concatenate(
+        [g_qkv.reshape(4, n_sp, cut, 128), g_out.reshape(4, n_sp, c // n_sp, 128)], axis=2
+    ).reshape(4, 1, nz, 2, -1, 128)
+    g_conv_out = g_conv_out.reshape(4, 9, nz, 2, -1, 128)
+    grad_image, s_in, s_out, s_small, g_temb, g_cap, g_wemb, g_wcap, g_aff = tail_call(
+        g_conv_out, g_small, x, st0, rows, act0, pre_grad, pa, pb, su1, su2, st1, hidden, ha, hb, w_in, res_grad,
+        dt_all, cap_all, emb_all, embed_proj, caption_proj, temb, nz, width, 7,
+    )
+    unflat = lambda g: g.reshape(3, 3, g.shape[1], 128).transpose(3, 0, 1, 2)
+    return (
+        output.reshape(image_in.shape),
+        grad_image.reshape(image_in.shape),
+        g_temb[:1],
+        g_cap[None],
+        unflat(s_in),
+        unflat(s_out),
+        g_wemb,
+        s_small[0, :cut].T,
+        g_wcap,
+        s_small[0, cut:].T,
+        g_aff[:3],
+        g_aff[3:6],
+    )
+
+
+def body(*args):
+    image_in, qkv_proj = args[0], args[7]
+    n, height, width, c = image_in.shape
+    n_img, n_sp = lax.axis_size("img"), lax.axis_size("sp")
+    fits = n == 1 and n_img == 4 and n_sp == HEADS and c == 512 and width == 64
+    return fast_body(*args) if fits else plain_body(*args)
+
+
 def solution(mesh):
     rows = P("img", "sp", None, None)
     kernel = P("img", None, None, "sp")

time: 1070 us -> 438 us (0.41); the launches traced: 1060 us -> 437 us
  Pallas kernels: 0 us -> 412 us
  blocking collectives: 307 us -> 0 us
  waiting for transfers between devices: 297 us -> 0 us
  matrix products: 216 us -> 0 us
  local copies, waits for them, and re-layouts: 99.4 us -> 17.3 us
  other arithmetic: 87.4 us -> 7.16 us
  starting transfers between devices: 32.3 us -> 0 us
  between operations: 17.7 us -> 0.79 us
    pallas_call x0 -> x9, Pallas kernels: none -> 412 us  [the longest x1 88.5 us: tail_call(): pl.pallas_call(functools.partial(tail_kernel, nz, width), out_shape=[jax....]
    reduce_scatter x9 -> x0, waiting for transfers between devices: 269 us -> none  [scatter_sum(): return lax.psum_scatter(x, axis, scatter_dimension=dim, tiled=True)]
    dot_general x114 -> x0, matrix products: 216 us -> none  [the longest x62 56.6 us: dot(): lax.dot_general(a, b, (((ca,), (cb,)), ((), ())), preferred_element_type=...]
    all_gather x14 -> x0, blocking collectives: 181 us -> none  [the longest x11 138 us: gather(): return lax.all_gather(x, axis, axis=dim, tiled=True)]
    psum x3 -> x0, blocking collectives: 60.8 us -> none  [sums(): return lax.psum(both, 'sp')]
    all_to_all x1 -> x0, blocking collectives: 53.1 us -> none  [swap(): return lax.all_to_all(x, axis, split, concat, tiled=True)]
    unnamed x8 -> x0, other arithmetic: 34.1 us -> none
    unnamed x210 -> x25, local copies, waits for them, and re-layouts: 39.1 us -> 6.62 us
  transfers between devices with their start and end apart: 27 -> 0, of which waited for: 12 -> 0; matrix products, arithmetic and copies ran while one was open for 12% -> 0% of each run, Pallas kernels for 0% -> 0%
where the time goes in v2:
time: 438 us; the launch traced here: 437 us
  Pallas kernels  412 us (94%)
  local copies, waits for them, and re-layouts  17.3 us (4%)
  other arithmetic  7.16 us (2%)
    pallas_call x1, Pallas kernels, tail_call(): pl.pallas_call(functools.partial(tail_kernel, nz, width), out_shape=[jax....  88.5 us
    pallas_call x1, Pallas kernels, head_call(): pl.pallas_call(functools.partial(head_kernel, nz, width, dims), out_shape...  71.7 us
    pallas_call x1, Pallas kernels, attention_call(): pl.pallas_call(functools.partial(attention_kernel, L, T, BQ, BK), grid=(L...  65.3 us
    pallas_call x1, Pallas kernels, trade(): pl.pallas_call(functools.partial(trade_kernel, n_sp, na), out_shape=[jax....  53.4 us
    pallas_call x1, Pallas kernels, qkv_call(): pl.pallas_call(functools.partial(qkv_kernel, n_sp), out_shape=[jax.ShapeD...  40.6 us
    pallas_call x2, Pallas kernels, conv_call(): pl.pallas_call(functools.partial(conv_kernel, n_sp, width, base is not No...  39.9 us
    pallas_call x1, Pallas kernels, post_call(): pl.pallas_call(functools.partial(post_kernel, n_sp, width), out_shape=[ja...  27.4 us
    pallas_call x1, Pallas kernels, back_call(): pl.pallas_call(functools.partial(back_kernel, n_sp, width, bool(base)), g...  24.8 us

profile of v2, /device:TPU:0, one launch (start us, length us, event | category | flops | bytes accessed | tf_op | source)
XLA Modules:
  0.0 436.9 jit_solution(280588779957225897)
XLA Ops:
  0.6 0.7 convert_reduce_fusion
  2.0 1.4 maximum_bitcast_fusion.refs_2_
  3.6 1.4 maximum_convert_fusion.refs_9_
  4.9 71.7 %gather_weights.1 = (bf16[4,9,512,128]{3,2,1,0:T(8,128)(2,1)}, bf16[4,9,512,128]{3,2,1,0:T(8,128)(2,1)}, bf16[4,1,2048,128]{3,2,1,0:T(8,128)(2,1)}, f32[8,8,512]...) custom-call(bf16[9,64,128]{2,1,0:T(8,128)(2,1)} %bitcast.73, ...), custom_call_target="tpu_custom_call" | custom-call | tf_op jit(solution)/shard_map/gather_weights/pallas_call | solution.py:1031
  76.6 1.4 slice_bitcast_fusion.2
  78.0 21.3 %conv_forward.2 = (f32[512,512]{1,0:T(8,128)}, bf16[640,512]{1,0:T(8,128)(2,1)}, f32[8,8,512]{2,1,0:T(8,128)}, f32[64,512]{1,0:T(8,128)}, f32[64,512]{1,0:T(8,128)}) custom-call(bf16[512,512]{1,0:T(8,128)(2,1)} %bitcast.54, bf16[64,512]{1,0:T(8,128)(2,1)} %get-tuple-element.65.up, bf16[64,512]{1,0:T(8,128)(2,1)} %get-tuple-element.66.dn, ...), custom_call_target="tpu_custom_call" | custom-call | tf_op jit(solution)/shard_map/conv_forward/pallas_call | solution.py:543
  99.3 18.7 %conv_forward.3 = (f32[512,512]{1,0:T(8,128)}, bf16[640,512]{1,0:T(8,128)(2,1)}, f32[8,8,512]{2,1,0:T(8,128)}, f32[64,512]{1,0:T(8,128)}, f32[64,512]{1,0:T(8,128)}) custom-call(f32[512,512]{1,0:T(8,128)} %get-tuple-element.70.x.refs_12_, f32[64,512]{1,0:T(8,128)} %get-tuple-element.71.up.refs_13_, f32[64,512]{1,0:T(8,128)} %get-tuple-element.72.dn.refs_14_, ...), custom_call_target="tpu_custom_call" | custom-call | tf_op jit(solution)/shard_map/conv_forward/pallas_call | solution.py:543
  118.0 1.3 slice.43
  119.3 0.8 slice.44
  120.1 40.6 %project_and_send.1 = (bf16[512,512]{1,0:T(8,128)(2,1)}, bf16[8,512,128]{2,1,0:T(8,128)(2,1)}, bf16[8,512,128]{2,1,0:T(8,128)(2,1)}) custom-call(f32[512,512]{1,0:T(8,128)} %get-tuple-element.75.res.y, f32[8,8,512]{2,1,0:T(8,128)} %get-tuple-element.76.every.every2, f32[8,512]{1,0:T(8,128)} %get-tuple-element.118.rows.rows2, bf16[4,1536,128]{2,1,0:T(8,128)(2,1)} %bitcast.47, ...), custom_call_target="tpu_custom_call" | custom-call | tf_op jit(solution)/shard_map/project_and_send/pallas_call | solution.py:594
  161.2 65.3 %attention.1 = (bf16[4096,128]{1,0:T(8,128)(2,1)}, bf16[4096,128]{1,0:T(8,128)(2,1)}, bf16[128,128]{1,0:T(8,128)(2,1)}) custom-call(bf16[4096,128]{1,0:T(8,128)(2,1)} %bitcast.63, bf16[4096,128]{1,0:T(8,128)(2,1)} %bitcast.64, bf16[8,128,128]{2,1,0:T(8,128)(2,1)} %get-tuple-element.80.text, f32[1,128]{1,0:T(1,128)} %compare_select_fusion.bias), custom_call_target="tpu_custom_call" | custom-call | tf_op jit(solution)/shard_map/attention/pallas_call | solution.py:830
  226.5 53.4 %trade.1 = (bf16[8,512,128]{2,1,0:T(8,128)(2,1)}, bf16[8,512,128]{2,1,0:T(8,128)(2,1)}, bf16[8,128,128]{2,1,0:T(8,128)(2,1)}) custom-call(bf16[8,512,128]{2,1,0:T(8,128)(2,1)} %bitcast.66, bf16[8,512,128]{2,1,0:T(8,128)(2,1)} %bitcast.67, bf16[128,128]{1,0:T(8,128)(2,1)} %get-tuple-element.83.refs_2_), custom_call_target="tpu_custom_call" | custom-call | tf_op jit(solution)/shard_map/trade/pallas_call | solution.py:380
  279.9 27.4 %project_back.1 = (bf16[512,512]{1,0:T(8,128)(2,1)}, bf16[4,512,128]{2,1,0:T(8,128)(2,1)}, bf16[4,1536,128]{2,1,0:T(8,128)(2,1)}, f32[512,512]{1,0:T(8,128)}, f3...) custom-call(bf16[8,512,128]{2,1,0:T(8,128)(2,1)} %get-tuple-element.84.od, ...), custom_call_target="tpu_custom_call" | custom-call | tf_op jit(solution)/shard_map/project_back/pallas_call | solution.py:651
  307.4 3.1 pad_maximum_fusion.refs_1_
  310.5 24.8 %conv_backward.1 = (bf16[4,9,512,128]{3,2,1,0:T(8,128)(2,1)}, f32[512,512]{1,0:T(8,128)}, f32[8,8,512]{2,1,0:T(8,128)}, f32[64,512]{1,0:T(8,128)}, f32[64,512]{1,0:T(8,128)}, /*index=5*/f32[512,512]{1,0:T(8,128)}) custom-call(f32[512,512]{1,0:T(8,128)} %get-tuple-element.70.x.refs_12_, f32[8,8,512]{2,1,0:T(8,128)} %get-tuple-element.73.every.refs_11_, ...), custom_call_target="tpu_custom_call" | custom-call | tf_op jit(solution)/shard_map/conv_backward/pallas_call | solution.py:748
  336.0 88.5 %first_backward_and_sums.1 = (f32[512,512]{1,0:T(8,128)}, f32[9,64,128]{2,1,0:T(8,128)}, f32[9,64,128]{2,1,0:T(8,128)}, f32[1,256,128]{2,1,0:T(8,128)}, f32[8,20...) custom-call(bf16[4,9,4,2,64,128]{5,4,3,2,1,0:T(8,128)(2,1)} %bitcast.57, ...), custom_call_target="tpu_custom_call" | custom-call | tf_op jit(solution)/shard_map/first_backward_and_sums/pallas_call | solution.py:1395
  424.5 1.6 slice_bitcast_fusion
  426.1 1.4 slice_bitcast_fusion.1
  427.5 1.4 slice.38
  428.9 1.3 fusion.2
  430.3 0.8 copy.32
  431.1 2.3 copy.33
  434.0 0.7 copy.35
  434.8 0.7 copy.36
  (29 shorter events, 4.0 us)
Async XLA Ops:
  99.3 18.7 %copy-start = (bf16[4,1,2048,128]{3,2,1,0:T(8,128)(2,1)S(1)}, bf16[4,1,2048,128]{3,2,1,0:T(8,128)(2,1)}, u32[]{:S(2)}) copy-start(bf16[4,1,2048,128]{3,2,1,0:T(8,128)(2,1)} %get-tuple-element.77) | copy-start | bytes 6291460
  120.1 40.6 %copy-start.8 = (s32[1,128]{1,0:T(1,128)S(1)}, s32[1,128]{1,0:T(1,128)}, u32[]{:S(2)}) copy-start(s32[1,128]{1,0:T(1,128)} %param.16) | copy-start | bytes 1540
  310.5 24.8 %copy-start.7 = (bf16[1,2048]{1,0:T(2,128)(2,1)S(1)}, bf16[1,2048]{1,0:T(2,128)(2,1)}, u32[]{:S(2)}) copy-start(bf16[1,2048]{1,0:T(2,128)(2,1)} %param.14) | copy-start | bytes 12292
  336.0 94.3 %copy-start.1 = (bf16[512,512]{1,0:T(8,128)(2,1)S(1)}, bf16[512,512]{1,0:T(8,128)(2,1)}, u32[]{:S(2)}) copy-start(bf16[512,512]{1,0:T(8,128)(2,1)} %get-tuple-element.87) | copy-start | bytes 1572868
  424.5 8.9 %copy-start.6 = (f32[16,2048]{1,0:T(8,128)S(1)}, f32[16,2048]{1,0:T(8,128)}, u32[]{:S(2)}) copy-start(f32[16,2048]{1,0:T(8,128)} %get-tuple-element.111) | copy-start | bytes 393220
  424.5 9.6 %copy-start.3 = (f32[9,64,128]{2,1,0:T(8,128)S(1)}, f32[9,64,128]{2,1,0:T(8,128)}, u32[]{:S(2)}) copy-start(f32[9,64,128]{2,1,0:T(8,128)} %get-tuple-element.112) | copy-start | bytes 884740
  426.1 8.7 %copy-start.2 = (f32[9,64,128]{2,1,0:T(8,128)S(1)}, f32[9,64,128]{2,1,0:T(8,128)}, u32[]{:S(2)}) copy-start(f32[9,64,128]{2,1,0:T(8,128)} %get-tuple-element.113) | copy-start | bytes 884740
  430.3 5.2 %copy-start.5 = (f32[512,128]{1,0:T(8,128)S(1)}, f32[512,128]{1,0:T(8,128)}, u32[]{:S(2)}) copy-start(f32[512,128]{1,0:T(8,128)} %get-tuple-element.141) | copy-start | bytes 786436
  431.1 5.1 %copy-start.4 = (f32[512,128]{1,0:T(8,128)S(1)}, f32[512,128]{1,0:T(8,128)}, u32[]{:S(2)}) copy-start(f32[512,128]{1,0:T(8,128)} %get-tuple-element.143) | copy-start | bytes 786436

commit v3 on v2

--- a/solution.py
+++ b/solution.py
@@ -434,12 +434,19 @@
 def group_total(rows):
     c = rows.shape[1]
     size = c // GROUPS
-    a = lax.broadcasted_iota(jnp.int32, (c, c), 0)
-    b = lax.broadcasted_iota(jnp.int32, (c, c), 1)
-    same = jnp.where(lax.div(a, size) == lax.div(b, size), 1.0, 0.0)
-    return lax.dot_general(
-        rows, same, (((1,), (0,)), ((), ())), preferred_element_type=F32, precision=PRECISE
+    a = lax.broadcasted_iota(jnp.int32, (128, 128), 0)
+    b = lax.broadcasted_iota(jnp.int32, (128, 128), 1)
+    same = jnp.where(lax.bitwise_xor(a, b) < size, 1.0, 0.0).astype(BF16)
+    high = rows.astype(BF16)
+    rest = rows - high.astype(F32)
+    mid = rest.astype(BF16)
+    low = (rest - mid.astype(F32)).astype(BF16)
+    parts = jnp.concatenate([high.astype(F32), mid.astype(F32), low.astype(F32)]).astype(BF16)
+    total = jnp.concatenate(
+        [dot(parts[:, j * 128 : (j + 1) * 128], same, 1, 0) for j in range(c // 128)], axis=1
     )
+    n = rows.shape[0]
+    return total[:n] + total[n : 2 * n] + total[2 * n :]
 
 
 def combine_stats(every, px):
@@ -478,6 +485,16 @@
 
 def joined(w_ref, *lead):
     return jnp.concatenate([w_ref[(j,) + lead] for j in range(4)], axis=-1)
+
+
+def split_small(whole, n_sp):
+    c = whole.shape[1]
+    cols, out = 3 * c // n_sp, c // n_sp
+    chunk = cols + out
+    return (
+        jnp.concatenate([whole[j * chunk : j * chunk + cols] for j in range(n_sp)]),
+        jnp.concatenate([whole[j * chunk + cols : (j + 1) * chunk] for j in range(n_sp)]),
+    )
 
 
 def conv_kernel(n_sp, width, refs_in, x, up, dn, every, rows, w, *rest):
@@ -552,7 +569,7 @@
     )(*ins)
 
 
-def qkv_kernel(n_sp, res, every, rows, w_qkv, w_proj, cot, normed, qk, vg, qk_s, vg_s, ssem, rsem, lsem):
+def qkv_kernel(n_sp, res, every, rows, w_small, cot, normed, qk, vg, qk_s, vg_s, ssem, rsem, lsem):
     at = Place()
     px, c = res.shape
     d = c // HEADS
@@ -561,8 +578,7 @@
     center, inverse = combine_stats(every, px)
     n = ((res[...] - center) * (inverse * rows[0:1, :]) + rows[1:2, :]).astype(BF16)
     normed[...] = n
-    wq = joined(w_qkv)
-    wp = joined(w_proj)
+    wq, wp = split_small(joined(w_small), n_sp)
     q = dot(n, wq[:c], 1, 1).astype(BF16)
     k = dot(n, wq[c : 2 * c], 1, 1).astype(BF16)
     v = dot(n, wq[2 * c :], 1, 1).astype(BF16)
@@ -588,13 +604,13 @@
         cp.wait()
 
 
-def qkv_call(res, every, rows, w_qkv, w_proj, cot, n_sp, cid):
+def qkv_call(res, every, rows, w_small, cot, n_sp, cid):
     px, c = res.shape
     big = jax.ShapeDtypeStruct((n_sp, px, 128), BF16)
     return pl.pallas_call(
         functools.partial(qkv_kernel, n_sp),
         out_shape=[jax.ShapeDtypeStruct((px, c), BF16), big, big],
-        in_specs=[VM] * 6,
+        in_specs=[VM] * 5,
         out_specs=[VM, ANY, ANY],
         scratch_shapes=[
             pltpu.VMEM((HEADS, px, 128), BF16),
@@ -605,162 +621,10 @@
         ],
         compiler_params=params(cid),
         name="project_and_send",
-    )(res, every, rows, w_qkv, w_proj, cot)
-
-
-def post_kernel(
-    n_sp, width, od, dkv, w_qkv, w_proj, res, cot, normed, every, rows,
-    output, g_out, g_qkv, n_grad, stats, above, below, *scratch,
-):
-    exchange_greet(n_sp)
-    px, c = res.shape
-    d = c // HEADS
-    att = jnp.concatenate([od[h][:, :d] for h in range(HEADS)], axis=1)
-    pg = jnp.concatenate(
-        [od[h][:, d:] for h in range(HEADS)]
-        + [dkv[h][:, :d] for h in range(HEADS)]
-        + [dkv[h][:, d:] for h in range(HEADS)],
-        axis=1,
-    )
-    wq = joined(w_qkv)
-    wp = joined(w_proj)
-    ng = dot(pg, wq, 1, 0)
-    n_grad[...] = ng
-    center, inverse = combine_stats(every, px)
-    hat = (res[...] - center) * inverse
-    scratch[0][0:1, :] = jnp.sum(ng, axis=0, keepdims=True)
-    scratch[0][1:2, :] = jnp.sum(ng * hat, axis=0, keepdims=True)
-    output[...] = (res[...] + dot(att, wp, 1, 1)).astype(BF16)
-    go = dot(cot[...], att, 0, 0).astype(BF16)
-    gq = dot(pg, normed[...], 0, 0).astype(BF16)
-    for j in range(4):
-        g_out[j] = go[:, j * 128 : (j + 1) * 128]
-        g_qkv[j] = gq[:, j * 128 : (j + 1) * 128]
-    exchange(n_sp, width, scratch, [n_grad])
-    stats[...] = scratch[1][...]
-    above[...] = scratch[2][...]
-    below[...] = scratch[3][...]
-
-
-def post_call(od, dkv, w_qkv, w_proj, res, cot, normed, every, rows, n_sp, width, cid):
-    px, c = res.shape
-    outs = [
-        ((px, c), BF16), ((4, c, 128), BF16), ((4, 3 * c, 128), BF16), ((px, c), F32),
-        ((n_sp, 8, c), F32), ((width, c), F32), ((width, c), F32),
-    ]
-    return pl.pallas_call(
-        functools.partial(post_kernel, n_sp, width),
-        out_shape=[jax.ShapeDtypeStruct(s, ty) for s, ty in outs],
-        in_specs=[VM] * 9,
-        out_specs=[VM] * len(outs),
-        scratch_shapes=exchange_scratch(n_sp, width, [F32], c),
-        compiler_params=params(cid),
-        name="project_back",
-    )(od, dkv, w_qkv, w_proj, res, cot, normed, every, rows)
-
-
-def back_kernel(n_sp, width, has_base, x, every, rows, act, u, ua, ub, sums, every2, rows2, y, ya, yb, *rest):
-    if has_base:
-        cot, cota, cotb = rest[:3]
-        rest = rest[3:]
-    w = rest[0]
-    rest = rest[1:]
-    if has_base:
-        dw, out, stats, above, below, res_grad = rest[:6]
-        rest = rest[6:]
-    else:
-        dw, out, stats, above, below = rest[:5]
-        rest = rest[5:]
-    a3, g3, gt = rest[:3]
-    scratch = rest[3:]
-    step = pl.program_id(0)
-    px, c = u.shape
-    height = px // width
-    members = px * n_sp * (c // GROUPS)
-
-    @pl.when(step == 0)
-    def _():
-        exchange_greet(n_sp)
-        center, inverse = combine_stats(every2, px)
-        gain, fac = rows2[0:1, :], rows2[2:3, :]
-        total = combine_sums(sums) * (gain * fac)
-        total = group_total(total) / members
-        s1, s2 = total[0:1, :], total[1:2, :]
-        mul = gain * fac
-        has_up, has_dn = edge_flags(n_sp, lax.axis_index("sp"))
-        for r in range(height + 2):
-            if r == 0:
-                uu, yy, flag = ua[...], ya[...], has_up
-            elif r == height + 1:
-                uu, yy, flag = ub[...], yb[...], has_dn
-            else:
-                cut = slice((r - 1) * width, r * width)
-                uu, yy, flag = u[cut, :], y[cut, :], None
-            hat = (yy - center) * inverse
-            g = inverse * (uu * mul - s1 - hat * s2)
-            if has_base:
-                cc = cota[...] if r == 0 else cotb[...] if r == height + 1 else cot[cut, :]
-                g = g + cc.astype(F32)
-            if flag is not None:
-                g = g * flag
-            elif has_base:
-                res_grad[cut, :] = g
-            g = g.astype(BF16).astype(F32)
-            shifted(g3, r, width, g)
-            shifted(a3, r, width, act[r * width : (r + 1) * width, :].astype(F32))
-        gt[...] = g3[1, width : width + px, :].T
-        out[...] = jnp.zeros_like(out)
-
-    i, j = lax.div(step, 3), lax.rem(step, 3)
-    lhs = g3[2 - j, pl.ds(pl.multiple_of((2 - i) * width, width), px), :]
-    out[...] += dot(lhs, joined(w, 0), 1, 0)
-    part = dot(gt[...], a3[j, pl.ds(pl.multiple_of(i * width, width), px), :], 1, 0).astype(BF16)
-    for b in range(4):
-        dw[b, 0] = part[:, b * 128 : (b + 1) * 128]
-
-    @pl.when(step == 8)
-    def _():
-        center, inverse = combine_stats(every, px)
-        hat = (x[...].astype(F32) - center) * inverse
-        pre = hat * (rows[0:1, :] * rows[2:3, :]) + (rows[1:2, :] * rows[2:3, :] + rows[3:4, :])
-        v = out[...] * silu_slope(pre)
-        out[...] = v
-        scratch[0][0:1, :] = jnp.sum(v, axis=0, keepdims=True)
-        scratch[0][1:2, :] = jnp.sum(v * hat, axis=0, keepdims=True)
-        exchange(n_sp, width, scratch, [out])
-        stats[...] = scratch[1][...]
-        above[...] = scratch[2][...]
-        below[...] = scratch[3][...]
-
-
-def back_call(x, every, rows, act, u, ua, ub, sums, every2, rows2, y, ya, yb, base, w, n_sp, width, cid):
-    px, c = u.shape
-    padded = px + 2 * width
-    ins = [x, every, rows, act, u, ua, ub, sums, every2, rows2, y, ya, yb] + list(base or ()) + [w]
-    in_specs = [whole_spec(v.shape) for v in ins]
-    in_specs[-1] = pl.BlockSpec((4, 1, c, 128), lambda t: (0, t, 0, 0))
-    outs = [((4, 9, c, 128), BF16), ((px, c), F32), ((n_sp, 8, c), F32), ((width, c), F32), ((width, c), F32)]
-    out_specs = [whole_spec(s) for s, _ in outs]
-    out_specs[0] = pl.BlockSpec((4, 1, c, 128), lambda t: (0, t, 0, 0))
-    if base:
-        outs.append(((px, c), F32))
-        out_specs.append(whole_spec((px, c)))
-    return pl.pallas_call(
-        functools.partial(back_kernel, n_sp, width, bool(base)),
-        grid=(9,),
-        in_specs=in_specs,
-        out_specs=out_specs,
-        out_shape=[jax.ShapeDtypeStruct(s, ty) for s, ty in outs],
-        scratch_shapes=[
-            pltpu.VMEM((3, padded, c), BF16), pltpu.VMEM((3, padded, c), BF16), pltpu.VMEM((c, px), BF16),
-        ]
-        + exchange_scratch(n_sp, width, [F32], c),
-        compiler_params=params(cid, 1),
-        name="conv_backward",
-    )(*ins)
-
-
-def attention_kernel(L, T, BQ, BK, qk, vg, text, bias, od, dkv, dt, k_s, v_s, s_s, e_s, dk_s, dv_s):
+    )(res, every, rows, w_small, cot)
+
+
+def attention_kernel(L, T, BQ, BK, qk, vg, text, keep, od, dkv, dt, k_s, v_s, s_s, e_s, dk_s, dv_s):
     d = qk.shape[1] // 2
     step = pl.program_id(0)
 
@@ -789,7 +653,7 @@
     for at, n in blocks:
         s = dot(q, k_s[at : at + n, :], 1, 1)
         if at == 0:
-            s = s + bias[...]
+            s = jnp.where(keep[...] > 0, s, MASKED)
         s_s[:, at : at + n] = s
         for j in range(n // 128):
             part = s[:, 128 * j : 128 * j + 128]
@@ -823,7 +687,7 @@
         dkv[...] = both[T:]
 
 
-def attention_call(qk, vg, text, bias):
+def attention_call(qk, vg, text, keep):
     (L, d2), T = qk.shape, text.shape[1]
     BQ, BK = 256, 1024
     full = lambda shape: pl.BlockSpec(shape, lambda t: (0, 0))
@@ -843,7 +707,7 @@
         ],
         compiler_params=params(None, 1),
         name="attention",
-    )(qk, vg, text, bias)
+    )(qk, vg, text, keep)
 
 
 class Mail:
@@ -866,12 +730,13 @@
 
 def head_kernel(nz, width, dims, *refs):
     na = len(dims)
-    ins, refs = refs[:na], refs[na:]
-    x, cot, emb, cap, w_emb, w_cap, affine = refs[:7]
-    outs, refs = refs[7 : 7 + na], refs[7 + na :]
+    ins, refs = refs[: na - 1], refs[na - 1 :]
+    x, cot, temb, cap, w_emb, w_cap, gains, biases, w_qkv, w_proj = refs[:10]
+    outs, refs = refs[10 : 10 + na], refs[10 + na :]
     st0, xa, xb, ca, cb, rows, kv_all, cap_all, emb_all = refs[:9]
     (ssem, rsem, lsem, mine, every, h0, h1, h2, h3, aff_s, emb_s, cap_s, part, part_r, kv_s, kv_r, mod_s, mod_r,
-     msend, mrecv) = refs[9:]
+     msend, mrecv, emb, affine, small) = refs[9:]
+    ins = list(ins) + [small]
     n_sp = 2 * nz
     at = Place()
     line = [at.rp(k, n_sp) for k in range(1, n_sp)]
@@ -929,10 +794,18 @@
             sent[a, ("db", k)].wait_recv()
             forward(a, ("sb", k), view(a, at.id, k, at.c, 1), at.sib)
 
+    cut = w_qkv.shape[0]
+    small[0, :cut] = w_qkv[...]
+    small[0, cut:] = w_proj[...]
+    e = cap.shape[1] // 4
+    embedded = silu(temb[...].astype(F32)).astype(BF16).astype(F32)
+    for j in range(4):
+        emb[j] = jnp.broadcast_to(embedded[:, j * e : (j + 1) * e], (8, e))
+    affine[0:3] = gains[...].astype(F32)
+    affine[3:6] = biases[...].astype(F32)
     channel_stats(mine, x[...].astype(F32))
     greeted(n_sp + 2)
     first(0)
-    e = cap.shape[1] // 4
     round1 = []
     for dev in grid:
         round1.append(mail.send(affine, aff_s.at[at.i], dev))
@@ -1015,9 +888,9 @@
         cp.wait_send()
 
 
-def head_call(chunks, x, cot, emb, cap, w_emb, w_cap, affine, nz, width, cid):
-    dims = [c.shape[:2] for c in chunks]
-    na = len(chunks)
+def head_call(chunks, x, cot, temb, cap, w_emb, w_cap, gains, biases, w_qkv, w_proj, nz, width, cid):
+    dims = [c.shape[:2] for c in chunks] + [(1, w_qkv.shape[0] + w_proj.shape[0])]
+    na = len(dims)
     n_sp = 2 * nz
     copies = 3 * nz - 1 + 7 * nz
     px, c = x.shape
@@ -1032,7 +905,7 @@
         functools.partial(head_kernel, nz, width, dims),
         out_shape=[jax.ShapeDtypeStruct((4, t, n_sp * r, 128), BF16) for t, r in dims]
         + [jax.ShapeDtypeStruct(s, ty) for s, ty in outs],
-        in_specs=[ANY] * na + [VM, VM, VM, ANY, VM, VM, VM],
+        in_specs=[ANY] * (na - 1) + [VM, VM, VM, ANY] + [VM] * 6,
         out_specs=[ANY] * na + [VM] * len(outs),
         scratch_shapes=[
             pltpu.SemaphoreType.DMA((na, copies)),
@@ -1053,24 +926,27 @@
             pltpu.VMEM((n_sp, 8, 128), F32),
             pltpu.SemaphoreType.DMA((HEAD_MAIL,)),
             pltpu.SemaphoreType.DMA((HEAD_MAIL,)),
+            pltpu.VMEM((4, 8, e), F32),
+            pltpu.VMEM((8, 128), F32),
+            pltpu.VMEM((1,) + dims[-1][1:] + (128,), BF16),
         ],
         compiler_params=params(cid),
         name="gather_weights",
-    )(*chunks, x, cot, emb, cap, w_emb, w_cap, affine)
+    )(*chunks, x, cot, temb, cap, w_emb, w_cap, gains, biases, w_qkv, w_proj)
 
 
 class Reducer:
-    NAMES = ("q", "sb", "da", "db", "rx", "ry", "r", "zr")
-
-    def __init__(self, at, nz, arrays, ssem, rsem, lsem):
+    NAMES = ("d", "sb", "da", "db", "rx", "ry", "r", "zr")
+
+    def __init__(self, at, nz, arrays, ssem, rsem):
         self.at, self.nz, self.arrays = at, nz, arrays
-        self.ssem, self.rsem, self.lsem = ssem, rsem, lsem
-        self.sent, self.local, self.groups = {}, {}, []
+        self.ssem, self.rsem = ssem, rsem
+        self.sent, self.groups = {}, []
 
     @staticmethod
     def buffers(nz, t, r):
         return [
-            pltpu.VMEM((4, t, nz, r, 128), BF16),
+            pltpu.VMEM((2, 4, t, nz, r, 128), BF16),
             pltpu.VMEM((4, t, nz, r, 128), BF16),
             pltpu.VMEM((t, nz, r // 2, 128), BF16),
             pltpu.VMEM((t, nz, r // 2, 128), BF16),
@@ -1083,85 +959,78 @@
     def send(self, g, j, src, dst, dev):
         self.sent[g, j] = remote(src, dst, self.ssem.at[g, j], self.rsem.at[g, j], dev)
 
-    def load(self, a, t0, t1):
+    def add(self, a, t0, t1):
         g = len(self.groups)
         self.groups.append((a, t0, t1))
-        src, hbm, _, b = self.arrays[a]
-        if hbm:
-            cp = pltpu.make_async_copy(src.at[:, t0:t1, :, self.at.c], b["q"].at[:, t0:t1], self.lsem.at[g])
-            cp.start()
-            self.local[g] = cp
-        return g
-
-    def start(self, g):
-        a, t0, t1 = self.groups[g]
-        src, _, _, b = self.arrays[a]
-        self.send(g, 0, src.at[:, t0:t1, :, 1 - self.at.c], b["sb"].at[:, t0:t1], self.at.sib)
-
-    def stage1(self, g):
-        a, t0, t1 = self.groups[g]
-        src, hbm, _, b = self.arrays[a]
-        q, sb, at = b["q"], b["sb"], self.at
-        if hbm:
-            self.local[g].wait()
+        b = self.arrays[a][1]
+        self.send(g, 0, b["d"].at[1 - self.at.c, :, t0:t1], b["sb"].at[:, t0:t1], self.at.sib)
+
+    def run(self, stage, *groups):
+        one = (self.stage1, self.stage2, self.stage3, self.stage4)[stage - 1]
+        for g in groups:
+            one(g, *self.groups[g])
+
+    def stage1(self, g, a, t0, t1):
+        b, at = self.arrays[a][1], self.at
+        d, sb = b["d"], b["sb"]
         self.sent[g, 0].wait_recv()
         n = t1 - t0
 
         def add(j, _):
             ii, tt = lax.div(j, n), t0 + lax.rem(j, n)
-            own = q[ii, tt] if hbm else src[ii, tt, :, at.c]
-            q[ii, tt] = (own.astype(F32) + sb[ii, tt].astype(F32)).astype(BF16)
+            d[at.c, ii, tt] = (d[at.c, ii, tt].astype(F32) + sb[ii, tt].astype(F32)).astype(BF16)
             return 0
 
         lax.fori_loop(0, 4 * n, add, 0)
-        h = q.shape[3] // 2
-        self.send(g, 1, q.at[at.id, t0:t1, :, :h], b["da"].at[t0:t1], at.yn)
-        self.send(g, 2, q.at[at.id, t0:t1, :, h:], b["db"].at[t0:t1], at.xn)
-
-    def stage2(self, g):
-        a, t0, t1 = self.groups[g]
-        b, at = self.arrays[a][3], self.at
-        q = b["q"]
-        h = q.shape[3] // 2
+        h = d.shape[4] // 2
+        self.send(g, 1, d.at[at.c, at.id, t0:t1, :, :h], b["da"].at[t0:t1], at.yn)
+        self.send(g, 2, d.at[at.c, at.id, t0:t1, :, h:], b["db"].at[t0:t1], at.xn)
+
+    def stage2(self, g, a, t0, t1):
+        b, at = self.arrays[a][1], self.at
+        d = b["d"]
+        h = d.shape[4] // 2
         self.sent[g, 1].wait_recv()
         self.sent[g, 2].wait_recv()
 
         def add(tt, _):
-            q[at.ix, tt, :, :h] = (q[at.ix, tt, :, :h].astype(F32) + b["da"][tt].astype(F32)).astype(BF16)
-            q[at.iy, tt, :, h:] = (q[at.iy, tt, :, h:].astype(F32) + b["db"][tt].astype(F32)).astype(BF16)
+            d[at.c, at.ix, tt, :, :h] = (
+                d[at.c, at.ix, tt, :, :h].astype(F32) + b["da"][tt].astype(F32)
+            ).astype(BF16)
+            d[at.c, at.iy, tt, :, h:] = (
+                d[at.c, at.iy, tt, :, h:].astype(F32) + b["db"][tt].astype(F32)
+            ).astype(BF16)
             return 0
 
         lax.fori_loop(t0, t1, add, 0)
-        self.send(g, 3, q.at[at.ix, t0:t1], b["rx"].at[t0:t1], at.xn)
-        self.send(g, 4, q.at[at.iy, t0:t1], b["ry"].at[t0:t1], at.yn)
-
-    def stage3(self, g):
-        a, t0, t1 = self.groups[g]
-        b, at = self.arrays[a][3], self.at
+        self.send(g, 3, d.at[at.c, at.ix, t0:t1], b["rx"].at[t0:t1], at.xn)
+        self.send(g, 4, d.at[at.c, at.iy, t0:t1], b["ry"].at[t0:t1], at.yn)
+
+    def stage3(self, g, a, t0, t1):
+        b, at = self.arrays[a][1], self.at
         self.sent[g, 3].wait_recv()
         self.sent[g, 4].wait_recv()
 
         def add(tt, _):
-            total = b["q"][at.i, tt].astype(F32) + b["rx"][tt].astype(F32) + b["ry"][tt].astype(F32)
+            total = b["d"][at.c, at.i, tt].astype(F32) + b["rx"][tt].astype(F32) + b["ry"][tt].astype(F32)
             b["r"][tt] = total.astype(BF16)
             return 0
 
         lax.fori_loop(t0, t1, add, 0)
         for k in range(1, self.nz):
-            dev = at.zp(k, self.nz)
             there = lax.rem(at.z + k, self.nz)
-            self.send(g, 4 + k, b["r"].at[t0:t1, there], b["zr"].at[k - 1, t0:t1], dev)
-
-    def stage4(self, g):
-        a, t0, t1 = self.groups[g]
-        _, _, out, b = self.arrays[a]
-        at = self.at
+            self.send(g, 4 + k, b["r"].at[t0:t1, there], b["zr"].at[k - 1, t0:t1], at.zp(k, self.nz))
+
+    def stage4(self, g, a, t0, t1):
+        (out, b), at = self.arrays[a], self.at
         for k in range(1, self.nz):
             self.sent[g, 4 + k].wait_recv()
 
         def add(tt, _):
             total = (
-                b["q"][at.i, tt, at.z].astype(F32) + b["rx"][tt, at.z].astype(F32) + b["ry"][tt, at.z].astype(F32)
+                b["d"][at.c, at.i, tt, at.z].astype(F32)
+                + b["rx"][tt, at.z].astype(F32)
+                + b["ry"][tt, at.z].astype(F32)
             )
             for k in range(1, self.nz):
                 total = total + b["zr"][k - 1, tt].astype(F32)
@@ -1175,65 +1044,105 @@
             cp.wait_send()
 
 
-class Pipeline:
-    def __init__(self, red):
-        self.red, self.queue = red, []
-
-    def add(self, g):
-        self.red.start(g)
-        self.queue.append([g, 1])
-
-    def tick(self):
-        for item in list(self.queue):
-            g, stage = item
-            getattr(self.red, "stage%d" % stage)(g)
-            item[1] += 1
-            if stage == 4:
-                self.queue.remove(item)
-
-    def drain(self):
-        while self.queue:
-            self.tick()
-
-
-TAIL_MAIL = 6 + 14 + 6 + 3 + 7
-TAIL_GROUPS = 7
-
-
-def tail_kernel(nz, width, *refs):
-    (g_out, g_small, x, st0, rows, act, u, ua, ub, su1, su2, st1, y, ya, yb, w, res_grad,
-     dt_all, cap_all, emb_all, w_emb, w_cap, temb) = refs[:23]
-    image_grad, s_in, s_out, s_small, g_temb, g_cap, g_wemb, g_wcap, g_aff = refs[23:32]
-    refs = refs[32:]
-    names = Reducer.NAMES
-    bufs = [dict(zip(names, refs[8 * a : 8 * a + 8])) for a in range(3)]
-    (ssem, rsem, lsem, msend, mrecv, dw, a3, g3, gt, acc, mine, every, tg_s, tg_r, mod_s, mod_r,
+BACK_MAIL = 6 + 14 + 6 + 3 + 7 + 9 + 9
+BACK_GROUPS = 7
+BIG = 10
+
+
+def conv_taps(t0, t1, w, ring, rsem, one):
+    slots = ring.shape[0]
+
+    def step(tap, _):
+        slot = lax.rem(tap, slots)
+        pltpu.make_async_copy(w.at[:, tap], ring.at[slot], rsem.at[slot]).wait()
+        one(tap, jnp.concatenate([ring[slot, j] for j in range(4)], axis=-1))
+
+        @pl.when(tap + slots < 9)
+        def _():
+            pltpu.make_async_copy(w.at[:, tap + slots], ring.at[slot], rsem.at[slot]).start()
+
+        return 0
+
+    lax.fori_loop(t0, t1, step, 0)
+
+
+def ring_start(w, ring, rsem):
+    for j in range(ring.shape[0]):
+        pltpu.make_async_copy(w.at[:, j], ring.at[j], rsem.at[j]).start()
+
+
+def backward_kernel(nz, width, *refs):
+    hbm, refs = refs[:BIG], refs[BIG:]
+    w_in, w_out = refs[:2]
+    (st0, st1, st2, rows, ca, cb, ra, rb, ha, hb, dt_all, cap_all, emb_all, w_emb, w_cap, temb) = refs[2:18]
+    output, image_grad, s_in, s_out, s_small, g_temb, g_cap, g_wemb, g_wcap, g_aff = refs[18:28]
+    refs = refs[28:]
+    big, refs = refs[:BIG], refs[BIG:]
+    bufs = [dict(zip(Reducer.NAMES, refs[8 * a : 8 * a + 8])) for a in range(3)]
+    (bsem, gsend, grecv, msend, mrecv, ring, rsem, a3, g3, gt, acc, ng, pre_grad, res_grad,
+     mine, every, na, nb, pa, pb, tg_s, tg_r, mod_s, mod_r,
      gc_s, gc_r, pe_s, pe_r, gs_s, gs_r, ps_s, ps_r, aff_s, aff_r) = refs[24:]
     n_sp = 2 * nz
     at = Place()
     line = [at.rp(k, n_sp) for k in range(1, n_sp)]
     grid = img_peers(at)
     greet(line + grid)
+    loads = []
+    for j in range(BIG):
+        cp = pltpu.make_async_copy(hbm[j], big[j], bsem.at[j])
+        cp.start()
+        loads.append(cp)
+    od, dkv, w_small, res, cot, normed, act1, hidden, act0, x = big
+    ring_start(w_out, ring, rsem)
     mail = Mail(msend, mrecv)
-    red = Reducer(
-        at, nz,
-        [(g_out, True, s_out, bufs[0]), (g_small, True, s_small, bufs[1]), (dw, False, s_in, bufs[2])],
-        ssem, rsem, lsem,
-    )
-    pipe = Pipeline(red)
-    early = [red.load(0, 0, 3), red.load(0, 3, 6), red.load(0, 6, 9), red.load(1, 0, 1)]
-    px, c = u.shape
+    red = Reducer(at, nz, [(s_out, bufs[0]), (s_small, bufs[1]), (s_in, bufs[2])], gsend, grecv)
+    px, c = res.shape
     height = px // width
     members = px * n_sp * (c // GROUPS)
     d = c // HEADS
-    rows0, rows1 = rows[0], rows[1]
-    gain1, bias1, fac1 = rows1[0:1], rows1[1:2], rows1[2:3]
-
-    t1 = combine_sums(su1)
-    t2 = combine_sums(su2)
-    mod = jnp.concatenate([t1[1:2] * gain1 + t1[0:1] * bias1, t1[0:1]], axis=1)
+    cols = 3 * c // n_sp
+
+    def publish(j, rows01, edges):
+        out = []
+        for ref, above, below in edges:
+            out.append(mail.send(ref.at[px - width :], above, line[0]))
+            out.append(mail.send(ref.at[:width], below, line[-1]))
+        mine[j] = jnp.zeros((8, c), F32)
+        mine[j, 0:1] = rows01[0]
+        mine[j, 1:2] = rows01[1]
+        for dev in line:
+            out.append(mail.send(mine.at[j], every.at[j, at.s], dev))
+        every[j, at.s] = mine[j]
+        return out
+
+    for j in range(6):
+        loads[j].wait()
+    att = jnp.concatenate([od[h][:, :d] for h in range(HEADS)], axis=1)
+    pg = jnp.concatenate(
+        [od[h][:, d:] for h in range(HEADS)]
+        + [dkv[h][:, :d] for h in range(HEADS)]
+        + [dkv[h][:, d:] for h in range(HEADS)],
+        axis=1,
+    )
+    wq, wp = split_small(joined(w_small), n_sp)
+    ng[...] = dot(pg, wq, 1, 0)
+    center2, inverse2 = combine_stats(st2, px)
+    hat = (res[...] - center2) * inverse2
+    u = ng[...]
+    sums = (jnp.sum(u, axis=0, keepdims=True), jnp.sum(u * hat, axis=0, keepdims=True))
+    greeted(n_sp + 2)
+    round_2 = publish(2, sums, [(ng, na, nb)])
+    gq = dot(pg, normed[...], 0, 0).astype(BF16)
+    go = dot(cot[...], att, 0, 0).astype(BF16)
+    small = bufs[1]["d"]
     for j in range(n_sp):
-        mod_s[j] = jnp.broadcast_to(mod[:, j * 128 : (j + 1) * 128], (8, 128))
+        for b in range(4):
+            lanes = slice(b * 128, (b + 1) * 128)
+            small[j % 2, b, 0, j // 2, :cols] = gq[j * cols : (j + 1) * cols, lanes]
+            small[j % 2, b, 0, j // 2, cols:] = go[j * (c // n_sp) : (j + 1) * (c // n_sp), lanes]
+    red.add(1, 0, 1)
+    output[...] = (res[...] + dot(att, wp, 1, 1)).astype(BF16)
+
     first = 2 * lax.rem(at.s, nz)
     value = lax.div(at.s, nz)
     halves = []
@@ -1241,90 +1150,144 @@
         blk = dt_all[first + j].astype(F32)
         halves.append(jnp.where(value > 0, blk[:, d:], blk[:, :d]))
     tg_s[...] = jnp.concatenate(halves, axis=1).astype(BF16)
-    greeted(n_sp + 2)
-    for g in early:
-        pipe.add(g)
-    round_a = []
-    for dev in grid:
-        round_a.append(mail.send(tg_s, tg_r.at[at.i], dev))
-        round_a.append(mail.send(mod_s.at[at.s], mod_r.at[at.i], dev))
+    round_a = [mail.send(tg_s, tg_r.at[at.i], dev) for dev in grid]
     tg_r[at.i] = tg_s[...]
-    mod_r[at.i] = mod_s[at.s]
-
-    center, inverse = combine_stats(st1, px)
-    total = group_total(t1 * (gain1 * fac1)) / members
-    s1, s2 = total[0:1, :], total[1:2, :]
-    mul = gain1 * fac1
+
     has_up, has_dn = edge_flags(n_sp, at.s)
-    for r in range(height + 2):
-        cut = slice((r - 1) * width, r * width)
-        if r == 0:
-            uu, yy = ua[...], ya[...]
-        elif r == height + 1:
-            uu, yy = ub[...], yb[...]
-        else:
-            uu, yy = u[cut, :], y[cut, :]
-        g = inverse * (uu * mul - s1 - (yy - center) * inverse * s2)
-        if r == 0:
-            g = g * has_up
-        elif r == height + 1:
-            g = g * has_dn
-        shifted(g3, r, width, g.astype(BF16).astype(F32))
-        shifted(a3, r, width, act[r * width : (r + 1) * width, :].astype(F32))
-    gt[...] = g3[1, width : width + px, :].T
-    pipe.tick()
-
-    def weight_taps(t0, t1):
+
+    def upstream(j, uu, ua, ub, center, inverse, yy, ya, yb, act, base, keep):
+        total = combine_sums(every[j])
+        mul = rows[j, 0:1] * rows[j, 2:3]
+        back = group_total(total * mul) / members
+        s1, s2 = back[0:1, :], back[1:2, :]
+        for r in range(height + 2):
+            cut = slice((r - 1) * width, r * width)
+            top, end = r == 0, r == height + 1
+            un = ua[...] if top else ub[...] if end else uu[cut, :]
+            yn = ya[...] if top else yb[...] if end else yy[cut, :]
+            g = inverse * (un * mul - s1 - (yn - center) * inverse * s2)
+            if base:
+                g = g + (base[1][...] if top else base[2][...] if end else base[0][cut, :]).astype(F32)
+            if top:
+                g = g * has_up
+            elif end:
+                g = g * has_dn
+            elif keep is not None:
+                keep[cut, :] = g
+            shifted(g3, r, width, g.astype(BF16).astype(F32))
+            shifted(a3, r, width, act[r * width : (r + 1) * width, :].astype(F32))
+        gt[...] = g3[1, width : width + px, :].T
+        return total
+
+    def weight_taps(a, t0, t1):
+        dst = bufs[a]["d"]
+
         def one(tap, _):
             i, j = lax.div(tap, 3), lax.rem(tap, 3)
             part = dot(gt[...], a3[j, pl.ds(pl.multiple_of(i * width, width), px), :], 1, 0).astype(BF16)
-            for b in range(4):
-                dw[b, tap] = part[:, b * 128 : (b + 1) * 128].reshape(nz, 2, c // n_sp, 128)
+            r = c // n_sp
+            for k in range(n_sp):
+                for b in range(4):
+                    dst[k % 2, b, tap, k // 2] = part[k * r : (k + 1) * r, b * 128 : (b + 1) * 128]
             return 0
 
         lax.fori_loop(t0, t1, one, 0)
-        pipe.add(red.load(2, t0, t1))
-
-    def input_taps(t0, t1):
-        def one(tap, _):
+        red.add(a, t0, t1)
+
+    def input_taps(w):
+        def one(tap, wt):
             i, j = lax.div(tap, 3), lax.rem(tap, 3)
             lhs = g3[2 - j, pl.ds(pl.multiple_of((2 - i) * width, width), px), :]
-            part = dot(lhs, joined(w, tap), 1, 0)
-            acc[...] = part + jnp.where(tap > 0, acc[...], 0.0)
-            return 0
-
-        lax.fori_loop(t0, t1, one, 0)
-
-    weight_taps(0, 3)
-    pipe.tick()
-    weight_taps(3, 6)
+            acc[...] = dot(lhs, wt, 1, 0) + jnp.where(tap > 0, acc[...], 0.0)
+
+        conv_taps(0, 9, w, ring, rsem, one)
+
+    for cp in round_2:
+        cp.wait_recv()
+    loads[6].wait()
+    t2 = upstream(2, ng, na, nb, center2, inverse2, res, ra, rb, act1, (cot, ca, cb), res_grad)
+    red.run(1, 0)
+    for tap in (0, 3, 6):
+        weight_taps(0, tap, tap + 3)
+    red.run(2, 0)
+    input_taps(w_out)
+    ring_start(w_in, ring, rsem)
+    for j in range(7, BIG):
+        loads[j].wait()
+    center1, inverse1 = combine_stats(st1, px)
+    hat = (hidden[...] - center1) * inverse1
+    gain1, bias1, fac1 = rows[1, 0:1], rows[1, 1:2], rows[1, 2:3]
+    v = acc[...] * silu_slope(hat * (gain1 * fac1) + (bias1 * fac1 + rows[1, 3:4]))
+    pre_grad[...] = v
+    sums = (jnp.sum(v, axis=0, keepdims=True), jnp.sum(v * hat, axis=0, keepdims=True))
+    round_1 = publish(1, sums, [(pre_grad, pa, pb)])
+    red.run(1, 1, 2, 3)
+    red.run(3, 0)
+
+    exact = lambda a, b, ca_, cb_: lax.dot_general(
+        a, b, (((ca_,), (cb_,)), ((), ())), preferred_element_type=F32, precision=PRECISE
+    )
+    tokens = tg_s.shape[0]
+    share = tokens // n_sp
     for cp in round_a:
         cp.wait_recv()
-    tokens = tg_s.shape[0]
     flat_tg = tg_r[...].reshape(4 * tokens, 128)
     g_wcap[...] = dot(cap_all[...].reshape(4 * tokens, cap_all.shape[2]), flat_tg, 0, 0)
     gc_s[...] = dot(flat_tg, w_cap[...], 1, 1).astype(BF16).reshape(gc_s.shape)
-    mods = jnp.concatenate([mod_r[j][0:1] for j in range(4)] + [jnp.zeros((4, 128), F32)])
-    exact = lambda a, b, ca, cb: lax.dot_general(
-        a, b, (((ca,), (cb,)), ((), ())), preferred_element_type=F32, precision=PRECISE
-    )
-    emb_t = emb_all[...].T
-    g_wemb[...] = sum(emb_t[:, j : j + 1] * mods[j : j + 1] for j in range(4))
-    pe_s[...] = exact(mods, w_emb[...].astype(F32), 1, 1)
-    share = tokens // n_sp
     round_b = []
     for dev in line:
         cut = pl.ds(pl.multiple_of(dev[1] * share, share), share)
         round_b.append(mail.send(gc_s.at[:, cut, :], gc_r.at[at.s], dev))
-        round_b.append(mail.send(pe_s, pe_r.at[at.s], dev))
     gc_r[at.s] = gc_s[:, pl.ds(pl.multiple_of(at.s * share, share), share), :]
+
+    for cp in round_1:
+        cp.wait_recv()
+    t1 = upstream(1, pre_grad, pa, pb, center1, inverse1, hidden, ha, hb, act0, None, None)
+    mod = jnp.concatenate([t1[1:2] * gain1 + t1[0:1] * bias1, t1[0:1]], axis=1)
+    for j in range(n_sp):
+        mod_s[j] = jnp.broadcast_to(mod[:, j * 128 : (j + 1) * 128], (8, 128))
+    round_m = [mail.send(mod_s.at[at.s], mod_r.at[at.i], dev) for dev in grid]
+    mod_r[at.i] = mod_s[at.s]
+    red.run(2, 1)
+    weight_taps(2, 0, 3)
+    red.run(2, 2)
+    weight_taps(2, 3, 6)
+    red.run(2, 3)
+    weight_taps(2, 6, 9)
+    input_taps(w_in)
+
+    center0, inverse0 = combine_stats(st0, px)
+    hat = (x[...].astype(F32) - center0) * inverse0
+    gain0 = rows[0, 0:1]
+    v = acc[...] * silu_slope(hat * gain0 + rows[0, 1:2])
+    acc[...] = v
+    sums = (jnp.sum(v, axis=0, keepdims=True), jnp.sum(v * hat, axis=0, keepdims=True))
+    round_0 = publish(0, sums, [])
+    red.run(1, 4, 5, 6)
+    red.run(4, 0)
+    for cp in round_m:
+        cp.wait_recv()
+    mods = jnp.concatenate([mod_r[j][0:1] for j in range(4)] + [jnp.zeros((4, 128), F32)])
+    emb_t = emb_all[...].T
+    g_wemb[...] = sum(emb_t[:, j : j + 1] * mods[j : j + 1] for j in range(4))
+    pe_s[...] = exact(mods, w_emb[...].astype(F32), 1, 1)
+    round_p = [mail.send(pe_s, pe_r.at[at.s], dev) for dev in line]
     pe_r[at.s] = pe_s[...]
-    pipe.tick()
-    weight_taps(6, 9)
-    pipe.tick()
-    input_taps(0, 3)
-    pipe.tick()
-    for cp in round_b:
+    for cp in round_0:
+        cp.wait_recv()
+    t0 = combine_sums(every[0])
+    zero = jnp.zeros((2, c), F32)
+    aff = jnp.concatenate([t0[1:2], t1[1:2] * fac1, t2[1:2], t0[0:1], t1[0:1] * fac1, t2[0:1], zero])
+    for j in range(4):
+        aff_s[j] = aff[:, j * 128 : (j + 1) * 128]
+    round_e = [mail.send(aff_s.at[dev[0]], aff_r.at[at.i], dev) for dev in grid]
+    aff_r[at.i] = aff_s[at.i]
+    total = group_total(t0 * gain0) / members
+    image_grad[...] = res_grad[...] + inverse0 * (acc[...] * gain0 - total[0:1] - hat * total[1:2])
+    for g in (1, 2, 3):
+        red.run(3, g)
+        red.run(2, g + 3)
+    for cp in round_b + round_p:
         cp.wait_recv()
     gc = gc_r[0].astype(F32)
     pe = pe_r[0]
@@ -1340,73 +1303,53 @@
         round_c.append(mail.send(ps_s.at[dev[0]], ps_r.at[at.i], dev))
     gs_r[at.i] = gs_s[at.i]
     ps_r[at.i] = ps_s[at.i]
-    input_taps(3, 6)
-    pipe.tick()
-    input_taps(6, 9)
-    pipe.tick()
-
-    center, inverse = combine_stats(st0, px)
-    hat = (x[...].astype(F32) - center) * inverse
-    gain0 = rows0[0:1]
-    v = acc[...] * silu_slope(hat * gain0 + rows0[1:2])
-    acc[...] = v
-    mine[...] = jnp.zeros_like(mine)
-    mine[0:1, :] = jnp.sum(v, axis=0, keepdims=True)
-    mine[1:2, :] = jnp.sum(v * hat, axis=0, keepdims=True)
-    round_d = [mail.send(mine, every.at[at.s], dev) for dev in line]
-    every[at.s] = mine[...]
-    pipe.tick()
-    for cp in round_d:
-        cp.wait_recv()
-    t0 = combine_sums(every)
-    zero = jnp.zeros((2, c), F32)
-    aff = jnp.concatenate([t0[1:2], t1[1:2] * fac1, t2[1:2], t0[0:1], t1[0:1] * fac1, t2[0:1], zero])
-    for j in range(4):
-        aff_s[j] = aff[:, j * 128 : (j + 1) * 128]
-    round_e = [mail.send(aff_s.at[dev[0]], aff_r.at[at.i], dev) for dev in grid]
-    aff_r[at.i] = aff_s[at.i]
-    total = group_total(t0 * gain0) / members
-    image_grad[...] = res_grad[...] + inverse * (acc[...] * gain0 - total[0:1] - hat * total[1:2])
-    pipe.drain()
+    red.run(4, 1, 2, 3)
+    red.run(3, 4, 5, 6)
+    red.run(4, 4, 5, 6)
+    red.finish()
     for cp in round_c + round_e:
         cp.wait_recv()
     g_cap[...] = jnp.concatenate([gs_r[j] for j in range(4)], axis=1)
-    g_temb[...] = jnp.concatenate([ps_r[j] for j in range(4)], axis=1) * silu_slope(temb[...])
+    g_temb[...] = jnp.concatenate([ps_r[j] for j in range(4)], axis=1) * silu_slope(temb[...].astype(F32))
     g_aff[...] = aff_r[0] + aff_r[1] + aff_r[2] + aff_r[3]
-    red.finish()
     for cp in mail.sent:
         cp.wait_send()
 
 
-def tail_call(g_out, g_small, x, st0, rows, act, u, ua, ub, su1, su2, st1, y, ya, yb, w, res_grad,
-              dt_all, cap_all, emb_all, w_emb, w_cap, temb, nz, width, cid):
-    px, c = u.shape
+def backward_call(big, w_in, w_out, small, nz, width, cid):
+    px, c = big[3].shape
     n_sp = 2 * nz
     padded = px + 2 * width
     r = c // n_sp
-    rs = g_small.shape[4]
+    rs = big[2].shape[1] // n_sp
+    dt_all, cap_all = small[10], small[11]
     tokens = dt_all.shape[1]
     e = cap_all.shape[2]
     share = tokens // n_sp
-    ins = [g_out, g_small, x, st0, rows, act, u, ua, ub, su1, su2, st1, y, ya, yb, w, res_grad,
-           dt_all, cap_all, emb_all, w_emb, w_cap, temb]
-    outs = [(px, c), (9, r, 128), (9, r, 128), (1, rs, 128), (8, 4 * e), (share, 4 * e), (e, 128), (e, 128), (8, 128)]
+    outs = [
+        ((px, c), BF16), ((px, c), F32), ((9, r, 128), F32), ((9, r, 128), F32), ((1, rs, 128), F32),
+        ((8, 4 * e), F32), ((share, 4 * e), F32), ((e, 128), F32), ((e, 128), F32), ((8, 128), F32),
+    ]
     vm = pltpu.VMEM
     return pl.pallas_call(
-        functools.partial(tail_kernel, nz, width),
-        out_shape=[jax.ShapeDtypeStruct(s, F32) for s in outs],
-        in_specs=[ANY, ANY] + [VM] * (len(ins) - 2),
+        functools.partial(backward_kernel, nz, width),
+        out_shape=[jax.ShapeDtypeStruct(s, ty) for s, ty in outs],
+        in_specs=[ANY] * (len(big) + 2) + [VM] * len(small),
         out_specs=[VM] * len(outs),
-        scratch_shapes=Reducer.buffers(nz, 9, r) + Reducer.buffers(nz, 1, rs) + Reducer.buffers(nz, 9, r)
+        scratch_shapes=[vm(v.shape, v.dtype) for v in big]
+        + Reducer.buffers(nz, 9, r) + Reducer.buffers(nz, 1, rs) + Reducer.buffers(nz, 9, r)
         + [
-            pltpu.SemaphoreType.DMA((TAIL_GROUPS, 4 + nz)),
-            pltpu.SemaphoreType.DMA((TAIL_GROUPS, 4 + nz)),
-            pltpu.SemaphoreType.DMA((TAIL_GROUPS,)),
-            pltpu.SemaphoreType.DMA((TAIL_MAIL,)),
-            pltpu.SemaphoreType.DMA((TAIL_MAIL,)),
-            vm((4, 9, nz, 2, r, 128), BF16),
-            vm((3, padded, c), BF16), vm((3, padded, c), BF16), vm((c, px), BF16), vm((px, c), F32),
-            vm((8, c), F32), vm((n_sp, 8, c), F32),
+            pltpu.SemaphoreType.DMA((len(big),)),
+            pltpu.SemaphoreType.DMA((BACK_GROUPS, 4 + nz)),
+            pltpu.SemaphoreType.DMA((BACK_GROUPS, 4 + nz)),
+            pltpu.SemaphoreType.DMA((BACK_MAIL,)),
+            pltpu.SemaphoreType.DMA((BACK_MAIL,)),
+            vm((3, 4, c, 128), BF16),
+            pltpu.SemaphoreType.DMA((3,)),
+            vm((3, padded, c), BF16), vm((3, padded, c), BF16), vm((c, px), BF16),
+            vm((px, c), F32), vm((px, c), F32), vm((px, c), F32), vm((px, c), F32),
+            vm((3, 8, c), F32), vm((3, n_sp, 8, c), F32),
+            vm((width, c), F32), vm((width, c), F32), vm((width, c), F32), vm((width, c), F32),
             vm((tokens, 128), BF16), vm((4, tokens, 128), BF16),
             vm((n_sp, 8, 128), F32), vm((4, 8, 128), F32),
             vm((4, tokens, e), BF16), vm((n_sp, 4, share, e), BF16),
@@ -1416,8 +1359,55 @@
             vm((4, 8, 128), F32), vm((4, 8, 128), F32),
         ],
         compiler_params=params(cid),
-        name="first_backward_and_sums",
-    )(*ins)
+        name="backward",
+    )(*big, w_in, w_out, *small)
+
+
+def emit_kernel(cut, *refs):
+    ins, outs, mids, loads, stores = refs[:10], refs[10:22], refs[22:31], refs[31], refs[32]
+    output, image, s_in, s_out, s_small, g_temb, g_cap, g_wemb, g_wcap, g_aff = ins
+    pairs = [
+        (output, outs[0]), (image, outs[1]), (g_cap, outs[3]), (s_in, outs[4]), (s_out, outs[5]), (g_wemb, outs[6]),
+        (s_small.at[0, :cut], outs[7]), (g_wcap, outs[8]), (s_small.at[0, cut:], outs[9]),
+    ]
+    copies = [pltpu.make_async_copy(src, mid, loads.at[j]) for j, ((src, _), mid) in enumerate(zip(pairs, mids))]
+    for cp in copies:
+        cp.start()
+    backs = []
+    for j, cp in enumerate(copies):
+        cp.wait()
+        backs.append(pltpu.make_async_copy(mids[j], pairs[j][1], stores.at[j]))
+        backs[-1].start()
+    outs[2][...] = g_temb[0:1, :]
+    outs[10][...] = g_aff[0:3, :]
+    outs[11][...] = g_aff[3:6, :]
+    for cp in backs:
+        cp.wait()
+
+
+def emit_call(parts, cut):
+    output, image, s_in, s_out, s_small, g_temb, g_cap, g_wemb, g_wcap, g_aff = parts
+    rest = s_small.shape[1] - cut
+    like = lambda v: jax.ShapeDtypeStruct(v.shape, v.dtype)
+    f32 = lambda *s: jax.ShapeDtypeStruct(s, F32)
+    shapes = [
+        like(output), like(image), f32(1, g_temb.shape[1]), like(g_cap), like(s_in), like(s_out), like(g_wemb),
+        f32(cut, 128), like(g_wcap), f32(rest, 128), f32(3, 128), f32(3, 128),
+    ]
+    in_specs = [ANY] * 10
+    in_specs[5] = in_specs[9] = VM
+    out_specs = [ANY] * 12
+    out_specs[2] = out_specs[10] = out_specs[11] = VM
+    return pl.pallas_call(
+        functools.partial(emit_kernel, cut),
+        out_shape=shapes,
+        in_specs=in_specs,
+        out_specs=out_specs,
+        scratch_shapes=[pltpu.VMEM(shapes[j].shape, shapes[j].dtype) for j in (0, 1, 3, 4, 5, 6, 7, 8, 9)]
+        + [pltpu.SemaphoreType.DMA((9,)), pltpu.SemaphoreType.DMA((9,))],
+        compiler_params=params(),
+        name="emit",
+    )(*parts)
 
 
 def fast_body(
@@ -1434,54 +1424,30 @@
     cot = cotangent.reshape(px, c)
 
     flat = lambda w: w.transpose(1, 2, 3, 0).reshape(9, w.shape[3], w.shape[0])
-    small = jnp.concatenate([qkv_proj.T, out_proj.T], axis=0)[None]
-    affine = jnp.concatenate([norm_gains, norm_biases, jnp.zeros_like(norm_gains[:2])]).astype(F32)
-    temb = jnp.broadcast_to(time_embed.astype(F32), (8, time_embed.shape[1]))
-    emb = silu(temb).astype(BF16).astype(F32).reshape(8, 4, -1).transpose(1, 0, 2)
     (w_in, w_out, w_small, st0, xa, xb, ca, cb, rows, kv_all, cap_all, emb_all) = head_call(
-        [flat(conv_in), flat(conv_out), small], x, cot, emb, caption[0], embed_proj, caption_proj, affine, nz, width, 0
+        [flat(conv_in), flat(conv_out)], x, cot, time_embed, caption[0], embed_proj, caption_proj,
+        norm_gains, norm_biases, qkv_proj.T, out_proj.T, nz, width, 0,
     )
-    cut = qkv_proj.shape[1]
-    w_small = w_small.reshape(4, n_sp, -1, 128)
-    w_qkv = w_small[:, :, :cut].reshape(4, 3 * c, 128)
-    w_proj = w_small[:, :, cut:].reshape(4, c, 128)
-    bias = jnp.where(caption_mask > 0, 0.0, MASKED).astype(F32)
+    w_small = w_small.reshape(4, -1, 128)
 
     hidden, act0, st1, ha, hb = conv_call(x, xa, xb, st0, rows[0], w_in, None, n_sp, width, 1)
     res, act1, st2, ra, rb = conv_call(hidden, ha, hb, st1, rows[1], w_out, x, n_sp, width, 2)
-    normed, qk, vg = qkv_call(res, st2, rows[2], w_qkv, w_proj, cot, n_sp, 3)
-    od, dkv, dt = attention_call(qk.reshape(-1, 2 * d), vg.reshape(-1, 2 * d), kv_all, bias)
+    normed, qk, vg = qkv_call(res, st2, rows[2], w_small, cot, n_sp, 3)
+    od, dkv, dt = attention_call(qk.reshape(-1, 2 * d), vg.reshape(-1, 2 * d), kv_all, caption_mask)
     od, dkv, dt_all = trade([od.reshape(n_sp, px, 2 * d), dkv.reshape(n_sp, px, 2 * d)], dt, n_sp, 4)
 
-    output, g_out, g_qkv, ng, su2, na, nb = post_call(
-        od, dkv, w_qkv, w_proj, res, cot, normed, st2, rows[2], n_sp, width, 5
+    parts = backward_call(
+        [od, dkv, w_small, res, cot, normed, act1, hidden, act0, x], w_in, w_out,
+        [st0, st1, st2, rows, ca, cb, ra, rb, ha, hb, dt_all, cap_all, emb_all, embed_proj, caption_proj, time_embed],
+        nz, width, 5,
     )
-    g_conv_out, pre_grad, su1, pa, pb, res_grad = back_call(
-        hidden, st1, rows[1], act1, ng, na, nb, su2, st2, rows[2], res, ra, rb,
-        (cot, ca, cb), w_out, n_sp, width, 6,
-    )
-    g_small = jnp.concatenate(
-        [g_qkv.reshape(4, n_sp, cut, 128), g_out.reshape(4, n_sp, c // n_sp, 128)], axis=2
-    ).reshape(4, 1, nz, 2, -1, 128)
-    g_conv_out = g_conv_out.reshape(4, 9, nz, 2, -1, 128)
-    grad_image, s_in, s_out, s_small, g_temb, g_cap, g_wemb, g_wcap, g_aff = tail_call(
-        g_conv_out, g_small, x, st0, rows, act0, pre_grad, pa, pb, su1, su2, st1, hidden, ha, hb, w_in, res_grad,
-        dt_all, cap_all, emb_all, embed_proj, caption_proj, temb, nz, width, 7,
+    output, image, g_temb, g_cap, s_in, s_out, g_wemb, g_qkv, g_wcap, g_out, g_gains, g_biases = emit_call(
+        parts, qkv_proj.shape[1]
     )
     unflat = lambda g: g.reshape(3, 3, g.shape[1], 128).transpose(3, 0, 1, 2)
     return (
-        output.reshape(image_in.shape),
-        grad_image.reshape(image_in.shape),
-        g_temb[:1],
-        g_cap[None],
-        unflat(s_in),
-        unflat(s_out),
-        g_wemb,
-        s_small[0, :cut].T,
-        g_wcap,
-        s_small[0, cut:].T,
-        g_aff[:3],
-        g_aff[3:6],
+        output.reshape(image_in.shape), image.reshape(image_in.shape), g_temb, g_cap[None], unflat(s_in), unflat(s_out),
+        g_wemb, g_qkv.T, g_wcap, g_out.T, g_gains, g_biases,
     )
 
 

time: 438 us -> 376 us (0.86)
  Pallas kernels: 412 us -> 374 us
  local copies, waits for them, and re-layouts: 17.3 us -> 1.37 us
  other arithmetic: 7.16 us -> 0 us
    pallas_call x3 -> x2, Pallas kernels: 141 us -> 104 us  [the longest x1 99.9 us: backward_call(): pl.pallas_call(functools.partial(backward_kernel, nz, width), out_shape=[...]
    unnamed x25 -> x0, local copies, waits for them, and re-layouts: 6.62 us -> none
    slice x4 -> x0, local copies, waits for them, and re-layouts: 4.89 us -> none  [the longest x1 1.44 us: fast_body(): g_temb[:1]]
where the time goes in v3:
time: 376 us
  Pallas kernels  374 us (99%)
    pallas_call x1, Pallas kernels, backward_call(): pl.pallas_call(functools.partial(backward_kernel, nz, width), out_shape=[...  99.9 us
    pallas_call x1, Pallas kernels, head_call(): pl.pallas_call(functools.partial(head_kernel, nz, width, dims), out_shape...  71.7 us
    pallas_call x1, Pallas kernels, attention_call(): pl.pallas_call(functools.partial(attention_kernel, L, T, BQ, BK), grid=(L...  65.4 us
    pallas_call x1, Pallas kernels, trade(): pl.pallas_call(functools.partial(trade_kernel, n_sp, na), out_shape=[jax....  53.4 us
    pallas_call x1, Pallas kernels, qkv_call(): pl.pallas_call(functools.partial(qkv_kernel, n_sp), out_shape=[jax.ShapeD...  40 us
    pallas_call x2, Pallas kernels, conv_call(): pl.pallas_call(functools.partial(conv_kernel, n_sp, width, base is not No...  38.7 us

profile of v3, /device:TPU:0, one launch (start us, length us, event | category | flops | bytes accessed | tf_op | source)
XLA Modules:
  0.0 375.8 jit_solution(12261774009326880528)
XLA Ops:
  0.6 71.7 %gather_weights.1 = (bf16[4,9,512,128]{3,2,1,0:T(8,128)(2,1)}, bf16[4,9,512,128]{3,2,1,0:T(8,128)(2,1)}, bf16[4,1,2048,128]{3,2,1,0:T(8,128)(2,1)}, f32[8,8,512]...) custom-call(bf16[9,64,128]{2,1,0:T(8,128)(2,1)} %bitcast.47, ...), custom_call_target="tpu_custom_call" | custom-call | tf_op jit(solution)/shard_map/gather_weights/pallas_call | solution.py:904
  72.4 1.4 slice_bitcast_fusion
  73.8 20.0 %conv_forward.2 = (f32[512,512]{1,0:T(8,128)}, bf16[640,512]{1,0:T(8,128)(2,1)}, f32[8,8,512]{2,1,0:T(8,128)}, f32[64,512]{1,0:T(8,128)}, f32[64,512]{1,0:T(8,128)}) custom-call(bf16[512,512]{1,0:T(8,128)(2,1)} %bitcast.36, bf16[64,512]{1,0:T(8,128)(2,1)} %get-tuple-element.65.up, bf16[64,512]{1,0:T(8,128)(2,1)} %get-tuple-element.66.dn, ...), custom_call_target="tpu_custom_call" | custom-call | tf_op jit(solution)/shard_map/conv_forward/pallas_call | solution.py:560
  93.8 18.7 %conv_forward.3 = (f32[512,512]{1,0:T(8,128)}, bf16[640,512]{1,0:T(8,128)(2,1)}, f32[8,8,512]{2,1,0:T(8,128)}, f32[64,512]{1,0:T(8,128)}, f32[64,512]{1,0:T(8,128)}) custom-call(f32[512,512]{1,0:T(8,128)} %get-tuple-element.70.x.refs_7_, f32[64,512]{1,0:T(8,128)} %get-tuple-element.71.up.refs_20_, f32[64,512]{1,0:T(8,128)} %get-tuple-element.72.dn.refs_21_, ...), custom_call_target="tpu_custom_call" | custom-call | tf_op jit(solution)/shard_map/conv_forward/pallas_call | solution.py:560
  112.5 40.0 %project_and_send.1 = (bf16[512,512]{1,0:T(8,128)(2,1)}, bf16[8,512,128]{2,1,0:T(8,128)(2,1)}, bf16[8,512,128]{2,1,0:T(8,128)(2,1)}) custom-call(f32[512,512]{1,0:T(8,128)} %get-tuple-element.75.res.refs_3_, f32[8,8,512]{2,1,0:T(8,128)} %get-tuple-element.76.every.refs_14_, f32[8,512]{1,0:T(8,128)} %get-tuple-element.118.rows, ...), custom_call_target="tpu_custom_call" | custom-call | tf_op jit(solution)/shard_map/project_and_send/pallas_call | solution.py:610
  152.5 65.4 %attention.1 = (bf16[4096,128]{1,0:T(8,128)(2,1)}, bf16[4096,128]{1,0:T(8,128)(2,1)}, bf16[128,128]{1,0:T(8,128)(2,1)}) custom-call(bf16[4096,128]{1,0:T(8,128)(2,1)} %bitcast.42, bf16[4096,128]{1,0:T(8,128)(2,1)} %bitcast.43, bf16[8,128,128]{2,1,0:T(8,128)(2,1)} %get-tuple-element.80.text, s32[1,128]{1,0:T(1,128)} %keep.1), custom_call_target="tpu_custom_call" | custom-call | tf_op jit(solution)/shard_map/attention/pallas_call | solution.py:694
  217.9 53.4 %trade.1 = (bf16[8,512,128]{2,1,0:T(8,128)(2,1)}, bf16[8,512,128]{2,1,0:T(8,128)(2,1)}, bf16[8,128,128]{2,1,0:T(8,128)(2,1)}) custom-call(bf16[8,512,128]{2,1,0:T(8,128)(2,1)} %bitcast.44, bf16[8,512,128]{2,1,0:T(8,128)(2,1)} %bitcast.45, bf16[128,128]{1,0:T(8,128)(2,1)} %get-tuple-element.83.refs_2_), custom_call_target="tpu_custom_call" | custom-call | tf_op jit(solution)/shard_map/trade/pallas_call | solution.py:380
  271.3 99.9 %backward.1 = (bf16[512,512]{1,0:T(8,128)(2,1)}, f32[512,512]{1,0:T(8,128)}, f32[9,64,128]{2,1,0:T(8,128)}, f32[9,64,128]{2,1,0:T(8,128)}, f32[1,256,128]{2,1,0:...) custom-call(bf16[8,512,128]{2,1,0:T(8,128)(2,1)} %get-tuple-element., ...), custom_call_target="tpu_custom_call" | custom-call | tf_op jit(solution)/shard_map/backward/pallas_call | solution.py:1334
  371.2 4.4 %emit.1 = (bf16[512,512]{1,0:T(8,128)(2,1)}, f32[512,512]{1,0:T(8,128)}, f32[1,2048]{1,0:T(1,128)}, f32[16,2048]{1,0:T(8,128)}, f32[9,64,128]{2,1,0:T(8,128)}, /...) custom-call(bf16[512,512]{1,0:T(8,128)(2,1)} %get-tuple-element.96.r, ...), custom_call_target="tpu_custom_call" | custom-call | tf_op jit(solution)/shard_map/emit/pallas_call | solution.py:1401

commit v4 on v3

--- a/solution.py
+++ b/solution.py
@@ -351,45 +351,6 @@
 
 ANY = pl.BlockSpec(memory_space=pl.ANY)
 VM = pl.BlockSpec(memory_space=pltpu.VMEM)
-def trade_kernel(n_sp, na, *refs):
-    ins, outs = refs[: na + 1], refs[na + 1 : 2 * na + 2]
-    ssem, rsem, lsem = refs[2 * na + 2 :]
-    at = Place()
-    peers = [at.rp(k, n_sp) for k in range(1, n_sp)]
-    greet(peers)
-    local = [pltpu.make_async_copy(ins[a].at[at.s], outs[a].at[at.s], lsem.at[a]) for a in range(na)]
-    local.append(pltpu.make_async_copy(ins[na], outs[na].at[at.s], lsem.at[na]))
-    for cp in local:
-        cp.start()
-    greeted(len(peers))
-    sent = []
-    for k in range(1, n_sp):
-        dev = at.rp(k, n_sp)
-        for a in range(na):
-            sent.append(remote(ins[a].at[dev[1]], outs[a].at[at.s], ssem.at[a, k], rsem.at[a, k], dev))
-        sent.append(remote(ins[na], outs[na].at[at.s], ssem.at[na, k], rsem.at[na, k], dev))
-    for cp in local:
-        cp.wait()
-    for cp in sent:
-        cp.wait()
-
-
-def trade(parts, common, n_sp, cid):
-    na = len(parts)
-    shapes = [p.shape for p in parts] + [(n_sp,) + common.shape]
-    return pl.pallas_call(
-        functools.partial(trade_kernel, n_sp, na),
-        out_shape=[jax.ShapeDtypeStruct(s, BF16) for s in shapes],
-        in_specs=[ANY] * (na + 1),
-        out_specs=[ANY] * (na + 1),
-        scratch_shapes=[
-            pltpu.SemaphoreType.DMA((na + 1, n_sp)),
-            pltpu.SemaphoreType.DMA((na + 1, n_sp)),
-            pltpu.SemaphoreType.DMA((na + 1,)),
-        ],
-        compiler_params=params(cid),
-        name="trade",
-    )(*parts, common)
 
 
 def exchange_scratch(n_sp, width, halo_types, chans):
@@ -569,145 +530,196 @@
     )(*ins)
 
 
-def qkv_kernel(n_sp, res, every, rows, w_small, cot, normed, qk, vg, qk_s, vg_s, ssem, rsem, lsem):
-    at = Place()
+def project_kernel(n_sp, res, every, rows, w_small, cot, normed, kv, qg):
     px, c = res.shape
     d = c // HEADS
-    peers = [at.rp(k, n_sp) for k in range(1, n_sp)]
-    greet(peers)
     center, inverse = combine_stats(every, px)
     n = ((res[...] - center) * (inverse * rows[0:1, :]) + rows[1:2, :]).astype(BF16)
     normed[...] = n
     wq, wp = split_small(joined(w_small), n_sp)
-    q = dot(n, wq[:c], 1, 1).astype(BF16)
+    q = (dot(n, wq[:c], 1, 1).astype(BF16).astype(F32) * (d ** -0.5)).astype(BF16)
     k = dot(n, wq[c : 2 * c], 1, 1).astype(BF16)
     v = dot(n, wq[2 * c :], 1, 1).astype(BF16)
     g = dot(cot[...], wp, 1, 0).astype(BF16)
     for h in range(HEADS):
         cut = slice(h * d, (h + 1) * d)
-        qk_s[h] = jnp.concatenate([q[:, cut], k[:, cut]], axis=1)
-        vg_s[h] = jnp.concatenate([v[:, cut], g[:, cut]], axis=1)
-    local = []
-    for a, (src, dst) in enumerate(((qk_s, qk), (vg_s, vg))):
-        cp = pltpu.make_async_copy(src.at[at.s], dst.at[at.s], lsem.at[a])
+        kv[h] = jnp.concatenate([k[:, cut], v[:, cut]], axis=1)
+        qg[h] = jnp.concatenate([q[:, cut], g[:, cut]], axis=1)
+
+
+def project_call(res, every, rows, w_small, cot, n_sp):
+    px, c = res.shape
+    big = jax.ShapeDtypeStruct((HEADS, px, 128), BF16)
+    return pl.pallas_call(
+        functools.partial(project_kernel, n_sp),
+        out_shape=[jax.ShapeDtypeStruct((px, c), BF16), big, big],
+        in_specs=[VM] * 5,
+        out_specs=[VM] * 3,
+        compiler_params=params(),
+        name="project",
+    )(res, every, rows, w_small, cot)
+
+
+def attention_kernel(
+    n_sp, BQ, BK, kv, qg, text, keep, od, dkv, dt,
+    kv_r, qg_r, od_s, dkv_s, dt_s, k_s, v_s, s_s, e_s, dk_s, dv_s, lsem, ssem, rsem,
+):
+    at = Place()
+    px = kv.shape[1]
+    L, T = n_sp * px, text.shape[1]
+    d = kv.shape[2] // 2
+    line = [at.rp(k, n_sp) for k in range(1, n_sp)]
+    greet(line)
+    own = [
+        pltpu.make_async_copy(kv.at[at.s], kv_r.at[at.s], lsem.at[0]),
+        pltpu.make_async_copy(qg.at[at.s], qg_r.at[at.s], lsem.at[1]),
+    ]
+    for cp in own:
         cp.start()
-        local.append(cp)
-    greeted(len(peers))
-    sent = []
-    for j in range(1, n_sp):
-        dev = at.rp(j, n_sp)
-        for a, (src, dst) in enumerate(((qk_s, qk), (vg_s, vg))):
-            sent.append(remote(src.at[dev[1]], dst.at[at.s], ssem.at[a, j], rsem.at[a, j], dev))
+    greeted(n_sp - 1)
+    sent = [remote(kv.at[dev[1]], kv_r.at[at.s], ssem.at[0, k + 1], rsem.at[0, k + 1], dev) for k, dev in enumerate(line)]
+    odd = lax.rem(at.s, 2)
+    pair = lax.div(at.s, 2)
+    ones = (lax.broadcasted_iota(jnp.int32, (1, d), 1) == 0).astype(BF16)
+    picked = []
+    for j in (pair, HEADS // 2 + pair):
+        blk = text[j].astype(F32)
+        picked.append(jnp.where(odd > 0, blk[:, d:], blk[:, :d]).astype(BF16))
+    k_s[0:T, :] = picked[0]
+    v_s[0:T, :] = jnp.concatenate([picked[1], jnp.broadcast_to(ones, (T, d))], axis=1)
+    dk_s[...] = jnp.zeros_like(dk_s)
+    dv_s[...] = jnp.zeros_like(dv_s)
+
+    def take(j):
+        rows = pl.ds(pl.multiple_of(T + j * px, px if T % px == 0 else T), px)
+        k_s[rows, :] = kv_r[j][:, :d]
+        v_s[rows, :] = jnp.concatenate([kv_r[j][:, d:], jnp.broadcast_to(ones, (px, d))], axis=1)
+
+    for cp in own:
+        cp.wait()
+    take(at.s)
+    for k in range(1, n_sp):
+        sent[k - 1].wait_recv()
+        take(lax.rem(at.s - k + n_sp, n_sp))
+    sent += [remote(qg.at[dev[1]], qg_r.at[at.s], ssem.at[1, k + 1], rsem.at[1, k + 1], dev) for k, dev in enumerate(line)]
+
+    blocks = [(0, T)] + [(T + j * BK, BK) for j in range(L // BK)]
+    per = px // BQ
+    scale = d ** -0.5
+
+    def query_copy(k):
+        return pltpu.make_async_remote_copy(
+            src_ref=qg.at[at.s], dst_ref=qg_r.at[at.s], send_sem=ssem.at[1, k], recv_sem=rsem.at[1, k],
+            device_id=(at.i, lax.rem(at.s + k, n_sp)), device_id_type=MESH,
+        )
+
+    def back_copy(k, o):
+        return pltpu.make_async_remote_copy(
+            src_ref=od_s.at[o], dst_ref=od.at[at.s], send_sem=ssem.at[2, k], recv_sem=rsem.at[2, k],
+            device_id=(at.i, o), device_id_type=MESH,
+        )
+
+    def step(t, _):
+        k, part = lax.div(t, per), lax.rem(t, per)
+        o_dev = lax.rem(at.s - k + n_sp, n_sp)
+
+        @pl.when(jnp.logical_and(part == 0, k > 0))
+        def _():
+            query_copy(k).wait_recv()
+
+        r = pl.ds(pl.multiple_of(part * BQ, BQ), BQ)
+        both = qg_r[o_dev, r, :]
+        q, g = both[:, :d], both[:, d:]
+        peak = None
+        for st, n in blocks:
+            s = dot(q, k_s[st : st + n, :], 1, 1)
+            if st == 0:
+                s = jnp.where(keep[...] > 0, s, MASKED)
+            s_s[:, st : st + n] = s
+            for j in range(n // 128):
+                piece = s[:, 128 * j : 128 * j + 128]
+                peak = piece if peak is None else jnp.maximum(peak, piece)
+        peak = jnp.max(peak, axis=1, keepdims=True)
+        o = jnp.zeros((BQ, 2 * d), F32)
+        for st, n in blocks:
+            e = jnp.exp(s_s[:, st : st + n] - peak).astype(BF16)
+            e_s[:, st : st + n] = e
+            o = o + dot(e, v_s[st : st + n, :], 1, 0)
+        inverse = 1.0 / o[:, d : d + 1]
+        o = o[:, :d] * inverse
+        g = g.astype(F32) * inverse
+        row = jnp.sum(o * g, axis=1, keepdims=True)
+        g = g.astype(BF16)
+        gt, qt = g.T, q.T
+        dq = jnp.zeros((BQ, d), F32)
+        for st, n in blocks:
+            e = e_s[:, st : st + n]
+            dp = dot(g, v_s[st : st + n, :d], 1, 1)
+            ds = (e.astype(F32) * (dp - row)).astype(BF16)
+            dq = dq + dot(ds, k_s[st : st + n, :], 1, 0)
+            dv_s[:, st : st + n] += dot(gt, e, 1, 0)
+            dk_s[:, st : st + n] += dot(qt, ds, 1, 0)
+        od_s[o_dev, r, :] = jnp.concatenate([o, dq * scale], axis=1).astype(BF16)
+
+        @pl.when(jnp.logical_and(part == per - 1, k > 0))
+        def _():
+            back_copy(k, o_dev).start()
+
+        return 0
+
+    lax.fori_loop(0, n_sp * per, step, 0)
+    local = [pltpu.make_async_copy(od_s.at[at.s], od.at[at.s], lsem.at[2])]
+
+    def gradients(st, n):
+        return jnp.concatenate([dk_s[:, st : st + n], dv_s[:, st : st + n]], axis=0).astype(BF16).T
+
+    for j in range(n_sp):
+        dkv_s[j] = gradients(T + j * px, px)
+    for k, dev in enumerate(line):
+        sent.append(remote(dkv_s.at[dev[1]], dkv.at[at.s], ssem.at[3, k + 1], rsem.at[3, k + 1], dev))
+    dt_s[...] = gradients(0, T)
+    for k, dev in enumerate(line):
+        sent.append(remote(dt_s, dt.at[at.s], ssem.at[4, k + 1], rsem.at[4, k + 1], dev))
+    local.append(pltpu.make_async_copy(dkv_s.at[at.s], dkv.at[at.s], lsem.at[3]))
+    local.append(pltpu.make_async_copy(dt_s, dt.at[at.s], lsem.at[4]))
+    for cp in local:
+        cp.start()
+    for k in range(1, n_sp):
+        back_copy(k, lax.rem(at.s - k + n_sp, n_sp)).wait()
+    for cp in sent[n_sp - 1 : 2 * (n_sp - 1)]:
+        cp.wait_send()
+    for cp in sent[: n_sp - 1]:
+        cp.wait_send()
+    for cp in sent[2 * (n_sp - 1) :]:
+        cp.wait()
     for cp in local:
         cp.wait()
-    for cp in sent:
-        cp.wait()
-
-
-def qkv_call(res, every, rows, w_small, cot, n_sp, cid):
-    px, c = res.shape
-    big = jax.ShapeDtypeStruct((n_sp, px, 128), BF16)
+
+
+def attention_call(kv, qg, text, keep, cid):
+    n_sp, px, d2 = kv.shape
+    T = text.shape[1]
+    L = n_sp * px
+    d = d2 // 2
+    BQ, BK = 256, 1024
+    outs = [(n_sp, px, d2), (n_sp, px, d2), (n_sp, T, d2)]
+    vm = pltpu.VMEM
     return pl.pallas_call(
-        functools.partial(qkv_kernel, n_sp),
-        out_shape=[jax.ShapeDtypeStruct((px, c), BF16), big, big],
-        in_specs=[VM] * 5,
-        out_specs=[VM, ANY, ANY],
+        functools.partial(attention_kernel, n_sp, BQ, BK),
+        out_shape=[jax.ShapeDtypeStruct(s, BF16) for s in outs],
+        in_specs=[ANY, ANY, VM, VM],
+        out_specs=[ANY] * 3,
         scratch_shapes=[
-            pltpu.VMEM((HEADS, px, 128), BF16),
-            pltpu.VMEM((HEADS, px, 128), BF16),
-            pltpu.SemaphoreType.DMA((2, n_sp)),
-            pltpu.SemaphoreType.DMA((2, n_sp)),
-            pltpu.SemaphoreType.DMA((2,)),
+            vm((n_sp, px, d2), BF16), vm((n_sp, px, d2), BF16), vm((n_sp, px, d2), BF16), vm((n_sp, px, d2), BF16),
+            vm((T, d2), BF16), vm((T + L, d), BF16), vm((T + L, d2), BF16),
+            vm((BQ, T + L), F32), vm((BQ, T + L), BF16), vm((d, T + L), F32), vm((d, T + L), F32),
+            pltpu.SemaphoreType.DMA((5,)),
+            pltpu.SemaphoreType.DMA((5, n_sp)),
+            pltpu.SemaphoreType.DMA((5, n_sp)),
         ],
         compiler_params=params(cid),
-        name="project_and_send",
-    )(res, every, rows, w_small, cot)
-
-
-def attention_kernel(L, T, BQ, BK, qk, vg, text, keep, od, dkv, dt, k_s, v_s, s_s, e_s, dk_s, dv_s):
-    d = qk.shape[1] // 2
-    step = pl.program_id(0)
-
-    @pl.when(step == 0)
-    def _():
-        ones = (lax.broadcasted_iota(jnp.int32, (1, d), 1) == 0).astype(BF16)
-        head = lax.axis_index("sp")
-        pair, odd = lax.div(head, 2), lax.rem(head, 2)
-        picked = []
-        for j in (pair, HEADS // 2 + pair):
-            blk = text[j].astype(F32)
-            picked.append(jnp.where(odd > 0, blk[:, d:], blk[:, :d]).astype(BF16))
-        k_s[0:T, :] = picked[0]
-        v_s[0:T, :] = jnp.concatenate([picked[1], jnp.broadcast_to(ones, (T, d))], axis=1)
-        k_s[T:, :] = qk[:, d:]
-        v_s[T:, :] = jnp.concatenate([vg[:, :d], jnp.broadcast_to(ones, (L, d))], axis=1)
-        dk_s[...] = jnp.zeros_like(dk_s)
-        dv_s[...] = jnp.zeros_like(dv_s)
-
-    r = pl.ds(pl.multiple_of(step * BQ, BQ), BQ)
-    scale = d ** -0.5
-    q = (qk[r, :][:, :d].astype(F32) * scale).astype(BF16)
-    g = vg[r, :][:, d:]
-    blocks = [(0, T)] + [(T + j * BK, BK) for j in range(L // BK)]
-    peak = None
-    for at, n in blocks:
-        s = dot(q, k_s[at : at + n, :], 1, 1)
-        if at == 0:
-            s = jnp.where(keep[...] > 0, s, MASKED)
-        s_s[:, at : at + n] = s
-        for j in range(n // 128):
-            part = s[:, 128 * j : 128 * j + 128]
-            peak = part if peak is None else jnp.maximum(peak, part)
-    peak = jnp.max(peak, axis=1, keepdims=True)
-    o = jnp.zeros((BQ, 2 * d), F32)
-    for at, n in blocks:
-        e = jnp.exp(s_s[:, at : at + n] - peak).astype(BF16)
-        e_s[:, at : at + n] = e
-        o = o + dot(e, v_s[at : at + n, :], 1, 0)
-    inverse = 1.0 / o[:, d : d + 1]
-    o = o[:, :d] * inverse
-    g = g.astype(F32) * inverse
-    row = jnp.sum(o * g, axis=1, keepdims=True)
-    g = g.astype(BF16)
-    gt, qt = g.T, q.T
-    dq = jnp.zeros((BQ, d), F32)
-    for at, n in blocks:
-        e = e_s[:, at : at + n]
-        dp = dot(g, v_s[at : at + n, :d], 1, 1)
-        ds = (e.astype(F32) * (dp - row)).astype(BF16)
-        dq = dq + dot(ds, k_s[at : at + n, :], 1, 0)
-        dv_s[:, at : at + n] += dot(gt, e, 1, 0)
-        dk_s[:, at : at + n] += dot(qt, ds, 1, 0)
-    od[...] = jnp.concatenate([o, dq * scale], axis=1).astype(BF16)
-
-    @pl.when(step == pl.num_programs(0) - 1)
-    def _():
-        both = jnp.concatenate([dk_s[...], dv_s[...]], axis=0).astype(BF16).T
-        dt[...] = both[:T]
-        dkv[...] = both[T:]
-
-
-def attention_call(qk, vg, text, keep):
-    (L, d2), T = qk.shape, text.shape[1]
-    BQ, BK = 256, 1024
-    full = lambda shape: pl.BlockSpec(shape, lambda t: (0, 0))
-    return pl.pallas_call(
-        functools.partial(attention_kernel, L, T, BQ, BK),
-        grid=(L // BQ,),
-        in_specs=[full((L, d2)), full((L, d2)), pl.BlockSpec(text.shape, lambda t: (0, 0, 0)), full((1, T))],
-        out_specs=[pl.BlockSpec((BQ, d2), lambda t: (t, 0)), full((L, d2)), full((T, d2))],
-        out_shape=[jax.ShapeDtypeStruct(s, BF16) for s in ((L, d2), (L, d2), (T, d2))],
-        scratch_shapes=[
-            pltpu.VMEM((T + L, d2 // 2), BF16),
-            pltpu.VMEM((T + L, d2), BF16),
-            pltpu.VMEM((BQ, T + L), F32),
-            pltpu.VMEM((BQ, T + L), BF16),
-            pltpu.VMEM((d2 // 2, T + L), F32),
-            pltpu.VMEM((d2 // 2, T + L), F32),
-        ],
-        compiler_params=params(None, 1),
         name="attention",
-    )(qk, vg, text, keep)
+    )(kv, qg, text, keep)
 
 
 class Mail:
@@ -1432,9 +1444,8 @@
 
     hidden, act0, st1, ha, hb = conv_call(x, xa, xb, st0, rows[0], w_in, None, n_sp, width, 1)
     res, act1, st2, ra, rb = conv_call(hidden, ha, hb, st1, rows[1], w_out, x, n_sp, width, 2)
-    normed, qk, vg = qkv_call(res, st2, rows[2], w_small, cot, n_sp, 3)
-    od, dkv, dt = attention_call(qk.reshape(-1, 2 * d), vg.reshape(-1, 2 * d), kv_all, caption_mask)
-    od, dkv, dt_all = trade([od.reshape(n_sp, px, 2 * d), dkv.reshape(n_sp, px, 2 * d)], dt, n_sp, 4)
+    normed, kv, qg = project_call(res, st2, rows[2], w_small, cot, n_sp)
+    od, dkv, dt_all = attention_call(kv, qg, kv_all, caption_mask, 3)
 
     parts = backward_call(
         [od, dkv, w_small, res, cot, normed, act1, hidden, act0, x], w_in, w_out,

time: 376 us -> 332 us (0.88)
  Pallas kernels: 374 us -> 329 us
    pallas_call x3 -> x2, Pallas kernels: 159 us -> 126 us  [the longest x1 121 us: attention_call(): pl.pallas_call(functools.partial(attention_kernel, n_sp, BQ, BK), out_sha...]
    pallas_call x1, Pallas kernels: 99.9 us -> 88.3 us  [backward_call(): pl.pallas_call(functools.partial(backward_kernel, nz, width), out_shape=[...]
where the time goes in v4:
time: 332 us
  Pallas kernels  329 us (99%)
    pallas_call x1, Pallas kernels, attention_call(): pl.pallas_call(functools.partial(attention_kernel, n_sp, BQ, BK), out_sha...  121 us
    pallas_call x1, Pallas kernels, backward_call(): pl.pallas_call(functools.partial(backward_kernel, nz, width), out_shape=[...  88.3 us
    pallas_call x1, Pallas kernels, head_call(): pl.pallas_call(functools.partial(head_kernel, nz, width, dims), out_shape...  71.7 us
    pallas_call x2, Pallas kernels, conv_call(): pl.pallas_call(functools.partial(conv_kernel, n_sp, width, base is not No...  38.7 us

profile of v4, /device:TPU:0, one launch (start us, length us, event | category | flops | bytes accessed | tf_op | source)
XLA Modules:
  0.0 331.6 jit_solution(4704714322379935841)
XLA Ops:
  0.6 71.7 %gather_weights.1 = (bf16[4,9,512,128]{3,2,1,0:T(8,128)(2,1)}, bf16[4,9,512,128]{3,2,1,0:T(8,128)(2,1)}, bf16[4,1,2048,128]{3,2,1,0:T(8,128)(2,1)}, f32[8,8,512]...) custom-call(bf16[9,64,128]{2,1,0:T(8,128)(2,1)} %bitcast.39, ...), custom_call_target="tpu_custom_call" | custom-call | tf_op jit(solution)/shard_map/gather_weights/pallas_call | solution.py:916
  72.4 1.4 slice_bitcast_fusion
  73.8 20.1 %conv_forward.2 = (f32[512,512]{1,0:T(8,128)}, bf16[640,512]{1,0:T(8,128)(2,1)}, f32[8,8,512]{2,1,0:T(8,128)}, f32[64,512]{1,0:T(8,128)}, f32[64,512]{1,0:T(8,128)}) custom-call(bf16[512,512]{1,0:T(8,128)(2,1)} %bitcast.32, bf16[64,512]{1,0:T(8,128)(2,1)} %get-tuple-element.62.up, bf16[64,512]{1,0:T(8,128)(2,1)} %get-tuple-element.63.dn, ...), custom_call_target="tpu_custom_call" | custom-call | tf_op jit(solution)/shard_map/conv_forward/pallas_call | solution.py:521
  93.9 18.6 %conv_forward.3 = (f32[512,512]{1,0:T(8,128)}, bf16[640,512]{1,0:T(8,128)(2,1)}, f32[8,8,512]{2,1,0:T(8,128)}, f32[64,512]{1,0:T(8,128)}, f32[64,512]{1,0:T(8,128)}) custom-call(f32[512,512]{1,0:T(8,128)} %get-tuple-element.67.x.refs_7_, f32[64,512]{1,0:T(8,128)} %get-tuple-element.68.up.refs_20_, f32[64,512]{1,0:T(8,128)} %get-tuple-element.69.dn.refs_21_, ...), custom_call_target="tpu_custom_call" | custom-call | tf_op jit(solution)/shard_map/conv_forward/pallas_call | solution.py:521
  112.5 4.8 %project.1 = (bf16[512,512]{1,0:T(8,128)(2,1)}, bf16[8,512,128]{2,1,0:T(8,128)(2,1)}, bf16[8,512,128]{2,1,0:T(8,128)(2,1)}) custom-call(f32[512,512]{1,0:T(8,128)} %get-tuple-element.72.res.refs_3_, f32[8,8,512]{2,1,0:T(8,128)} %get-tuple-element.73.every.refs_14_, f32[8,512]{1,0:T(8,128)} %get-tuple-element.112.rows, bf16[4,2048,128]{2,1,0:T(8,128)(2,1)} %bitcast.29, ...), custom_call_target="tpu_custom_call" | custom-call | tf_op jit(solution)/shard_map/project/pallas_call | solution.py:553
  117.3 121.4 %attention.1 = (bf16[8,512,128]{2,1,0:T(8,128)(2,1)}, bf16[8,512,128]{2,1,0:T(8,128)(2,1)}, bf16[8,128,128]{2,1,0:T(8,128)(2,1)}) custom-call(bf16[8,512,128]{2,1,0:T(8,128)(2,1)} %get-tuple-element.75.kv, bf16[8,512,128]{2,1,0:T(8,128)(2,1)} %get-tuple-element.76.qg, bf16[8,128,128]{2,1,0:T(8,128)(2,1)} %get-tuple-element.77.text, s32[1,128]{1,0:T(1,128)} %keep.1), custom_call_target="tpu_custom_call" | custom-call | tf_op jit(solution)/shard_map/attention/pallas_call | solution.py:707
  238.7 88.3 %backward.1 = (bf16[512,512]{1,0:T(8,128)(2,1)}, f32[512,512]{1,0:T(8,128)}, f32[9,64,128]{2,1,0:T(8,128)}, f32[9,64,128]{2,1,0:T(8,128)}, f32[1,256,128]{2,1,0:...) custom-call(bf16[8,512,128]{2,1,0:T(8,128)(2,1)} %get-tuple-element., ...), custom_call_target="tpu_custom_call" | custom-call | tf_op jit(solution)/shard_map/backward/pallas_call | solution.py:1346
  327.0 4.4 %emit.1 = (bf16[512,512]{1,0:T(8,128)(2,1)}, f32[512,512]{1,0:T(8,128)}, f32[1,2048]{1,0:T(1,128)}, f32[16,2048]{1,0:T(8,128)}, f32[9,64,128]{2,1,0:T(8,128)}, /...) custom-call(bf16[512,512]{1,0:T(8,128)(2,1)} %get-tuple-element.90.r, ...), custom_call_target="tpu_custom_call" | custom-call | tf_op jit(solution)/shard_map/emit/pallas_call | solution.py:1413

commit v5 on v4

--- a/solution.py
+++ b/solution.py
@@ -351,40 +351,6 @@
 
 ANY = pl.BlockSpec(memory_space=pl.ANY)
 VM = pl.BlockSpec(memory_space=pltpu.VMEM)
-
-
-def exchange_scratch(n_sp, width, halo_types, chans):
-    out = [pltpu.VMEM((8, chans), F32), pltpu.VMEM((n_sp, 8, chans), F32)]
-    for ty in halo_types:
-        out += [pltpu.VMEM((width, chans), ty), pltpu.VMEM((width, chans), ty)]
-    count = n_sp - 1 + 2 * len(halo_types)
-    return out + [pltpu.SemaphoreType.DMA((count,)), pltpu.SemaphoreType.DMA((count,))]
-
-
-def exchange_greet(n_sp):
-    at = Place()
-    greet([at.rp(k, n_sp) for k in range(1, n_sp)])
-
-
-def exchange(n_sp, width, scratch, edges):
-    at = Place()
-    mine, every = scratch[0], scratch[1]
-    ssem, rsem = scratch[-2:]
-    greeted(n_sp - 1)
-    sent = []
-    for e, ref in enumerate(edges):
-        above, below = scratch[2 + 2 * e], scratch[3 + 2 * e]
-        px = ref.shape[0]
-        j = n_sp - 1 + 2 * e
-        sent.append(remote(ref.at[px - width :], above, ssem.at[j], rsem.at[j], at.rp(1, n_sp)))
-        sent.append(remote(ref.at[:width], below, ssem.at[j + 1], rsem.at[j + 1], at.rp(n_sp - 1, n_sp)))
-    for k in range(1, n_sp):
-        sent.append(remote(mine, every.at[at.s], ssem.at[k - 1], rsem.at[k - 1], at.rp(k, n_sp)))
-    every[at.s] = mine[...]
-    for cp in sent:
-        cp.wait()
-
-
 def channel_stats(mine, v):
     mean = jnp.sum(v, axis=0, keepdims=True) / v.shape[0]
     dev = v - mean
@@ -456,108 +422,6 @@
         jnp.concatenate([whole[j * chunk : j * chunk + cols] for j in range(n_sp)]),
         jnp.concatenate([whole[j * chunk + cols : (j + 1) * chunk] for j in range(n_sp)]),
     )
-
-
-def conv_kernel(n_sp, width, refs_in, x, up, dn, every, rows, w, *rest):
-    base = None
-    if refs_in:
-        base, rest = rest[0], rest[1:]
-    out, act, stats, above, below, a3 = rest[:6]
-    scratch = rest[6:]
-    step = pl.program_id(0)
-    px, c = out.shape
-    height = px // width
-
-    @pl.when(step == 0)
-    def _():
-        exchange_greet(n_sp)
-        center, inverse = combine_stats(every, px)
-        mul = inverse * rows[0:1, :] * rows[2:3, :]
-        add = rows[1:2, :] * rows[2:3, :] + rows[3:4, :]
-        has_up, has_dn = edge_flags(n_sp, lax.axis_index("sp"))
-        for r in range(height + 2):
-            if r == 0:
-                v = up[...]
-            elif r == height + 1:
-                v = dn[...]
-            else:
-                v = x[(r - 1) * width : r * width, :]
-            v = silu((v.astype(F32) - center) * mul + add)
-            if r == 0:
-                v = v * has_up
-            elif r == height + 1:
-                v = v * has_dn
-            act[r * width : (r + 1) * width, :] = v.astype(BF16)
-            shifted(a3, r, width, v)
-        if base is None:
-            out[...] = jnp.zeros_like(out)
-        else:
-            out[...] = base[...].astype(F32)
-
-    i, j = lax.div(step, 3), lax.rem(step, 3)
-    lhs = a3[j, pl.ds(pl.multiple_of(i * width, width), px), :]
-    out[...] += dot(lhs, joined(w, 0), 1, 1)
-
-    @pl.when(step == 8)
-    def _():
-        channel_stats(scratch[0], out[...])
-        exchange(n_sp, width, scratch, [out])
-        stats[...] = scratch[1][...]
-        above[...] = scratch[2][...]
-        below[...] = scratch[3][...]
-
-
-def whole_spec(shape):
-    return pl.BlockSpec(shape, lambda t: (0,) * len(shape))
-
-
-def conv_call(x, up, dn, every, rows, w, base, n_sp, width, cid):
-    px, c = x.shape
-    padded = px + 2 * width
-    ins = [x, up, dn, every, rows, w] + ([] if base is None else [base])
-    in_specs = [whole_spec(v.shape) for v in ins]
-    in_specs[5] = pl.BlockSpec((4, 1, c, 128), lambda t: (0, t, 0, 0))
-    outs = [((px, c), F32), ((padded, c), BF16), ((n_sp, 8, c), F32), ((width, c), F32), ((width, c), F32)]
-    return pl.pallas_call(
-        functools.partial(conv_kernel, n_sp, width, base is not None),
-        grid=(9,),
-        in_specs=in_specs,
-        out_specs=[whole_spec(s) for s, _ in outs],
-        out_shape=[jax.ShapeDtypeStruct(s, ty) for s, ty in outs],
-        scratch_shapes=[pltpu.VMEM((3, padded, c), BF16)] + exchange_scratch(n_sp, width, [F32], c),
-        compiler_params=params(cid, 1),
-        name="conv_forward",
-    )(*ins)
-
-
-def project_kernel(n_sp, res, every, rows, w_small, cot, normed, kv, qg):
-    px, c = res.shape
-    d = c // HEADS
-    center, inverse = combine_stats(every, px)
-    n = ((res[...] - center) * (inverse * rows[0:1, :]) + rows[1:2, :]).astype(BF16)
-    normed[...] = n
-    wq, wp = split_small(joined(w_small), n_sp)
-    q = (dot(n, wq[:c], 1, 1).astype(BF16).astype(F32) * (d ** -0.5)).astype(BF16)
-    k = dot(n, wq[c : 2 * c], 1, 1).astype(BF16)
-    v = dot(n, wq[2 * c :], 1, 1).astype(BF16)
-    g = dot(cot[...], wp, 1, 0).astype(BF16)
-    for h in range(HEADS):
-        cut = slice(h * d, (h + 1) * d)
-        kv[h] = jnp.concatenate([k[:, cut], v[:, cut]], axis=1)
-        qg[h] = jnp.concatenate([q[:, cut], g[:, cut]], axis=1)
-
-
-def project_call(res, every, rows, w_small, cot, n_sp):
-    px, c = res.shape
-    big = jax.ShapeDtypeStruct((HEADS, px, 128), BF16)
-    return pl.pallas_call(
-        functools.partial(project_kernel, n_sp),
-        out_shape=[jax.ShapeDtypeStruct((px, c), BF16), big, big],
-        in_specs=[VM] * 5,
-        out_specs=[VM] * 3,
-        compiler_params=params(),
-        name="project",
-    )(res, every, rows, w_small, cot)
 
 
 def attention_kernel(
@@ -733,217 +597,316 @@
         return cp
 
 
+class Gather:
+    def __init__(self, at, nz, ins, outs, dims, ssem, rsem):
+        self.at, self.nz, self.ins, self.outs, self.dims = at, nz, ins, outs, dims
+        self.ssem, self.rsem = ssem, rsem
+        self.sent, self.kinds = {}, {}
+
+    @staticmethod
+    def copies(nz):
+        return 3 * nz - 1 + 7 * nz
+
+    def view(self, a, ii, k, core, half=None):
+        at, nz, r = self.at, self.nz, self.dims[a][1]
+        sp = 2 * lax.rem(at.z - k + nz, nz) + core
+        if half is None:
+            return self.outs[a].at[ii, :, pl.ds(pl.multiple_of(sp * r, r), r), :]
+        h = r // 2
+        return self.outs[a].at[ii, :, pl.ds(pl.multiple_of(sp * r + half * h, h), h), :]
+
+    def send(self, a, kind, src, dst, dev):
+        j = self.kinds.setdefault(kind, len(self.kinds))
+        self.sent[a, kind] = remote(src, dst, self.ssem.at[a, j], self.rsem.at[a, j], dev)
+
+    def forward(self, a, kind, ref, dev):
+        self.send(a, kind, ref, ref, dev)
+
+    def first(self, a):
+        at = self.at
+        own = self.view(a, at.i, 0, at.c)
+        for k in range(1, self.nz):
+            self.send(a, ("z", k), self.ins[a], own, at.zp(k, self.nz))
+        self.send(a, ("x", 0), self.ins[a], own, at.xn)
+        self.send(a, ("y", 0), self.ins[a], own, at.yn)
+        self.send(a, ("s", 0), self.ins[a], own, at.sib)
+
+    def second(self, a):
+        at = self.at
+        for k in range(1, self.nz):
+            self.sent[a, ("z", k)].wait_recv()
+            got = self.view(a, at.i, k, at.c)
+            self.forward(a, ("x", k), got, at.xn)
+            self.forward(a, ("y", k), got, at.yn)
+            self.forward(a, ("s", k), got, at.sib)
+
+    def third(self, a):
+        at = self.at
+        for k in range(self.nz):
+            self.sent[a, ("x", k)].wait_recv()
+            self.forward(a, ("da", k), self.view(a, at.ix, k, at.c, 0), at.yn)
+            self.forward(a, ("sx", k), self.view(a, at.ix, k, at.c), at.sib)
+            self.sent[a, ("y", k)].wait_recv()
+            self.forward(a, ("db", k), self.view(a, at.iy, k, at.c, 1), at.xn)
+            self.forward(a, ("sy", k), self.view(a, at.iy, k, at.c), at.sib)
+
+    def fourth(self, a):
+        at = self.at
+        for k in range(self.nz):
+            self.sent[a, ("da", k)].wait_recv()
+            self.forward(a, ("sa", k), self.view(a, at.id, k, at.c, 0), at.sib)
+            self.sent[a, ("db", k)].wait_recv()
+            self.forward(a, ("sb", k), self.view(a, at.id, k, at.c, 1), at.sib)
+
+    def complete(self, a):
+        for (b, kind), cp in self.sent.items():
+            if b == a and kind[0][0] == "s":
+                cp.wait_recv()
+
+    def finish(self):
+        for cp in self.sent.values():
+            cp.wait_send()
+
+
 def img_peers(at):
     return [(lax.rem(at.i + k, 4), at.s) for k in range(1, 4)]
 
 
-HEAD_MAIL = 3 * 3 + 3 + 2 * 7 + 7 + 4
-
-
-def head_kernel(nz, width, dims, *refs):
+FORWARD_MAIL = 3 * 3 + 3 + 2 * 7 + 4 + 7 + 2 * (2 + 7)
+
+
+def forward_kernel(nz, width, dims, *refs):
     na = len(dims)
-    ins, refs = refs[: na - 1], refs[na - 1 :]
+    chunks, refs = refs[: na - 1], refs[na - 1 :]
     x, cot, temb, cap, w_emb, w_cap, gains, biases, w_qkv, w_proj = refs[:10]
     outs, refs = refs[10 : 10 + na], refs[10 + na :]
-    st0, xa, xb, ca, cb, rows, kv_all, cap_all, emb_all = refs[:9]
-    (ssem, rsem, lsem, mine, every, h0, h1, h2, h3, aff_s, emb_s, cap_s, part, part_r, kv_s, kv_r, mod_s, mod_r,
-     msend, mrecv, emb, affine, small) = refs[9:]
-    ins = list(ins) + [small]
+    hidden_o, act0_o, res_o, act1_o, normed, kv, qg = refs[:7]
+    st0, st1, st2, rows, ca, cb, ra, rb, ha, hb, kv_all, cap_all, emb_all = refs[7:20]
+    refs = refs[20:]
+    weights, refs = refs[:na], refs[na:]
+    (ssem, rsem, lsem, msend, mrecv, small, emb, affine, mine, every, xa, xb, ca_s, cb_s, ha_s, hb_s, ra_s, rb_s,
+     aff_s, emb_s, cap_s, part, part_r, kv_s, kv_r, mod_s, mod_r, a3, act0, act1, hidden, res) = refs
     n_sp = 2 * nz
     at = Place()
     line = [at.rp(k, n_sp) for k in range(1, n_sp)]
     grid = img_peers(at)
     greet(line + grid)
     mail = Mail(msend, mrecv)
+    got = Gather(at, nz, list(chunks) + [small], weights, dims, ssem, rsem)
+    px, c = x.shape
+    height = px // width
+    d = c // HEADS
+    tokens = cap.shape[0]
+    e = cap.shape[1] // 4
+    cut = w_qkv.shape[0]
     local = []
-    sent = {}
-    kinds = {}
-
-    def view(a, ii, k, core, half=None):
-        r = dims[a][1]
-        sp = 2 * lax.rem(at.z - k + nz, nz) + core
-        if half is None:
-            return outs[a].at[ii, :, pl.ds(pl.multiple_of(sp * r, r), r), :]
-        h = r // 2
-        return outs[a].at[ii, :, pl.ds(pl.multiple_of(sp * r + half * h, h), h), :]
-
-    def send(a, kind, src, dst, dev):
-        j = kinds.setdefault(kind, len(kinds))
-        sent[a, kind] = remote(src, dst, ssem.at[a, j], rsem.at[a, j], dev)
-
-    def forward(a, kind, ref, dev):
-        send(a, kind, ref, ref, dev)
-
-    def first(a):
-        own = view(a, at.i, 0, at.c)
-        for k in range(1, nz):
-            send(a, ("z", k), ins[a], own, at.zp(k, nz))
-        send(a, ("x", 0), ins[a], own, at.xn)
-        send(a, ("y", 0), ins[a], own, at.yn)
-        send(a, ("s", 0), ins[a], own, at.sib)
-
-    def second(a):
-        for k in range(1, nz):
-            sent[a, ("z", k)].wait_recv()
-            got = view(a, at.i, k, at.c)
-            forward(a, ("x", k), got, at.xn)
-            forward(a, ("y", k), got, at.yn)
-            forward(a, ("s", k), got, at.sib)
-
-    def third(a):
-        for k in range(nz):
-            sent[a, ("x", k)].wait_recv()
-            forward(a, ("da", k), view(a, at.ix, k, at.c, 0), at.yn)
-            forward(a, ("sx", k), view(a, at.ix, k, at.c), at.sib)
-            sent[a, ("y", k)].wait_recv()
-            forward(a, ("db", k), view(a, at.iy, k, at.c, 1), at.xn)
-            forward(a, ("sy", k), view(a, at.iy, k, at.c), at.sib)
-
-    def fourth(a):
-        for k in range(nz):
-            sent[a, ("da", k)].wait_recv()
-            forward(a, ("sa", k), view(a, at.id, k, at.c, 0), at.sib)
-            sent[a, ("db", k)].wait_recv()
-            forward(a, ("sb", k), view(a, at.id, k, at.c, 1), at.sib)
-
-    cut = w_qkv.shape[0]
+
+    def copy(src, dst):
+        cp = pltpu.make_async_copy(src, dst, lsem.at[len(local)])
+        cp.start()
+        local.append(cp)
+        return cp
+
     small[0, :cut] = w_qkv[...]
     small[0, cut:] = w_proj[...]
-    e = cap.shape[1] // 4
     embedded = silu(temb[...].astype(F32)).astype(BF16).astype(F32)
     for j in range(4):
         emb[j] = jnp.broadcast_to(embedded[:, j * e : (j + 1) * e], (8, e))
     affine[0:3] = gains[...].astype(F32)
     affine[3:6] = biases[...].astype(F32)
-    channel_stats(mine, x[...].astype(F32))
+    mine[...] = jnp.zeros_like(mine)
+
+    def publish(j, v, edges):
+        channel_stats(mine.at[j], v)
+        out = []
+        for ref, above, below in edges:
+            out.append(mail.send(ref.at[px - width :], above, line[0]))
+            out.append(mail.send(ref.at[:width], below, line[-1]))
+        for dev in line:
+            out.append(mail.send(mine.at[j], every.at[j, at.s], dev))
+        every[j, at.s] = mine[j]
+        return out
+
     greeted(n_sp + 2)
-    first(0)
+    got.first(0)
+    stat0 = publish(0, x[...].astype(F32), [(x, xa, xb), (cot, ca_s, cb_s)])
     round1 = []
     for dev in grid:
         round1.append(mail.send(affine, aff_s.at[at.i], dev))
         round1.append(mail.send(emb.at[dev[0]], emb_s.at[at.i], dev))
         round1.append(mail.send(cap.at[:, pl.ds(pl.multiple_of(dev[0] * e, e), e)], cap_s.at[at.i], dev))
-    own_cap = pltpu.make_async_copy(cap.at[:, pl.ds(pl.multiple_of(at.i * e, e), e)], cap_s.at[at.i], lsem.at[na])
-    own_cap.start()
+    own_cap = copy(cap.at[:, pl.ds(pl.multiple_of(at.i * e, e), e)], cap_s.at[at.i])
     aff_s[at.i] = affine[...]
     emb_s[at.i] = emb[at.i]
-    px = x.shape[0]
-    stat = []
-    for ref, above, below in ((x, h0, h1), (cot, h2, h3)):
-        stat.append(mail.send(ref.at[px - width :], above, line[0]))
-        stat.append(mail.send(ref.at[:width], below, line[-1]))
+    got.first(1)
+    own = [copy(got.ins[a], got.view(a, at.i, 0, at.c)) for a in range(na)]
+    got.second(0)
+    got.first(2)
+    got.third(0)
+    got.second(1)
+
+    own_cap.wait()
+    for cp in round1:
+        cp.wait_recv()
+    for j in range(4):
+        part[j, :tokens] = dot(cap_s[j], w_cap[...], 1, 0)
+        part[j, tokens:] = dot(emb_s[j].astype(BF16), w_emb[...], 1, 0)
+    round2 = [mail.send(part.at[dev[0]], part_r.at[at.i], dev) for dev in grid]
+    part_r[at.i] = part[at.i]
+    cap_all[...] = cap_s[...]
+    emb_all[...] = jnp.concatenate([emb_s[j][0:1] for j in range(4)] + [jnp.zeros((4, e), F32)])
+    aff = jnp.concatenate([aff_s[j] for j in range(4)], axis=1)
+    rows[...] = jnp.zeros_like(rows)
+    for j in range(3):
+        rows[j, 0:1] = aff[j : j + 1]
+        rows[j, 1:2] = aff[3 + j : 4 + j]
+        rows[j, 2:3] = jnp.ones((1, c), F32)
+
+    has_up, has_dn = edge_flags(n_sp, at.s)
+
+    def activate(j, v, above, below, act):
+        center, inverse = combine_stats(every.at[j], px)
+        mul = inverse * rows[j, 0:1] * rows[j, 2:3]
+        add = rows[j, 1:2] * rows[j, 2:3] + rows[j, 3:4]
+        for r in range(height + 2):
+            top, end = r == 0, r == height + 1
+            t = above[...] if top else below[...] if end else v[(r - 1) * width : r * width, :]
+            t = silu((t.astype(F32) - center) * mul + add)
+            if top:
+                t = t * has_up
+            elif end:
+                t = t * has_dn
+            act[r * width : (r + 1) * width, :] = t.astype(BF16)
+            shifted(a3, r, width, t)
+
+    def taps(w, out, t0, t1, base):
+        def one(tap, _):
+            i, j = lax.div(tap, 3), lax.rem(tap, 3)
+            lhs = a3[j, pl.ds(pl.multiple_of(i * width, width), px), :]
+            first = 0.0 if base is None else base[...].astype(F32)
+            out[...] = dot(lhs, joined(w, tap), 1, 1) + jnp.where(tap > 0, out[...], first)
+            return 0
+
+        lax.fori_loop(t0, t1, one, 0)
+
+    for cp in stat0:
+        cp.wait_recv()
+    activate(0, x, xa, xb, act0)
+    copy(act0, act0_o)
+    got.fourth(0)
+    for cp in own:
+        cp.wait()
+    got.complete(0)
+    copy(weights[0], outs[0])
+    taps(weights[0], hidden, 0, 3, None)
+    got.second(2)
+    taps(weights[0], hidden, 3, 6, None)
+    got.third(1)
+    taps(weights[0], hidden, 6, 9, None)
+    stat1 = publish(1, hidden[...], [(hidden, ha_s, hb_s)])
+    copy(hidden, hidden_o)
+    for cp in round2:
+        cp.wait_recv()
+    total = part_r[0] + part_r[1] + part_r[2] + part_r[3]
+    kv_s[...] = total[:tokens].astype(BF16)
+    mod_s[...] = total[tokens:]
+    round3 = []
     for dev in line:
-        stat.append(mail.send(mine, every.at[at.s], dev))
-    every[at.s] = mine[...]
-    for a in range(na):
-        cp = pltpu.make_async_copy(ins[a], view(a, at.i, 0, at.c), lsem.at[a])
-        cp.start()
-        local.append(cp)
-    tokens = cap.shape[0]
-    round2, round3 = [], []
-
-    def extras(tick):
-        if tick == 1:
-            own_cap.wait()
-            for cp in round1:
-                cp.wait_recv()
-            for j in range(4):
-                part[j, :tokens] = dot(cap_s[j], w_cap[...], 1, 0)
-                part[j, tokens:] = dot(emb_s[j].astype(BF16), w_emb[...], 1, 0)
-            for dev in grid:
-                round2.append(mail.send(part.at[dev[0]], part_r.at[at.i], dev))
-            part_r[at.i] = part[at.i]
-        if tick == 2:
-            for cp in round2:
-                cp.wait_recv()
-            total = part_r[0] + part_r[1] + part_r[2] + part_r[3]
-            kv_s[...] = total[:tokens].astype(BF16)
-            mod_s[...] = total[tokens:]
-            for dev in line:
-                round3.append(mail.send(kv_s, kv_r.at[at.s], dev))
-                round3.append(mail.send(mod_s, mod_r.at[at.s], dev))
-            kv_r[at.s] = kv_s[...]
-            mod_r[at.s] = mod_s[...]
-        if tick == 4:
-            for cp in round3 + stat:
-                cp.wait_recv()
-            kv_all[...] = kv_r[...]
-            cap_all[...] = cap_s[...]
-            emb_all[...] = jnp.concatenate([emb_s[j][0:1] for j in range(4)] + [jnp.zeros((4, e), F32)])
-            st0[...] = every[...]
-            for dst, src in ((xa, h0), (xb, h1), (ca, h2), (cb, h3)):
-                dst[...] = src[...]
-            aff = jnp.concatenate([aff_s[j] for j in range(4)], axis=1)
-            mod = jnp.concatenate([mod_r[j][0:1] for j in range(n_sp)], axis=1)
-            c = aff.shape[1]
-            rows[...] = jnp.zeros_like(rows)
-            for j in range(3):
-                rows[j, 0:1] = aff[j : j + 1]
-                rows[j, 1:2] = aff[3 + j : 4 + j]
-                rows[j, 2:3] = 1.0 + mod[:, :c] if j == 1 else jnp.ones((1, c), F32)
-            rows[1, 3:4] = mod[:, c:]
-
-    stages = (first, second, third, fourth)
-    for tick in range(1, na + 3):
-        for a in range(na):
-            stage = tick - a
-            if 0 <= stage < 4 and (stage, a) != (0, 0):
-                stages[stage](a)
-        extras(tick)
-    for cp in local:
+        round3.append(mail.send(kv_s, kv_r.at[at.s], dev))
+        round3.append(mail.send(mod_s, mod_r.at[at.s], dev))
+    kv_r[at.s] = kv_s[...]
+    mod_r[at.s] = mod_s[...]
+    got.fourth(1)
+    got.third(2)
+    for cp in round3 + stat1:
+        cp.wait_recv()
+    kv_all[...] = kv_r[...]
+    mod = jnp.concatenate([mod_r[j][0:1] for j in range(n_sp)], axis=1)
+    rows[1, 2:3] = 1.0 + mod[:, :c]
+    rows[1, 3:4] = mod[:, c:]
+
+    activate(1, hidden, ha_s, hb_s, act1)
+    copy(act1, act1_o)
+    got.fourth(2)
+    got.complete(1)
+    copy(weights[1], outs[1])
+    taps(weights[1], res, 0, 9, x)
+    stat2 = publish(2, res[...], [(res, ra_s, rb_s)])
+    copy(res, res_o)
+    for dst, src in ((ca, ca_s), (cb, cb_s), (ha, ha_s), (hb, hb_s)):
+        dst[...] = src[...]
+    got.complete(2)
+    copy(weights[2], outs[2])
+    wq, wp = split_small(joined(weights[2], 0), n_sp)
+    g = dot(cot[...], wp, 1, 0).astype(BF16)
+
+    for cp in stat2:
+        cp.wait_recv()
+    center, inverse = combine_stats(every.at[2], px)
+    n = ((res[...] - center) * (inverse * rows[2, 0:1]) + rows[2, 1:2]).astype(BF16)
+    normed[...] = n
+    k = dot(n, wq[c : 2 * c], 1, 1).astype(BF16)
+    v = dot(n, wq[2 * c :], 1, 1).astype(BF16)
+    q = (dot(n, wq[:c], 1, 1).astype(BF16).astype(F32) * (d ** -0.5)).astype(BF16)
+    for h in range(HEADS):
+        lanes = slice(h * d, (h + 1) * d)
+        kv[h] = jnp.concatenate([k[:, lanes], v[:, lanes]], axis=1)
+        qg[h] = jnp.concatenate([q[:, lanes], g[:, lanes]], axis=1)
+    ra[...] = ra_s[...]
+    rb[...] = rb_s[...]
+    st0[...] = every[0]
+    st1[...] = every[1]
+    st2[...] = every[2]
+    for cp in local[1 + na :]:
         cp.wait()
-    for (a, kind), cp in sent.items():
-        if kind[0] in ("s", "sx", "sy", "sa", "sb"):
-            cp.wait_recv()
-        cp.wait_send()
+    got.finish()
     for cp in mail.sent:
         cp.wait_send()
 
 
-def head_call(chunks, x, cot, temb, cap, w_emb, w_cap, gains, biases, w_qkv, w_proj, nz, width, cid):
+def forward_call(chunks, x, cot, temb, cap, w_emb, w_cap, gains, biases, w_qkv, w_proj, nz, width, cid):
     dims = [c.shape[:2] for c in chunks] + [(1, w_qkv.shape[0] + w_proj.shape[0])]
     na = len(dims)
     n_sp = 2 * nz
-    copies = 3 * nz - 1 + 7 * nz
     px, c = x.shape
+    padded = px + 2 * width
     tokens, wide = cap.shape
     e = wide // 4
-    edge = ((width, c), BF16)
-    outs = [
-        ((n_sp, 8, c), F32), edge, edge, edge, edge, ((3, 8, c), F32), ((n_sp, tokens, 128), BF16),
-        ((4, tokens, e), BF16), ((8, e), F32),
+    d2 = 2 * c // HEADS
+    big = [((4, t, n_sp * r, 128), BF16) for t, r in dims]
+    edge16, edge32 = ((width, c), BF16), ((width, c), F32)
+    stat = ((n_sp, 8, c), F32)
+    outs = big + [
+        ((px, c), F32), ((padded, c), BF16), ((px, c), F32), ((padded, c), BF16), ((px, c), BF16),
+        ((HEADS, px, d2), BF16), ((HEADS, px, d2), BF16),
+        stat, stat, stat, ((3, 8, c), F32), edge16, edge16, edge32, edge32, edge32, edge32,
+        ((n_sp, tokens, 128), BF16), ((4, tokens, e), BF16), ((8, e), F32),
     ]
+    vm = pltpu.VMEM
     return pl.pallas_call(
-        functools.partial(head_kernel, nz, width, dims),
-        out_shape=[jax.ShapeDtypeStruct((4, t, n_sp * r, 128), BF16) for t, r in dims]
-        + [jax.ShapeDtypeStruct(s, ty) for s, ty in outs],
+        functools.partial(forward_kernel, nz, width, dims),
+        out_shape=[jax.ShapeDtypeStruct(s, ty) for s, ty in outs],
         in_specs=[ANY] * (na - 1) + [VM, VM, VM, ANY] + [VM] * 6,
-        out_specs=[ANY] * na + [VM] * len(outs),
-        scratch_shapes=[
-            pltpu.SemaphoreType.DMA((na, copies)),
-            pltpu.SemaphoreType.DMA((na, copies)),
-            pltpu.SemaphoreType.DMA((na + 1,)),
-            pltpu.VMEM((8, c), F32),
-            pltpu.VMEM((n_sp, 8, c), F32),
-            pltpu.VMEM((width, c), BF16), pltpu.VMEM((width, c), BF16),
-            pltpu.VMEM((width, c), BF16), pltpu.VMEM((width, c), BF16),
-            pltpu.VMEM((4, 8, 128), F32),
-            pltpu.VMEM((4, 8, e), F32),
-            pltpu.VMEM((4, tokens, e), BF16),
-            pltpu.VMEM((4, tokens + 8, 128), F32),
-            pltpu.VMEM((4, tokens + 8, 128), F32),
-            pltpu.VMEM((tokens, 128), BF16),
-            pltpu.VMEM((n_sp, tokens, 128), BF16),
-            pltpu.VMEM((8, 128), F32),
-            pltpu.VMEM((n_sp, 8, 128), F32),
-            pltpu.SemaphoreType.DMA((HEAD_MAIL,)),
-            pltpu.SemaphoreType.DMA((HEAD_MAIL,)),
-            pltpu.VMEM((4, 8, e), F32),
-            pltpu.VMEM((8, 128), F32),
-            pltpu.VMEM((1,) + dims[-1][1:] + (128,), BF16),
+        out_specs=[ANY] * (na + 4) + [VM] * (len(outs) - na - 4),
+        scratch_shapes=[vm(s, ty) for s, ty in big]
+        + [
+            pltpu.SemaphoreType.DMA((na, Gather.copies(nz))),
+            pltpu.SemaphoreType.DMA((na, Gather.copies(nz))),
+            pltpu.SemaphoreType.DMA((2 * na + 5,)),
+            pltpu.SemaphoreType.DMA((FORWARD_MAIL,)),
+            pltpu.SemaphoreType.DMA((FORWARD_MAIL,)),
+            vm((1, dims[-1][1], 128), BF16), vm((4, 8, e), F32), vm((8, 128), F32),
+            vm((3, 8, c), F32), vm((3, n_sp, 8, c), F32),
+        ]
+        + [vm(*edge16)] * 4 + [vm(*edge32)] * 4
+        + [
+            vm((4, 8, 128), F32), vm((4, 8, e), F32), vm((4, tokens, e), BF16),
+            vm((4, tokens + 8, 128), F32), vm((4, tokens + 8, 128), F32),
+            vm((tokens, 128), BF16), vm((n_sp, tokens, 128), BF16), vm((8, 128), F32), vm((n_sp, 8, 128), F32),
+            vm((3, padded, c), BF16), vm((padded, c), BF16), vm((padded, c), BF16), vm((px, c), F32), vm((px, c), F32),
         ],
         compiler_params=params(cid),
-        name="gather_weights",
+        name="forward",
     )(*chunks, x, cot, temb, cap, w_emb, w_cap, gains, biases, w_qkv, w_proj)
 
 
@@ -1427,30 +1390,25 @@
     caption_proj, out_proj, norm_gains, norm_biases, cotangent,
 ):
     n, height, width, c = image_in.shape
-    n_img, n_sp = lax.axis_size("img"), lax.axis_size("sp")
-    sp = lax.axis_index("sp")
+    n_sp = lax.axis_size("sp")
     nz = n_sp // 2
     px = height * width
-    d = c // HEADS
     x = image_in.reshape(px, c)
     cot = cotangent.reshape(px, c)
 
     flat = lambda w: w.transpose(1, 2, 3, 0).reshape(9, w.shape[3], w.shape[0])
-    (w_in, w_out, w_small, st0, xa, xb, ca, cb, rows, kv_all, cap_all, emb_all) = head_call(
+    (w_in, w_out, w_small, hidden, act0, res, act1, normed, kv, qg,
+     st0, st1, st2, rows, ca, cb, ra, rb, ha, hb, kv_all, cap_all, emb_all) = forward_call(
         [flat(conv_in), flat(conv_out)], x, cot, time_embed, caption[0], embed_proj, caption_proj,
         norm_gains, norm_biases, qkv_proj.T, out_proj.T, nz, width, 0,
     )
     w_small = w_small.reshape(4, -1, 128)
-
-    hidden, act0, st1, ha, hb = conv_call(x, xa, xb, st0, rows[0], w_in, None, n_sp, width, 1)
-    res, act1, st2, ra, rb = conv_call(hidden, ha, hb, st1, rows[1], w_out, x, n_sp, width, 2)
-    normed, kv, qg = project_call(res, st2, rows[2], w_small, cot, n_sp)
-    od, dkv, dt_all = attention_call(kv, qg, kv_all, caption_mask, 3)
+    od, dkv, dt_all = attention_call(kv, qg, kv_all, caption_mask, 1)
 
     parts = backward_call(
         [od, dkv, w_small, res, cot, normed, act1, hidden, act0, x], w_in, w_out,
         [st0, st1, st2, rows, ca, cb, ra, rb, ha, hb, dt_all, cap_all, emb_all, embed_proj, caption_proj, time_embed],
-        nz, width, 5,
+        nz, width, 2,
     )
     output, image, g_temb, g_cap, s_in, s_out, g_wemb, g_qkv, g_wcap, g_out, g_gains, g_biases = emit_call(
         parts, qkv_proj.shape[1]

time: 332 us -> 302 us (0.910)
  Pallas kernels: 329 us -> 301 us
    pallas_call x4 -> x1, Pallas kernels: 115 us -> 87.8 us  [forward_call(): pl.pallas_call(functools.partial(forward_kernel, nz, width, dims), out_sh...]
where the time goes in v5:
time: 302 us; the launch traced here: 301 us
  Pallas kernels  301 us (100%)
    pallas_call x1, Pallas kernels, attention_call(): pl.pallas_call(functools.partial(attention_kernel, n_sp, BQ, BK), out_sha...  120 us
    pallas_call x1, Pallas kernels, backward_call(): pl.pallas_call(functools.partial(backward_kernel, nz, width), out_shape=[...  88.7 us
    pallas_call x1, Pallas kernels, forward_call(): pl.pallas_call(functools.partial(forward_kernel, nz, width, dims), out_sh...  87.8 us

profile of v5, /device:TPU:0, one launch (start us, length us, event | category | flops | bytes accessed | tf_op | source)
XLA Modules:
  0.0 301.5 jit_solution(9659873799446438635)
XLA Ops:
  0.6 87.8 %forward.1 = (bf16[4,9,512,128]{3,2,1,0:T(8,128)(2,1)}, bf16[4,9,512,128]{3,2,1,0:T(8,128)(2,1)}, bf16[4,1,2048,128]{3,2,1,0:T(8,128)(2,1)}, f32[512,512]{1,0:T(...) custom-call(bf16[9,64,128]{2,1,0:T(8,128)(2,1)} %bitcast.29, ...), custom_call_target="tpu_custom_call" | custom-call | tf_op jit(solution)/shard_map/forward/pallas_call | solution.py:886
  88.4 119.7 %attention.1 = (bf16[8,512,128]{2,1,0:T(8,128)(2,1)}, bf16[8,512,128]{2,1,0:T(8,128)(2,1)}, bf16[8,128,128]{2,1,0:T(8,128)(2,1)}) custom-call(bf16[8,512,128]{2,1,0:T(8,128)(2,1)} %get-tuple-element.60.kv, bf16[8,512,128]{2,1,0:T(8,128)(2,1)} %get-tuple-element.61.qg, bf16[8,128,128]{2,1,0:T(8,128)(2,1)} %get-tuple-element.62.text, s32[1,128]{1,0:T(1,128)} %keep.1), custom_call_target="tpu_custom_call" | custom-call | tf_op jit(solution)/shard_map/attention/pallas_call | solution.py:571
  208.2 88.7 %backward.1 = (bf16[512,512]{1,0:T(8,128)(2,1)}, f32[512,512]{1,0:T(8,128)}, f32[9,64,128]{2,1,0:T(8,128)}, f32[9,64,128]{2,1,0:T(8,128)}, f32[1,256,128]{2,1,0:...) custom-call(bf16[8,512,128]{2,1,0:T(8,128)(2,1)} %get-tuple-element., ...), custom_call_target="tpu_custom_call" | custom-call | tf_op jit(solution)/shard_map/backward/pallas_call | solution.py:1309
  296.9 4.4 %emit.1 = (bf16[512,512]{1,0:T(8,128)(2,1)}, f32[512,512]{1,0:T(8,128)}, f32[1,2048]{1,0:T(1,128)}, f32[16,2048]{1,0:T(8,128)}, f32[9,64,128]{2,1,0:T(8,128)}, /...) custom-call(bf16[512,512]{1,0:T(8,128)(2,1)} %get-tuple-element.86.r, ...), custom_call_target="tpu_custom_call" | custom-call | tf_op jit(solution)/shard_map/emit/pallas_call | solution.py:1376

commit v6 on v5

--- a/solution.py
+++ b/solution.py
@@ -414,48 +414,51 @@
     return jnp.concatenate([w_ref[(j,) + lead] for j in range(4)], axis=-1)
 
 
-def split_small(whole, n_sp):
-    c = whole.shape[1]
-    cols, out = 3 * c // n_sp, c // n_sp
-    chunk = cols + out
-    return (
-        jnp.concatenate([whole[j * chunk : j * chunk + cols] for j in range(n_sp)]),
-        jnp.concatenate([whole[j * chunk + cols : (j + 1) * chunk] for j in range(n_sp)]),
-    )
+def three_parts(v):
+    a = v.astype(BF16).astype(F32)
+    b = (v - a).astype(BF16).astype(F32)
+    return a, b, v - a - b
+
+
+AHEAD = 2
 
 
 def attention_kernel(
-    n_sp, BQ, BK, kv, qg, text, keep, od, dkv, dt,
-    kv_r, qg_r, od_s, dkv_s, dt_s, k_s, v_s, s_s, e_s, dk_s, dv_s, lsem, ssem, rsem,
+    n_sp, BK, kv, qin, gin, text, keep, of, qf, dkv, dt,
+    kv_r, q_r, g_r, q_s, o_s, dq_o, dkv_s, dt_s, k_s, v_s, s_s, e_s, g_s, dq_s, peak_s, lsem, ssem, rsem,
 ):
     at = Place()
+    nz = n_sp // 2
     px = kv.shape[1]
     L, T = n_sp * px, text.shape[1]
     d = kv.shape[2] // 2
+    BQ = px // 2
     line = [at.rp(k, n_sp) for k in range(1, n_sp)]
     greet(line)
     own = [
         pltpu.make_async_copy(kv.at[at.s], kv_r.at[at.s], lsem.at[0]),
-        pltpu.make_async_copy(qg.at[at.s], qg_r.at[at.s], lsem.at[1]),
+        pltpu.make_async_copy(qin.at[at.s], q_r.at[at.s], lsem.at[1]),
+        pltpu.make_async_copy(gin, g_r, lsem.at[6]),
     ]
     for cp in own:
         cp.start()
     greeted(n_sp - 1)
-    sent = [remote(kv.at[dev[1]], kv_r.at[at.s], ssem.at[0, k + 1], rsem.at[0, k + 1], dev) for k, dev in enumerate(line)]
+    keys = [remote(kv.at[dev[1]], kv_r.at[at.s], ssem.at[0, k + 1], rsem.at[0, k + 1], dev) for k, dev in enumerate(line)]
     odd = lax.rem(at.s, 2)
     pair = lax.div(at.s, 2)
-    ones = (lax.broadcasted_iota(jnp.int32, (1, d), 1) == 0).astype(BF16)
+    ones = (lax.broadcasted_iota(jnp.int32, (1, d), 1) < 3).astype(F32).astype(BF16)
     picked = []
     for j in (pair, HEADS // 2 + pair):
         blk = text[j].astype(F32)
         picked.append(jnp.where(odd > 0, blk[:, d:], blk[:, :d]).astype(BF16))
     k_s[0:T, :] = picked[0]
     v_s[0:T, :] = jnp.concatenate([picked[1], jnp.broadcast_to(ones, (T, d))], axis=1)
-    dk_s[...] = jnp.zeros_like(dk_s)
-    dv_s[...] = jnp.zeros_like(dv_s)
+
+    def rows_of(o, n=px, start=0):
+        return pl.ds(pl.multiple_of(o * px + start, 128), n)
 
     def take(j):
-        rows = pl.ds(pl.multiple_of(T + j * px, px if T % px == 0 else T), px)
+        rows = rows_of(j, px, T)
         k_s[rows, :] = kv_r[j][:, :d]
         v_s[rows, :] = jnp.concatenate([kv_r[j][:, d:], jnp.broadcast_to(ones, (px, d))], axis=1)
 
@@ -463,127 +466,195 @@
         cp.wait()
     take(at.s)
     for k in range(1, n_sp):
-        sent[k - 1].wait_recv()
+        keys[k - 1].wait_recv()
         take(lax.rem(at.s - k + n_sp, n_sp))
-    sent += [remote(qg.at[dev[1]], qg_r.at[at.s], ssem.at[1, k + 1], rsem.at[1, k + 1], dev) for k, dev in enumerate(line)]
-
     blocks = [(0, T)] + [(T + j * BK, BK) for j in range(L // BK)]
-    per = px // BQ
     scale = d ** -0.5
 
     def query_copy(k):
         return pltpu.make_async_remote_copy(
-            src_ref=qg.at[at.s], dst_ref=qg_r.at[at.s], send_sem=ssem.at[1, k], recv_sem=rsem.at[1, k],
-            device_id=(at.i, lax.rem(at.s + k, n_sp)), device_id_type=MESH,
+            src_ref=qin.at[lax.rem(at.s + k, n_sp)], dst_ref=q_r.at[at.s], send_sem=ssem.at[1, k],
+            recv_sem=rsem.at[1, k], device_id=(at.i, lax.rem(at.s + k, n_sp)), device_id_type=MESH,
         )
 
-    def back_copy(k, o):
+    def back_copy(j, k, src, dst, o):
         return pltpu.make_async_remote_copy(
-            src_ref=od_s.at[o], dst_ref=od.at[at.s], send_sem=ssem.at[2, k], recv_sem=rsem.at[2, k],
+            src_ref=src.at[o], dst_ref=dst.at[at.s], send_sem=ssem.at[j, k], recv_sem=rsem.at[j, k],
             device_id=(at.i, o), device_id_type=MESH,
         )
 
-    def step(t, _):
-        k, part = lax.div(t, per), lax.rem(t, per)
-        o_dev = lax.rem(at.s - k + n_sp, n_sp)
-
-        @pl.when(jnp.logical_and(part == 0, k > 0))
-        def _():
-            query_copy(k).wait_recv()
-
-        r = pl.ds(pl.multiple_of(part * BQ, BQ), BQ)
-        both = qg_r[o_dev, r, :]
-        q, g = both[:, :d], both[:, d:]
+    def scores(q, slot, st, n, peak):
+        s = dot(q, k_s[st : st + n, :], 1, 1)
+        if st == 0:
+            s = jnp.where(keep[...] > 0, s, MASKED)
+        s_s[slot, :, st : st + n] = s
+        for j in range(n // 128):
+            piece = s[:, 128 * j : 128 * j + 128]
+            peak = piece if peak is None else jnp.maximum(peak, piece)
+        return peak
+
+    def query(o, part):
+        return q_r[o][:, part * d : (part + 1) * d]
+
+    def forward(o, part, o_next):
+        nxt = query(o_next, 1 - part)
+        g = g_r[o][:, part * d : (part + 1) * d]
+        rows = rows_of(o, BQ, part * BQ)
+        q_s[rows, :] = query(o, part)
+        top = jnp.max(peak_s[part], axis=1, keepdims=True)
+        out = jnp.zeros((BQ, 2 * d), F32)
         peak = None
         for st, n in blocks:
-            s = dot(q, k_s[st : st + n, :], 1, 1)
-            if st == 0:
-                s = jnp.where(keep[...] > 0, s, MASKED)
-            s_s[:, st : st + n] = s
-            for j in range(n // 128):
-                piece = s[:, 128 * j : 128 * j + 128]
-                peak = piece if peak is None else jnp.maximum(peak, piece)
-        peak = jnp.max(peak, axis=1, keepdims=True)
-        o = jnp.zeros((BQ, 2 * d), F32)
-        for st, n in blocks:
-            e = jnp.exp(s_s[:, st : st + n] - peak).astype(BF16)
-            e_s[:, st : st + n] = e
-            o = o + dot(e, v_s[st : st + n, :], 1, 0)
-        inverse = 1.0 / o[:, d : d + 1]
-        o = o[:, :d] * inverse
+            peak = scores(nxt, 1 - part, st, n, peak)
+            e = jnp.exp(s_s[part, :, st : st + n] - top).astype(BF16)
+            e_s[rows, st : st + n] = e
+            out = out + dot(e, v_s[st : st + n, :], 1, 0)
+        peak_s[1 - part] = peak
+        inverse = 1.0 / out[:, d : d + 1]
+        out = out[:, :d] * inverse
         g = g.astype(F32) * inverse
-        row = jnp.sum(o * g, axis=1, keepdims=True)
-        g = g.astype(BF16)
-        gt, qt = g.T, q.T
-        dq = jnp.zeros((BQ, d), F32)
-        for st, n in blocks:
-            e = e_s[:, st : st + n]
-            dp = dot(g, v_s[st : st + n, :d], 1, 1)
-            ds = (e.astype(F32) * (dp - row)).astype(BF16)
-            dq = dq + dot(ds, k_s[st : st + n, :], 1, 0)
-            dv_s[:, st : st + n] += dot(gt, e, 1, 0)
-            dk_s[:, st : st + n] += dot(qt, ds, 1, 0)
-        od_s[o_dev, r, :] = jnp.concatenate([o, dq * scale], axis=1).astype(BF16)
-
-        @pl.when(jnp.logical_and(part == per - 1, k > 0))
+        row = jnp.sum(out * g, axis=1, keepdims=True)
+        lane = lax.broadcasted_iota(jnp.int32, (BQ, d), 1)
+        extra = jnp.zeros((BQ, d), F32)
+        for j, piece in enumerate(three_parts(-row)):
+            extra = jnp.where(lane == j, piece, extra)
+        g_s[rows, :] = jnp.concatenate([g, extra], axis=1).astype(BF16)
+        o_s[o, :, part * d : (part + 1) * d] = out.astype(BF16)
+
+    peak = None
+    for st, n in blocks:
+        peak = scores(query(at.s, 0), 0, st, n, peak)
+    peak_s[0] = peak
+
+    for k in range(1, AHEAD):
+        query_copy(k).start()
+
+    def owner(k, _):
+        o = lax.rem(at.s - k + n_sp, n_sp)
+
+        @pl.when(k + AHEAD < n_sp)
         def _():
-            back_copy(k, o_dev).start()
+            query_copy(k + AHEAD).start()
+
+        forward(o, 0, o)
+
+        @pl.when(k + 1 < n_sp)
+        def _():
+            query_copy(k + 1).wait_recv()
+
+        forward(o, 1, lax.rem(at.s - k - 1 + n_sp, n_sp))
+
+        @pl.when(k > 0)
+        def _():
+            back_copy(2, k, o_s, of, o).start()
 
         return 0
 
-    lax.fori_loop(0, n_sp * per, step, 0)
-    local = [pltpu.make_async_copy(od_s.at[at.s], od.at[at.s], lsem.at[2])]
-
-    def gradients(st, n):
-        return jnp.concatenate([dk_s[:, st : st + n], dv_s[:, st : st + n]], axis=0).astype(BF16).T
-
-    for j in range(n_sp):
-        dkv_s[j] = gradients(T + j * px, px)
-    for k, dev in enumerate(line):
-        sent.append(remote(dkv_s.at[dev[1]], dkv.at[at.s], ssem.at[3, k + 1], rsem.at[3, k + 1], dev))
-    dt_s[...] = gradients(0, T)
-    for k, dev in enumerate(line):
-        sent.append(remote(dt_s, dt.at[at.s], ssem.at[4, k + 1], rsem.at[4, k + 1], dev))
-    local.append(pltpu.make_async_copy(dkv_s.at[at.s], dkv.at[at.s], lsem.at[3]))
-    local.append(pltpu.make_async_copy(dt_s, dt.at[at.s], lsem.at[4]))
+    lax.fori_loop(0, n_sp, owner, 0)
+    local = [pltpu.make_async_copy(o_s.at[at.s], of.at[at.s], lsem.at[2])]
+
+    def block(o, cols, kc, vc, dk, dv, fresh):
+        rows = rows_of(o)
+        g, q = g_s[rows, :], q_s[rows, :]
+        e = e_s[rows, cols]
+        ds = (e.astype(F32) * dot(g, vc, 1, 1)).astype(BF16)
+        part = dot(ds, kc, 1, 0)
+        dq_s[rows, :] = part if fresh else dq_s[rows, :] + part
+        return dk + dot(q.T, ds, 1, 0), dv + dot(g[:, :d].T, e, 1, 0)
+
+    def both(dk, dv):
+        return jnp.concatenate([dk, dv], axis=0).astype(BF16).T
+
+    def chunk(cols, n, fresh):
+        kc, vc = k_s[cols, :], v_s[cols, :]
+        zero = jnp.zeros((d, n), F32)
+        dk, dv = lax.fori_loop(
+            0, n_sp, lambda o, acc: block(o, cols, kc, vc, acc[0], acc[1], fresh), (zero, zero), unroll=4
+        )
+        return both(dk, dv)
+
+    def chip_columns(z):
+        return pl.ds(pl.multiple_of(T + z * (2 * px), 128), 2 * px)
+
+    dt_s[...] = chunk(pl.ds(0, T), T, True)
+    sent = [remote(dt_s, dt.at[at.s], ssem.at[5, k + 1], rsem.at[5, k + 1], dev) for k, dev in enumerate(line)]
+    local.append(pltpu.make_async_copy(dt_s, dt.at[at.s], lsem.at[3]))
+
+    def chip(k, _):
+        z = lax.rem(at.z + k, nz)
+        grads = chunk(chip_columns(z), 2 * px, False)
+        for core in range(2):
+            o = 2 * z + core
+            dkv_s[o] = grads[core * px : (core + 1) * px]
+            back_copy(4, lax.rem(o - at.s + n_sp, n_sp), dkv_s, dkv, o).start()
+        return 0
+
+    lax.fori_loop(1, nz, chip, 0)
+    cols = chip_columns(at.z)
+    kc, vc = k_s[cols, :], v_s[cols, :]
+    zero = jnp.zeros((d, 2 * px), F32)
+
+    def last(j, acc):
+        o = 2 * lax.rem(at.z + 1 + lax.div(j, 2), nz) + lax.rem(j, 2)
+        acc = block(o, cols, kc, vc, acc[0], acc[1], False)
+        dq = (dq_s[rows_of(o), :] * scale).astype(BF16)
+        dq_o[o] = jnp.concatenate([dq[:BQ], dq[BQ:]], axis=1)
+
+        @pl.when(o != at.s)
+        def _():
+            back_copy(3, lax.rem(o - at.s + n_sp, n_sp), dq_o, qf, o).start()
+
+        return acc
+
+    grads = both(*lax.fori_loop(0, n_sp, last, (zero, zero)))
+    for core in range(2):
+        dkv_s[2 * at.z + core] = grads[core * px : (core + 1) * px]
+    sib = at.sib[1]
+    back_copy(4, lax.rem(sib - at.s + n_sp, n_sp), dkv_s, dkv, sib).start()
+    local.append(pltpu.make_async_copy(dkv_s.at[at.s], dkv.at[at.s], lsem.at[4]))
+    local.append(pltpu.make_async_copy(dq_o.at[at.s], qf.at[at.s], lsem.at[5]))
     for cp in local:
         cp.start()
     for k in range(1, n_sp):
-        back_copy(k, lax.rem(at.s - k + n_sp, n_sp)).wait()
-    for cp in sent[n_sp - 1 : 2 * (n_sp - 1)]:
+        back_copy(2, k, o_s, of, lax.rem(at.s - k + n_sp, n_sp)).wait()
+        o = lax.rem(at.s + k, n_sp)
+        back_copy(4, k, dkv_s, dkv, o).wait()
+        back_copy(3, k, dq_o, qf, o).wait()
+    for k in range(1, n_sp):
+        query_copy(k).wait_send()
+    for cp in keys:
         cp.wait_send()
-    for cp in sent[: n_sp - 1]:
-        cp.wait_send()
-    for cp in sent[2 * (n_sp - 1) :]:
+    for cp in sent:
         cp.wait()
     for cp in local:
         cp.wait()
 
 
-def attention_call(kv, qg, text, keep, cid):
+def attention_call(kv, qin, gin, text, keep, cid):
     n_sp, px, d2 = kv.shape
     T = text.shape[1]
     L = n_sp * px
     d = d2 // 2
-    BQ, BK = 256, 1024
-    outs = [(n_sp, px, d2), (n_sp, px, d2), (n_sp, T, d2)]
+    outs = [(n_sp, px // 2, d2), (n_sp, px // 2, d2), (n_sp, px, d2), (n_sp, T, d2)]
     vm = pltpu.VMEM
     return pl.pallas_call(
-        functools.partial(attention_kernel, n_sp, BQ, BK),
+        functools.partial(attention_kernel, n_sp, 1024),
         out_shape=[jax.ShapeDtypeStruct(s, BF16) for s in outs],
-        in_specs=[ANY, ANY, VM, VM],
-        out_specs=[ANY] * 3,
+        in_specs=[ANY, ANY, ANY, VM, VM],
+        out_specs=[ANY] * 4,
         scratch_shapes=[
-            vm((n_sp, px, d2), BF16), vm((n_sp, px, d2), BF16), vm((n_sp, px, d2), BF16), vm((n_sp, px, d2), BF16),
-            vm((T, d2), BF16), vm((T + L, d), BF16), vm((T + L, d2), BF16),
-            vm((BQ, T + L), F32), vm((BQ, T + L), BF16), vm((d, T + L), F32), vm((d, T + L), F32),
-            pltpu.SemaphoreType.DMA((5,)),
-            pltpu.SemaphoreType.DMA((5, n_sp)),
-            pltpu.SemaphoreType.DMA((5, n_sp)),
+            vm((n_sp, px, d2), BF16), vm((n_sp, px // 2, d2), BF16), vm((n_sp, px // 2, d2), BF16), vm((L, d), BF16),
+            vm((n_sp, px // 2, d2), BF16),
+            vm((n_sp, px // 2, d2), BF16), vm((n_sp, px, d2), BF16), vm((T, d2), BF16),
+            vm((T + L, d), BF16), vm((T + L, d2), BF16), vm((2, px // 2, T + L), F32), vm((L, T + L), BF16),
+            vm((L, d2), BF16), vm((L, d), F32), vm((2, px // 2, 128), F32),
+            pltpu.SemaphoreType.DMA((7,)),
+            pltpu.SemaphoreType.DMA((6, n_sp)),
+            pltpu.SemaphoreType.DMA((6, n_sp)),
         ],
         compiler_params=params(cid),
         name="attention",
-    )(kv, qg, text, keep)
+    )(kv, qin, gin, text, keep)
 
 
 class Mail:
@@ -602,6 +673,7 @@
         self.at, self.nz, self.ins, self.outs, self.dims = at, nz, ins, outs, dims
         self.ssem, self.rsem = ssem, rsem
         self.sent, self.kinds = {}, {}
+        self.order = sorted(range(1, nz), key=lambda k: min(k, nz - k))
 
     @staticmethod
     def copies(nz):
@@ -622,18 +694,20 @@
     def forward(self, a, kind, ref, dev):
         self.send(a, kind, ref, ref, dev)
 
-    def first(self, a):
+    def near(self, a):
         at = self.at
         own = self.view(a, at.i, 0, at.c)
-        for k in range(1, self.nz):
-            self.send(a, ("z", k), self.ins[a], own, at.zp(k, self.nz))
         self.send(a, ("x", 0), self.ins[a], own, at.xn)
         self.send(a, ("y", 0), self.ins[a], own, at.yn)
         self.send(a, ("s", 0), self.ins[a], own, at.sib)
 
-    def second(self, a):
+    def along(self, a, ks):
+        for k in ks:
+            self.send(a, ("z", k), self.ins[a], self.view(a, self.at.i, 0, self.at.c), self.at.zp(k, self.nz))
+
+    def second(self, a, ks=None):
         at = self.at
-        for k in range(1, self.nz):
+        for k in self.order if ks is None else ks:
             self.sent[a, ("z", k)].wait_recv()
             got = self.view(a, at.i, k, at.c)
             self.forward(a, ("x", k), got, at.xn)
@@ -642,7 +716,7 @@
 
     def third(self, a):
         at = self.at
-        for k in range(self.nz):
+        for k in [0] + self.order:
             self.sent[a, ("x", k)].wait_recv()
             self.forward(a, ("da", k), self.view(a, at.ix, k, at.c, 0), at.yn)
             self.forward(a, ("sx", k), self.view(a, at.ix, k, at.c), at.sib)
@@ -652,7 +726,7 @@
 
     def fourth(self, a):
         at = self.at
-        for k in range(self.nz):
+        for k in [0] + self.order:
             self.sent[a, ("da", k)].wait_recv()
             self.forward(a, ("sa", k), self.view(a, at.id, k, at.c, 0), at.sib)
             self.sent[a, ("db", k)].wait_recv()
@@ -672,19 +746,19 @@
     return [(lax.rem(at.i + k, 4), at.s) for k in range(1, 4)]
 
 
-FORWARD_MAIL = 3 * 3 + 3 + 2 * 7 + 4 + 7 + 2 * (2 + 7)
+FORWARD_MAIL = 4 * 3 + 3 + 2 * 7 + 4 + 7 + 2 * (2 + 7) + 7
 
 
 def forward_kernel(nz, width, dims, *refs):
     na = len(dims)
-    chunks, refs = refs[: na - 1], refs[na - 1 :]
-    x, cot, temb, cap, w_emb, w_cap, gains, biases, w_qkv, w_proj = refs[:10]
-    outs, refs = refs[10 : 10 + na], refs[10 + na :]
-    hidden_o, act0_o, res_o, act1_o, normed, kv, qg = refs[:7]
-    st0, st1, st2, rows, ca, cb, ra, rb, ha, hb, kv_all, cap_all, emb_all = refs[7:20]
-    refs = refs[20:]
+    chunks, refs = refs[:na], refs[na:]
+    x, cot, temb, cap, w_emb, w_cap, gains, biases = refs[:8]
+    outs, refs = refs[8 : 8 + na], refs[8 + na :]
+    hidden_o, act0_o, res_o, act1_o, g_o, normed, kv, qf = refs[:8]
+    st0, st1, st2, rows, ca, cb, ra, rb, ha, hb, kv_all, cap_all, emb_all = refs[8:21]
+    refs = refs[21:]
     weights, refs = refs[:na], refs[na:]
-    (ssem, rsem, lsem, msend, mrecv, small, emb, affine, mine, every, xa, xb, ca_s, cb_s, ha_s, hb_s, ra_s, rb_s,
+    (ssem, rsem, lsem, msend, mrecv, g_s, emb, affine, mine, every, xa, xb, ca_s, cb_s, ha_s, hb_s, ra_s, rb_s,
      aff_s, emb_s, cap_s, part, part_r, kv_s, kv_r, mod_s, mod_r, a3, act0, act1, hidden, res) = refs
     n_sp = 2 * nz
     at = Place()
@@ -692,13 +766,14 @@
     grid = img_peers(at)
     greet(line + grid)
     mail = Mail(msend, mrecv)
-    got = Gather(at, nz, list(chunks) + [small], weights, dims, ssem, rsem)
+    got = Gather(at, nz, chunks, weights, dims, ssem, rsem)
+    PROJ, IN, OUT, QKV = range(4)
     px, c = x.shape
     height = px // width
     d = c // HEADS
     tokens = cap.shape[0]
     e = cap.shape[1] // 4
-    cut = w_qkv.shape[0]
+    half = px // 2
     local = []
 
     def copy(src, dst):
@@ -707,8 +782,6 @@
         local.append(cp)
         return cp
 
-    small[0, :cut] = w_qkv[...]
-    small[0, cut:] = w_proj[...]
     embedded = silu(temb[...].astype(F32)).astype(BF16).astype(F32)
     for j in range(4):
         emb[j] = jnp.broadcast_to(embedded[:, j * e : (j + 1) * e], (8, e))
@@ -727,26 +800,59 @@
         every[j, at.s] = mine[j]
         return out
 
+    def fold(v):
+        return jnp.concatenate([v[:half], v[half:]], axis=1)
+
     greeted(n_sp + 2)
-    got.first(0)
+    close, far = got.order[:2], got.order[2:]
+    got.along(PROJ, got.order)
+    got.near(PROJ)
+    got.along(IN, close)
+    got.near(IN)
     stat0 = publish(0, x[...].astype(F32), [(x, xa, xb), (cot, ca_s, cb_s)])
     round1 = []
+    share = tokens // 2
+    part_tokens = pl.ds(pl.multiple_of(at.c * share, share), share)
     for dev in grid:
         round1.append(mail.send(affine, aff_s.at[at.i], dev))
         round1.append(mail.send(emb.at[dev[0]], emb_s.at[at.i], dev))
-        round1.append(mail.send(cap.at[:, pl.ds(pl.multiple_of(dev[0] * e, e), e)], cap_s.at[at.i], dev))
+        round1.append(
+            mail.send(cap.at[part_tokens, pl.ds(pl.multiple_of(dev[0] * e, e), e)], cap_s.at[at.i, part_tokens], dev)
+        )
     own_cap = copy(cap.at[:, pl.ds(pl.multiple_of(at.i * e, e), e)], cap_s.at[at.i])
     aff_s[at.i] = affine[...]
     emb_s[at.i] = emb[at.i]
-    got.first(1)
+    got.near(OUT)
     own = [copy(got.ins[a], got.view(a, at.i, 0, at.c)) for a in range(na)]
-    got.second(0)
-    got.first(2)
-    got.third(0)
-    got.second(1)
+    got.second(PROJ)
+    got.second(IN, close[:1])
+    got.along(IN, far)
+    got.second(IN, close[1:])
+    got.third(PROJ)
+    got.near(QKV)
+    got.along(OUT, close)
+    got.second(IN, far)
+    got.along(OUT, far)
+    got.fourth(PROJ)
+    got.third(IN)
+    for cp in own:
+        cp.wait()
+    got.complete(PROJ)
+    g = dot(cot[...], joined(weights[PROJ], 0), 1, 0).astype(BF16)
+    for h in range(HEADS):
+        g_s[h] = fold(g[:, h * d : (h + 1) * d])
+    copy(weights[PROJ], outs[PROJ])
+    got.second(OUT)
+    got.along(QKV, got.order)
 
     own_cap.wait()
     for cp in round1:
+        cp.wait_recv()
+    halves = []
+    for dev in grid:
+        here = cap_s.at[dev[0], part_tokens]
+        halves.append(mail.send(here, here, at.sib))
+    for cp in halves:
         cp.wait_recv()
     for j in range(4):
         part[j, :tokens] = dot(cap_s[j], w_cap[...], 1, 0)
@@ -793,16 +899,16 @@
         cp.wait_recv()
     activate(0, x, xa, xb, act0)
     copy(act0, act0_o)
-    got.fourth(0)
-    for cp in own:
-        cp.wait()
-    got.complete(0)
-    copy(weights[0], outs[0])
-    taps(weights[0], hidden, 0, 3, None)
-    got.second(2)
-    taps(weights[0], hidden, 3, 6, None)
-    got.third(1)
-    taps(weights[0], hidden, 6, 9, None)
+    got.fourth(IN)
+    got.complete(IN)
+    copy(weights[IN], outs[IN])
+    taps(weights[IN], hidden, 0, 3, None)
+    got.second(QKV)
+    round_g = [mail.send(g_s.at[dev[1]], g_o.at[at.s], dev) for dev in line]
+    copy(g_s.at[at.s], g_o.at[at.s])
+    taps(weights[IN], hidden, 3, 6, None)
+    got.third(OUT)
+    taps(weights[IN], hidden, 6, 9, None)
     stat1 = publish(1, hidden[...], [(hidden, ha_s, hb_s)])
     copy(hidden, hidden_o)
     for cp in round2:
@@ -816,8 +922,8 @@
         round3.append(mail.send(mod_s, mod_r.at[at.s], dev))
     kv_r[at.s] = kv_s[...]
     mod_r[at.s] = mod_s[...]
-    got.fourth(1)
-    got.third(2)
+    got.fourth(OUT)
+    got.third(QKV)
     for cp in round3 + stat1:
         cp.wait_recv()
     kv_all[...] = kv_r[...]
@@ -827,18 +933,17 @@
 
     activate(1, hidden, ha_s, hb_s, act1)
     copy(act1, act1_o)
-    got.fourth(2)
-    got.complete(1)
-    copy(weights[1], outs[1])
-    taps(weights[1], res, 0, 9, x)
+    got.fourth(QKV)
+    got.complete(OUT)
+    copy(weights[OUT], outs[OUT])
+    taps(weights[OUT], res, 0, 9, x)
     stat2 = publish(2, res[...], [(res, ra_s, rb_s)])
     copy(res, res_o)
     for dst, src in ((ca, ca_s), (cb, cb_s), (ha, ha_s), (hb, hb_s)):
         dst[...] = src[...]
-    got.complete(2)
-    copy(weights[2], outs[2])
-    wq, wp = split_small(joined(weights[2], 0), n_sp)
-    g = dot(cot[...], wp, 1, 0).astype(BF16)
+    got.complete(QKV)
+    copy(weights[QKV], outs[QKV])
+    wq = joined(weights[QKV], 0)
 
     for cp in stat2:
         cp.wait_recv()
@@ -851,7 +956,7 @@
     for h in range(HEADS):
         lanes = slice(h * d, (h + 1) * d)
         kv[h] = jnp.concatenate([k[:, lanes], v[:, lanes]], axis=1)
-        qg[h] = jnp.concatenate([q[:, lanes], g[:, lanes]], axis=1)
+        qf[h] = fold(q[:, lanes])
     ra[...] = ra_s[...]
     rb[...] = rb_s[...]
     st0[...] = every[0]
@@ -860,12 +965,14 @@
     for cp in local[1 + na :]:
         cp.wait()
     got.finish()
+    for cp in round_g:
+        cp.wait_recv()
     for cp in mail.sent:
         cp.wait_send()
 
 
-def forward_call(chunks, x, cot, temb, cap, w_emb, w_cap, gains, biases, w_qkv, w_proj, nz, width, cid):
-    dims = [c.shape[:2] for c in chunks] + [(1, w_qkv.shape[0] + w_proj.shape[0])]
+def forward_call(chunks, x, cot, temb, cap, w_emb, w_cap, gains, biases, nz, width, cid):
+    dims = [c.shape[:2] for c in chunks]
     na = len(dims)
     n_sp = 2 * nz
     px, c = x.shape
@@ -877,8 +984,8 @@
     edge16, edge32 = ((width, c), BF16), ((width, c), F32)
     stat = ((n_sp, 8, c), F32)
     outs = big + [
-        ((px, c), F32), ((padded, c), BF16), ((px, c), F32), ((padded, c), BF16), ((px, c), BF16),
-        ((HEADS, px, d2), BF16), ((HEADS, px, d2), BF16),
+        ((px, c), F32), ((padded, c), BF16), ((px, c), F32), ((padded, c), BF16),
+        ((n_sp, px // 2, d2), BF16), ((px, c), BF16), ((HEADS, px, d2), BF16), ((HEADS, px // 2, d2), BF16),
         stat, stat, stat, ((3, 8, c), F32), edge16, edge16, edge32, edge32, edge32, edge32,
         ((n_sp, tokens, 128), BF16), ((4, tokens, e), BF16), ((8, e), F32),
     ]
@@ -886,16 +993,16 @@
     return pl.pallas_call(
         functools.partial(forward_kernel, nz, width, dims),
         out_shape=[jax.ShapeDtypeStruct(s, ty) for s, ty in outs],
-        in_specs=[ANY] * (na - 1) + [VM, VM, VM, ANY] + [VM] * 6,
-        out_specs=[ANY] * (na + 4) + [VM] * (len(outs) - na - 4),
+        in_specs=[ANY] * na + [VM, VM, VM, ANY] + [VM] * 4,
+        out_specs=[ANY] * (na + 5) + [VM] * (len(outs) - na - 5),
         scratch_shapes=[vm(s, ty) for s, ty in big]
         + [
             pltpu.SemaphoreType.DMA((na, Gather.copies(nz))),
             pltpu.SemaphoreType.DMA((na, Gather.copies(nz))),
-            pltpu.SemaphoreType.DMA((2 * na + 5,)),
+            pltpu.SemaphoreType.DMA((2 * na + 6,)),
             pltpu.SemaphoreType.DMA((FORWARD_MAIL,)),
             pltpu.SemaphoreType.DMA((FORWARD_MAIL,)),
-            vm((1, dims[-1][1], 128), BF16), vm((4, 8, e), F32), vm((8, 128), F32),
+            vm((HEADS, px // 2, d2), BF16), vm((4, 8, e), F32), vm((8, 128), F32),
             vm((3, 8, c), F32), vm((3, n_sp, 8, c), F32),
         ]
         + [vm(*edge16)] * 4 + [vm(*edge32)] * 4
@@ -907,7 +1014,7 @@
         ],
         compiler_params=params(cid),
         name="forward",
-    )(*chunks, x, cot, temb, cap, w_emb, w_cap, gains, biases, w_qkv, w_proj)
+    )(*chunks, x, cot, temb, cap, w_emb, w_cap, gains, biases)
 
 
 class Reducer:
@@ -1021,7 +1128,7 @@
 
 BACK_MAIL = 6 + 14 + 6 + 3 + 7 + 9 + 9
 BACK_GROUPS = 7
-BIG = 10
+BIG = 12
 
 
 def conv_taps(t0, t1, w, ring, rsem, one):
@@ -1067,7 +1174,7 @@
         cp = pltpu.make_async_copy(hbm[j], big[j], bsem.at[j])
         cp.start()
         loads.append(cp)
-    od, dkv, w_small, res, cot, normed, act1, hidden, act0, x = big
+    of, qf, dkv, w_qkv, w_proj, res, cot, normed, act1, hidden, act0, x = big
     ring_start(w_out, ring, rsem)
     mail = Mail(msend, mrecv)
     red = Reducer(at, nz, [(s_out, bufs[0]), (s_small, bufs[1]), (s_in, bufs[2])], gsend, grecv)
@@ -1090,16 +1197,17 @@
         every[j, at.s] = mine[j]
         return out
 
-    for j in range(6):
+    for j in range(8):
         loads[j].wait()
-    att = jnp.concatenate([od[h][:, :d] for h in range(HEADS)], axis=1)
+    unfold = lambda v: jnp.concatenate([v[:, :d], v[:, d:]], axis=0)
+    att = jnp.concatenate([unfold(of[h]) for h in range(HEADS)], axis=1)
     pg = jnp.concatenate(
-        [od[h][:, d:] for h in range(HEADS)]
+        [unfold(qf[h]) for h in range(HEADS)]
         + [dkv[h][:, :d] for h in range(HEADS)]
         + [dkv[h][:, d:] for h in range(HEADS)],
         axis=1,
     )
-    wq, wp = split_small(joined(w_small), n_sp)
+    wq, wp = joined(w_qkv), joined(w_proj)
     ng[...] = dot(pg, wq, 1, 0)
     center2, inverse2 = combine_stats(st2, px)
     hat = (res[...] - center2) * inverse2
@@ -1179,7 +1287,7 @@
 
     for cp in round_2:
         cp.wait_recv()
-    loads[6].wait()
+    loads[8].wait()
     t2 = upstream(2, ng, na, nb, center2, inverse2, res, ra, rb, act1, (cot, ca, cb), res_grad)
     red.run(1, 0)
     for tap in (0, 3, 6):
@@ -1187,7 +1295,7 @@
     red.run(2, 0)
     input_taps(w_out)
     ring_start(w_in, ring, rsem)
-    for j in range(7, BIG):
+    for j in range(9, BIG):
         loads[j].wait()
     center1, inverse1 = combine_stats(st1, px)
     hat = (hidden[...] - center1) * inverse1
@@ -1292,11 +1400,11 @@
 
 
 def backward_call(big, w_in, w_out, small, nz, width, cid):
-    px, c = big[3].shape
+    px, c = big[5].shape
     n_sp = 2 * nz
     padded = px + 2 * width
     r = c // n_sp
-    rs = big[2].shape[1] // n_sp
+    rs = (big[3].shape[1] + big[4].shape[1]) // n_sp
     dt_all, cap_all = small[10], small[11]
     tokens = dt_all.shape[1]
     e = cap_all.shape[2]
@@ -1397,16 +1505,16 @@
     cot = cotangent.reshape(px, c)
 
     flat = lambda w: w.transpose(1, 2, 3, 0).reshape(9, w.shape[3], w.shape[0])
-    (w_in, w_out, w_small, hidden, act0, res, act1, normed, kv, qg,
+    (w_proj, w_in, w_out, w_qkv, hidden, act0, res, act1, g, normed, kv, q,
      st0, st1, st2, rows, ca, cb, ra, rb, ha, hb, kv_all, cap_all, emb_all) = forward_call(
-        [flat(conv_in), flat(conv_out)], x, cot, time_embed, caption[0], embed_proj, caption_proj,
-        norm_gains, norm_biases, qkv_proj.T, out_proj.T, nz, width, 0,
+        [out_proj.T[None], flat(conv_in), flat(conv_out), qkv_proj.T[None]], x, cot, time_embed, caption[0], embed_proj, caption_proj,
+        norm_gains, norm_biases, nz, width, 0,
     )
-    w_small = w_small.reshape(4, -1, 128)
-    od, dkv, dt_all = attention_call(kv, qg, kv_all, caption_mask, 1)
+    w_proj, w_qkv = w_proj[:, 0], w_qkv[:, 0]
+    of, qf, dkv, dt_all = attention_call(kv, q, g, kv_all, caption_mask, 1)
 
     parts = backward_call(
-        [od, dkv, w_small, res, cot, normed, act1, hidden, act0, x], w_in, w_out,
+        [of, qf, dkv, w_qkv, w_proj, res, cot, normed, act1, hidden, act0, x], w_in, w_out,
         [st0, st1, st2, rows, ca, cb, ra, rb, ha, hb, dt_all, cap_all, emb_all, embed_proj, caption_proj, time_embed],
         nz, width, 2,
     )

time: 302 us -> 293 us (0.970)
  Pallas kernels: 301 us -> 291 us
    pallas_call x1, Pallas kernels: 120 us -> 106 us  [attention_call(): pl.pallas_call(functools.partial(attention_kernel, n_sp, 1024), out_shape...]
where the time goes in v6:
time: 293 us; the launch traced here: 292 us
  Pallas kernels  291 us (99%)
    pallas_call x1, Pallas kernels, attention_call(): pl.pallas_call(functools.partial(attention_kernel, n_sp, 1024), out_shape...  106 us
    pallas_call x1, Pallas kernels, backward_call(): pl.pallas_call(functools.partial(backward_kernel, nz, width), out_shape=[...  91.5 us
    pallas_call x1, Pallas kernels, forward_call(): pl.pallas_call(functools.partial(forward_kernel, nz, width, dims), out_sh...  89.7 us

profile of v6, /device:TPU:0, one launch (start us, length us, event | category | flops | bytes accessed | tf_op | source)
XLA Modules:
  0.0 292.2 jit_solution(7407660454758330648)
XLA Ops:
  0.6 89.7 %forward.1 = (bf16[4,1,512,128]{3,2,1,0:T(8,128)(2,1)}, bf16[4,9,512,128]{3,2,1,0:T(8,128)(2,1)}, bf16[4,9,512,128]{3,2,1,0:T(8,128)(2,1)}, bf16[4,1,1536,128]{3...) custom-call(bf16[1,64,128]{2,1,0:T(8,128)(2,1)} %bitcast.38, ...), custom_call_target="tpu_custom_call" | custom-call | tf_op jit(solution)/shard_map/forward/pallas_call | solution.py:993
  90.4 105.7 %attention.1 = (bf16[8,256,128]{2,1,0:T(8,128)(2,1)}, bf16[8,256,128]{2,1,0:T(8,128)(2,1)}, bf16[8,512,128]{2,1,0:T(8,128)(2,1)}, bf16[8,128,128]{2,1,0:T(8,128)(2,1)}) custom-call(bf16[8,512,128]{2,1,0:T(8,128)(2,1)} %get-tuple-element.63.kv, bf16[8,256,128]{2,1,0:T(8,128)(2,1)} %get-tuple-element.64.qin, bf16[8,256,128]{2,1,0:T(8,128)(2,1)} %get-tuple-element.65.gin, ...), custom_call_target="tpu_custom_call" | custom-call | tf_op jit(solution)/shard_map/attention/pallas_call | solution.py:640
  196.1 91.5 %backward.1 = (bf16[512,512]{1,0:T(8,128)(2,1)}, f32[512,512]{1,0:T(8,128)}, f32[9,64,128]{2,1,0:T(8,128)}, f32[9,64,128]{2,1,0:T(8,128)}, f32[1,256,128]{2,1,0:...) custom-call(bf16[8,256,128]{2,1,0:T(8,128)(2,1)} %get-tuple-element., ...), custom_call_target="tpu_custom_call" | custom-call | tf_op jit(solution)/shard_map/backward/pallas_call | solution.py:1417
  287.6 4.4 %emit.1 = (bf16[512,512]{1,0:T(8,128)(2,1)}, f32[512,512]{1,0:T(8,128)}, f32[1,2048]{1,0:T(1,128)}, f32[16,2048]{1,0:T(8,128)}, f32[9,64,128]{2,1,0:T(8,128)}, /...) custom-call(bf16[512,512]{1,0:T(8,128)(2,1)} %get-tuple-element.92.r, ...), custom_call_target="tpu_custom_call" | custom-call | tf_op jit(solution)/shard_map/emit/pallas_call | solution.py:1484

commit v7 on v6

--- a/solution.py
+++ b/solution.py
@@ -351,16 +351,27 @@
 
 ANY = pl.BlockSpec(memory_space=pl.ANY)
 VM = pl.BlockSpec(memory_space=pltpu.VMEM)
-def channel_stats(mine, v):
+def channel_stats(v):
     mean = jnp.sum(v, axis=0, keepdims=True) / v.shape[0]
     dev = v - mean
-    mine[0:1, :] = mean
-    mine[1:2, :] = jnp.sum(dev * dev, axis=0, keepdims=True)
+    return mean, jnp.sum(dev * dev, axis=0, keepdims=True)
+
+
+def put_rows(dst, pair):
+    n = pair[0].shape[1] // 128
+    for a, row in enumerate(pair):
+        for j in range(n):
+            dst[a * n + j : a * n + j + 1, :] = row[:, j * 128 : (j + 1) * 128]
+
+
+def get_rows(block):
+    n = block.shape[0] // 2
+    return tuple(jnp.concatenate([block[a * n + j : a * n + j + 1] for j in range(n)], axis=1) for a in range(2))
 
 
 def group_total(rows):
     c = rows.shape[1]
-    size = c // GROUPS
+    size = 512 // GROUPS
     a = lax.broadcasted_iota(jnp.int32, (128, 128), 0)
     b = lax.broadcasted_iota(jnp.int32, (128, 128), 1)
     same = jnp.where(lax.bitwise_xor(a, b) < size, 1.0, 0.0).astype(BF16)
@@ -377,25 +388,26 @@
 
 
 def combine_stats(every, px):
-    n_sp, _, c = every.shape
-    size = c // GROUPS
-    means = [every[j, 0:1, :] for j in range(n_sp)]
+    n_sp, rows, lanes = every.shape
+    half = rows // 2
+    size = half * lanes // GROUPS
+    means = [every[j, :half, :] for j in range(n_sp)]
     center_c = sum(means) / n_sp
-    dev = sum(every[j, 1:2, :] for j in range(n_sp))
+    dev = sum(every[j, half:, :] for j in range(n_sp))
     dev = dev + px * sum((m - center_c) * (m - center_c) for m in means)
-    center = group_total(jnp.broadcast_to(center_c, (8, c)))[0:1] / size
+    spread = lambda v: group_total(jnp.concatenate([v, v]))[:half]
+    center = spread(center_c) / size
     off = center_c - center
-    dev = dev + (px * n_sp) * (off * off)
-    var = group_total(jnp.broadcast_to(dev, (8, c)))[0:1] / (px * n_sp * size)
-    return center, lax.rsqrt(var + EPSILON)
+    var = spread(dev + (px * n_sp) * (off * off)) / (px * n_sp * size)
+    return get_rows(jnp.concatenate([center, lax.rsqrt(var + EPSILON)]))
 
 
 def combine_sums(every):
-    n_sp = every.shape[0]
     total = every[0]
-    for j in range(1, n_sp):
+    for j in range(1, every.shape[0]):
         total = total + every[j]
-    return total
+    a, b = get_rows(total)
+    return jnp.concatenate([a, b, jnp.zeros((6, a.shape[1]), F32)])
 
 
 def edge_flags(n_sp, s):
@@ -754,12 +766,12 @@
     chunks, refs = refs[:na], refs[na:]
     x, cot, temb, cap, w_emb, w_cap, gains, biases = refs[:8]
     outs, refs = refs[8 : 8 + na], refs[8 + na :]
-    hidden_o, act0_o, res_o, act1_o, g_o, normed, kv, qf = refs[:8]
+    hidden_o, a0_o, res_o, a1_o, g_o, normed, kv, qf = refs[:8]
     st0, st1, st2, rows, ca, cb, ra, rb, ha, hb, kv_all, cap_all, emb_all = refs[8:21]
     refs = refs[21:]
     weights, refs = refs[:na], refs[na:]
-    (ssem, rsem, lsem, msend, mrecv, g_s, emb, affine, mine, every, xa, xb, ca_s, cb_s, ha_s, hb_s, ra_s, rb_s,
-     aff_s, emb_s, cap_s, part, part_r, kv_s, kv_r, mod_s, mod_r, a3, act0, act1, hidden, res) = refs
+    (ssem, rsem, lsem, msend, mrecv, g_s, emb, affine, mine, every, edge_s, xa, xb, ca_s, cb_s, ha_s, hb_s, ra_s, rb_s,
+     aff_s, emb_s, cap_s, part, part_r, kv_s, kv_r, mod_s, mod_r, acts, hidden, res) = refs
     n_sp = 2 * nz
     at = Place()
     line = [at.rp(k, n_sp) for k in range(1, n_sp)]
@@ -787,14 +799,20 @@
         emb[j] = jnp.broadcast_to(embedded[:, j * e : (j + 1) * e], (8, e))
     affine[0:3] = gains[...].astype(F32)
     affine[3:6] = biases[...].astype(F32)
-    mine[...] = jnp.zeros_like(mine)
 
     def publish(j, v, edges):
-        channel_stats(mine.at[j], v)
+        pair = channel_stats(v)
+        put_rows(mine.at[j], pair)
         out = []
         for ref, above, below in edges:
-            out.append(mail.send(ref.at[px - width :], above, line[0]))
-            out.append(mail.send(ref.at[:width], below, line[-1]))
+            if ref is None:
+                edge_s[j - 1, 0] = (v[px - width :] - pair[0]).astype(BF16)
+                edge_s[j - 1, 1] = (v[:width] - pair[0]).astype(BF16)
+                out.append(mail.send(edge_s.at[j - 1, 0], above, line[0]))
+                out.append(mail.send(edge_s.at[j - 1, 1], below, line[-1]))
+            else:
+                out.append(mail.send(ref.at[px - width :], above, line[0]))
+                out.append(mail.send(ref.at[:width], below, line[-1]))
         for dev in line:
             out.append(mail.send(mine.at[j], every.at[j, at.s], dev))
         every[j, at.s] = mine[j]
@@ -835,13 +853,6 @@
     got.along(OUT, far)
     got.fourth(PROJ)
     got.third(IN)
-    for cp in own:
-        cp.wait()
-    got.complete(PROJ)
-    g = dot(cot[...], joined(weights[PROJ], 0), 1, 0).astype(BF16)
-    for h in range(HEADS):
-        g_s[h] = fold(g[:, h * d : (h + 1) * d])
-    copy(weights[PROJ], outs[PROJ])
     got.second(OUT)
     got.along(QKV, got.order)
 
@@ -870,7 +881,11 @@
 
     has_up, has_dn = edge_flags(n_sp, at.s)
 
-    def activate(j, v, above, below, act):
+    def restore(j, above, below, above_o, below_o):
+        for src, dst, dev in ((above, above_o, line[-1]), (below, below_o, line[0])):
+            dst[...] = src[...].astype(F32) + get_rows(every[j, dev[1]])[0]
+
+    def activate(j, v, above, below):
         center, inverse = combine_stats(every.at[j], px)
         mul = inverse * rows[j, 0:1] * rows[j, 2:3]
         add = rows[j, 1:2] * rows[j, 2:3] + rows[j, 3:4]
@@ -882,10 +897,11 @@
                 t = t * has_up
             elif end:
                 t = t * has_dn
-            act[r * width : (r + 1) * width, :] = t.astype(BF16)
-            shifted(a3, r, width, t)
+            shifted(acts.at[j], r, width, t)
 
     def taps(w, out, t0, t1, base):
+        a3 = acts.at[0 if base is None else 1]
+
         def one(tap, _):
             i, j = lax.div(tap, 3), lax.rem(tap, 3)
             lhs = a3[j, pl.ds(pl.multiple_of(i * width, width), px), :]
@@ -897,19 +913,26 @@
 
     for cp in stat0:
         cp.wait_recv()
-    activate(0, x, xa, xb, act0)
-    copy(act0, act0_o)
+    activate(0, x, xa, xb)
+    copy(acts.at[0], a0_o)
     got.fourth(IN)
+    for cp in own:
+        cp.wait()
     got.complete(IN)
     copy(weights[IN], outs[IN])
     taps(weights[IN], hidden, 0, 3, None)
     got.second(QKV)
+    got.complete(PROJ)
+    g = dot(cot[...], joined(weights[PROJ], 0), 1, 0).astype(BF16)
+    for h in range(HEADS):
+        g_s[h] = fold(g[:, h * d : (h + 1) * d])
+    copy(weights[PROJ], outs[PROJ])
     round_g = [mail.send(g_s.at[dev[1]], g_o.at[at.s], dev) for dev in line]
     copy(g_s.at[at.s], g_o.at[at.s])
     taps(weights[IN], hidden, 3, 6, None)
     got.third(OUT)
     taps(weights[IN], hidden, 6, 9, None)
-    stat1 = publish(1, hidden[...], [(hidden, ha_s, hb_s)])
+    stat1 = publish(1, hidden[...], [(None, ha_s, hb_s)])
     copy(hidden, hidden_o)
     for cp in round2:
         cp.wait_recv()
@@ -931,15 +954,16 @@
     rows[1, 2:3] = 1.0 + mod[:, :c]
     rows[1, 3:4] = mod[:, c:]
 
-    activate(1, hidden, ha_s, hb_s, act1)
-    copy(act1, act1_o)
+    restore(1, ha_s, hb_s, ha, hb)
+    activate(1, hidden, ha, hb)
+    copy(acts.at[1], a1_o)
     got.fourth(QKV)
     got.complete(OUT)
     copy(weights[OUT], outs[OUT])
     taps(weights[OUT], res, 0, 9, x)
-    stat2 = publish(2, res[...], [(res, ra_s, rb_s)])
+    stat2 = publish(2, res[...], [(None, ra_s, rb_s)])
     copy(res, res_o)
-    for dst, src in ((ca, ca_s), (cb, cb_s), (ha, ha_s), (hb, hb_s)):
+    for dst, src in ((ca, ca_s), (cb, cb_s)):
         dst[...] = src[...]
     got.complete(QKV)
     copy(weights[QKV], outs[QKV])
@@ -957,8 +981,7 @@
         lanes = slice(h * d, (h + 1) * d)
         kv[h] = jnp.concatenate([k[:, lanes], v[:, lanes]], axis=1)
         qf[h] = fold(q[:, lanes])
-    ra[...] = ra_s[...]
-    rb[...] = rb_s[...]
+    restore(2, ra_s, rb_s, ra, rb)
     st0[...] = every[0]
     st1[...] = every[1]
     st2[...] = every[2]
@@ -982,9 +1005,9 @@
     d2 = 2 * c // HEADS
     big = [((4, t, n_sp * r, 128), BF16) for t, r in dims]
     edge16, edge32 = ((width, c), BF16), ((width, c), F32)
-    stat = ((n_sp, 8, c), F32)
+    stat = ((n_sp, 8, c // 4), F32)
     outs = big + [
-        ((px, c), F32), ((padded, c), BF16), ((px, c), F32), ((padded, c), BF16),
+        ((px, c), F32), ((3, padded, c), BF16), ((px, c), F32), ((3, padded, c), BF16),
         ((n_sp, px // 2, d2), BF16), ((px, c), BF16), ((HEADS, px, d2), BF16), ((HEADS, px // 2, d2), BF16),
         stat, stat, stat, ((3, 8, c), F32), edge16, edge16, edge32, edge32, edge32, edge32,
         ((n_sp, tokens, 128), BF16), ((4, tokens, e), BF16), ((8, e), F32),
@@ -1003,14 +1026,14 @@
             pltpu.SemaphoreType.DMA((FORWARD_MAIL,)),
             pltpu.SemaphoreType.DMA((FORWARD_MAIL,)),
             vm((HEADS, px // 2, d2), BF16), vm((4, 8, e), F32), vm((8, 128), F32),
-            vm((3, 8, c), F32), vm((3, n_sp, 8, c), F32),
+            vm((3, 8, c // 4), F32), vm((3, n_sp, 8, c // 4), F32), vm((2, 2, width, c), BF16),
         ]
-        + [vm(*edge16)] * 4 + [vm(*edge32)] * 4
+        + [vm(*edge16)] * 8
         + [
             vm((4, 8, 128), F32), vm((4, 8, e), F32), vm((4, tokens, e), BF16),
             vm((4, tokens + 8, 128), F32), vm((4, tokens + 8, 128), F32),
             vm((tokens, 128), BF16), vm((n_sp, tokens, 128), BF16), vm((8, 128), F32), vm((n_sp, 8, 128), F32),
-            vm((3, padded, c), BF16), vm((padded, c), BF16), vm((padded, c), BF16), vm((px, c), F32), vm((px, c), F32),
+            vm((2, 3, padded, c), BF16), vm((px, c), F32), vm((px, c), F32),
         ],
         compiler_params=params(cid),
         name="forward",
@@ -1161,8 +1184,8 @@
     refs = refs[28:]
     big, refs = refs[:BIG], refs[BIG:]
     bufs = [dict(zip(Reducer.NAMES, refs[8 * a : 8 * a + 8])) for a in range(3)]
-    (bsem, gsend, grecv, msend, mrecv, ring, rsem, a3, g3, gt, acc, ng, pre_grad, res_grad,
-     mine, every, na, nb, pa, pb, tg_s, tg_r, mod_s, mod_r,
+    (bsem, gsend, grecv, msend, mrecv, ring, rsem, g3, gt, acc, ng, pre_grad, res_grad,
+     mine, every, edge_s, na, nb, pa, pb, tg_s, tg_r, mod_s, mod_r,
      gc_s, gc_r, pe_s, pe_r, gs_s, gs_r, ps_s, ps_r, aff_s, aff_r) = refs[24:]
     n_sp = 2 * nz
     at = Place()
@@ -1174,7 +1197,7 @@
         cp = pltpu.make_async_copy(hbm[j], big[j], bsem.at[j])
         cp.start()
         loads.append(cp)
-    of, qf, dkv, w_qkv, w_proj, res, cot, normed, act1, hidden, act0, x = big
+    of, qf, dkv, w_qkv, w_proj, res, cot, normed, a3_out, hidden, a3_in, x = big
     ring_start(w_out, ring, rsem)
     mail = Mail(msend, mrecv)
     red = Reducer(at, nz, [(s_out, bufs[0]), (s_small, bufs[1]), (s_in, bufs[2])], gsend, grecv)
@@ -1186,12 +1209,13 @@
 
     def publish(j, rows01, edges):
         out = []
+        put_rows(mine.at[j], rows01)
         for ref, above, below in edges:
-            out.append(mail.send(ref.at[px - width :], above, line[0]))
-            out.append(mail.send(ref.at[:width], below, line[-1]))
-        mine[j] = jnp.zeros((8, c), F32)
-        mine[j, 0:1] = rows01[0]
-        mine[j, 1:2] = rows01[1]
+            mean = rows01[0] / px
+            edge_s[j - 1, 0] = (ref[px - width :, :] - mean).astype(BF16)
+            edge_s[j - 1, 1] = (ref[:width, :] - mean).astype(BF16)
+            out.append(mail.send(edge_s.at[j - 1, 0], above, line[0]))
+            out.append(mail.send(edge_s.at[j - 1, 1], below, line[-1]))
         for dev in line:
             out.append(mail.send(mine.at[j], every.at[j, at.s], dev))
         every[j, at.s] = mine[j]
@@ -1238,7 +1262,7 @@
 
     has_up, has_dn = edge_flags(n_sp, at.s)
 
-    def upstream(j, uu, ua, ub, center, inverse, yy, ya, yb, act, base, keep):
+    def upstream(j, uu, ua, ub, center, inverse, yy, ya, yb, base, keep):
         total = combine_sums(every[j])
         mul = rows[j, 0:1] * rows[j, 2:3]
         back = group_total(total * mul) / members
@@ -1246,7 +1270,11 @@
         for r in range(height + 2):
             cut = slice((r - 1) * width, r * width)
             top, end = r == 0, r == height + 1
-            un = ua[...] if top else ub[...] if end else uu[cut, :]
+            if top or end:
+                near = line[-1] if top else line[0]
+                un = (ua if top else ub)[...].astype(F32) + get_rows(every[j, near[1]])[0] / px
+            else:
+                un = uu[cut, :]
             yn = ya[...] if top else yb[...] if end else yy[cut, :]
             g = inverse * (un * mul - s1 - (yn - center) * inverse * s2)
             if base:
@@ -1258,12 +1286,12 @@
             elif keep is not None:
                 keep[cut, :] = g
             shifted(g3, r, width, g.astype(BF16).astype(F32))
-            shifted(a3, r, width, act[r * width : (r + 1) * width, :].astype(F32))
         gt[...] = g3[1, width : width + px, :].T
         return total
 
     def weight_taps(a, t0, t1):
         dst = bufs[a]["d"]
+        a3 = a3_in if a == 2 else a3_out
 
         def one(tap, _):
             i, j = lax.div(tap, 3), lax.rem(tap, 3)
@@ -1287,9 +1315,9 @@
 
     for cp in round_2:
         cp.wait_recv()
+    t2 = upstream(2, ng, na, nb, center2, inverse2, res, ra, rb, (cot, ca, cb), res_grad)
+    red.run(1, 0)
     loads[8].wait()
-    t2 = upstream(2, ng, na, nb, center2, inverse2, res, ra, rb, act1, (cot, ca, cb), res_grad)
-    red.run(1, 0)
     for tap in (0, 3, 6):
         weight_taps(0, tap, tap + 3)
     red.run(2, 0)
@@ -1325,7 +1353,7 @@
 
     for cp in round_1:
         cp.wait_recv()
-    t1 = upstream(1, pre_grad, pa, pb, center1, inverse1, hidden, ha, hb, act0, None, None)
+    t1 = upstream(1, pre_grad, pa, pb, center1, inverse1, hidden, ha, hb, None, None)
     mod = jnp.concatenate([t1[1:2] * gain1 + t1[0:1] * bias1, t1[0:1]], axis=1)
     for j in range(n_sp):
         mod_s[j] = jnp.broadcast_to(mod[:, j * 128 : (j + 1) * 128], (8, 128))
@@ -1337,6 +1365,7 @@
     weight_taps(2, 3, 6)
     red.run(2, 3)
     weight_taps(2, 6, 9)
+    red.run(1, 4, 5, 6)
     input_taps(w_in)
 
     center0, inverse0 = combine_stats(st0, px)
@@ -1346,8 +1375,9 @@
     acc[...] = v
     sums = (jnp.sum(v, axis=0, keepdims=True), jnp.sum(v * hat, axis=0, keepdims=True))
     round_0 = publish(0, sums, [])
-    red.run(1, 4, 5, 6)
     red.run(4, 0)
+    red.run(3, 1)
+    red.run(2, 4)
     for cp in round_m:
         cp.wait_recv()
     mods = jnp.concatenate([mod_r[j][0:1] for j in range(4)] + [jnp.zeros((4, 128), F32)])
@@ -1367,7 +1397,7 @@
     aff_r[at.i] = aff_s[at.i]
     total = group_total(t0 * gain0) / members
     image_grad[...] = res_grad[...] + inverse0 * (acc[...] * gain0 - total[0:1] - hat * total[1:2])
-    for g in (1, 2, 3):
+    for g in (2, 3):
         red.run(3, g)
         red.run(2, g + 3)
     for cp in round_b + round_p:
@@ -1429,10 +1459,10 @@
             pltpu.SemaphoreType.DMA((BACK_MAIL,)),
             vm((3, 4, c, 128), BF16),
             pltpu.SemaphoreType.DMA((3,)),
-            vm((3, padded, c), BF16), vm((3, padded, c), BF16), vm((c, px), BF16),
+            vm((3, padded, c), BF16), vm((c, px), BF16),
             vm((px, c), F32), vm((px, c), F32), vm((px, c), F32), vm((px, c), F32),
-            vm((3, 8, c), F32), vm((3, n_sp, 8, c), F32),
-            vm((width, c), F32), vm((width, c), F32), vm((width, c), F32), vm((width, c), F32),
+            vm((3, 8, c // 4), F32), vm((3, n_sp, 8, c // 4), F32), vm((2, 2, width, c), BF16),
+            vm((width, c), BF16), vm((width, c), BF16), vm((width, c), BF16), vm((width, c), BF16),
             vm((tokens, 128), BF16), vm((4, tokens, 128), BF16),
             vm((n_sp, 8, 128), F32), vm((4, 8, 128), F32),
             vm((4, tokens, e), BF16), vm((n_sp, 4, share, e), BF16),
@@ -1505,7 +1535,7 @@
     cot = cotangent.reshape(px, c)
 
     flat = lambda w: w.transpose(1, 2, 3, 0).reshape(9, w.shape[3], w.shape[0])
-    (w_proj, w_in, w_out, w_qkv, hidden, act0, res, act1, g, normed, kv, q,
+    (w_proj, w_in, w_out, w_qkv, hidden, a3_in, res, a3_out, g, normed, kv, q,
      st0, st1, st2, rows, ca, cb, ra, rb, ha, hb, kv_all, cap_all, emb_all) = forward_call(
         [out_proj.T[None], flat(conv_in), flat(conv_out), qkv_proj.T[None]], x, cot, time_embed, caption[0], embed_proj, caption_proj,
         norm_gains, norm_biases, nz, width, 0,
@@ -1514,7 +1544,7 @@
     of, qf, dkv, dt_all = attention_call(kv, q, g, kv_all, caption_mask, 1)
 
     parts = backward_call(
-        [of, qf, dkv, w_qkv, w_proj, res, cot, normed, act1, hidden, act0, x], w_in, w_out,
+        [of, qf, dkv, w_qkv, w_proj, res, cot, normed, a3_out, hidden, a3_in, x], w_in, w_out,
         [st0, st1, st2, rows, ca, cb, ra, rb, ha, hb, dt_all, cap_all, emb_all, embed_proj, caption_proj, time_embed],
         nz, width, 2,
     )

time: 293 us -> 274 us (0.935)
  Pallas kernels: 291 us -> 273 us
    pallas_call x1, Pallas kernels: 91.5 us -> 80.5 us  [backward_call(): pl.pallas_call(functools.partial(backward_kernel, nz, width), out_shape=[...]
    pallas_call x1, Pallas kernels: 89.7 us -> 83.1 us  [forward_call(): pl.pallas_call(functools.partial(forward_kernel, nz, width, dims), out_sh...]
where the time goes in v7:
time: 274 us
  Pallas kernels  273 us (100%)
    pallas_call x1, Pallas kernels, attention_call(): pl.pallas_call(functools.partial(attention_kernel, n_sp, 1024), out_shape...  105 us
    pallas_call x1, Pallas kernels, forward_call(): pl.pallas_call(functools.partial(forward_kernel, nz, width, dims), out_sh...  83.1 us
    pallas_call x1, Pallas kernels, backward_call(): pl.pallas_call(functools.partial(backward_kernel, nz, width), out_shape=[...  80.5 us

profile of v7, /device:TPU:0, one launch (start us, length us, event | category | flops | bytes accessed | tf_op | source)
XLA Modules:
  0.0 273.8 jit_solution(9745818742796979643)
XLA Ops:
  0.6 83.1 %forward.1 = (bf16[4,1,512,128]{3,2,1,0:T(8,128)(2,1)}, bf16[4,9,512,128]{3,2,1,0:T(8,128)(2,1)}, bf16[4,9,512,128]{3,2,1,0:T(8,128)(2,1)}, bf16[4,1,1536,128]{3...) custom-call(bf16[1,64,128]{2,1,0:T(8,128)(2,1)} %bitcast.38, ...), custom_call_target="tpu_custom_call" | custom-call | tf_op jit(solution)/shard_map/forward/pallas_call | solution.py:1016
  83.7 105.0 %attention.1 = (bf16[8,256,128]{2,1,0:T(8,128)(2,1)}, bf16[8,256,128]{2,1,0:T(8,128)(2,1)}, bf16[8,512,128]{2,1,0:T(8,128)(2,1)}, bf16[8,128,128]{2,1,0:T(8,128)(2,1)}) custom-call(bf16[8,512,128]{2,1,0:T(8,128)(2,1)} %get-tuple-element.63.kv, bf16[8,256,128]{2,1,0:T(8,128)(2,1)} %get-tuple-element.64.qin, bf16[8,256,128]{2,1,0:T(8,128)(2,1)} %get-tuple-element.65.gin, ...), custom_call_target="tpu_custom_call" | custom-call | tf_op jit(solution)/shard_map/attention/pallas_call | solution.py:652
  188.8 80.5 %backward.1 = (bf16[512,512]{1,0:T(8,128)(2,1)}, f32[512,512]{1,0:T(8,128)}, f32[9,64,128]{2,1,0:T(8,128)}, f32[9,64,128]{2,1,0:T(8,128)}, f32[1,256,128]{2,1,0:...) custom-call(bf16[8,256,128]{2,1,0:T(8,128)(2,1)} %get-tuple-element., ...), custom_call_target="tpu_custom_call" | custom-call | tf_op jit(solution)/shard_map/backward/pallas_call | solution.py:1447
  269.2 4.4 %emit.1 = (bf16[512,512]{1,0:T(8,128)(2,1)}, f32[512,512]{1,0:T(8,128)}, f32[1,2048]{1,0:T(1,128)}, f32[16,2048]{1,0:T(8,128)}, f32[9,64,128]{2,1,0:T(8,128)}, /...) custom-call(bf16[512,512]{1,0:T(8,128)(2,1)} %get-tuple-element.92.r, ...), custom_call_target="tpu_custom_call" | custom-call | tf_op jit(solution)/shard_map/emit/pallas_call | solution.py:1514

commit v8 on v7

--- a/solution.py
+++ b/solution.py
@@ -432,7 +432,7 @@
     return a, b, v - a - b
 
 
-AHEAD = 2
+AHEAD = 3
 
 
 def attention_kernel(
@@ -456,6 +456,19 @@
         cp.start()
     greeted(n_sp - 1)
     keys = [remote(kv.at[dev[1]], kv_r.at[at.s], ssem.at[0, k + 1], rsem.at[0, k + 1], dev) for k, dev in enumerate(line)]
+
+    def source(k):
+        return 2 * lax.rem(at.z - lax.div(k, 2) + nz, nz) + lax.rem(at.c + lax.rem(k, 2), 2)
+
+    def target(k):
+        return 2 * lax.rem(at.z + lax.div(k, 2), nz) + lax.rem(at.c + lax.rem(k, 2), 2)
+
+    def query_copy(k):
+        return pltpu.make_async_remote_copy(
+            src_ref=qin.at[target(k)], dst_ref=q_r.at[at.s], send_sem=ssem.at[1, k], recv_sem=rsem.at[1, k],
+            device_id=(at.i, target(k)), device_id_type=MESH,
+        )
+
     odd = lax.rem(at.s, 2)
     pair = lax.div(at.s, 2)
     ones = (lax.broadcasted_iota(jnp.int32, (1, d), 1) < 3).astype(F32).astype(BF16)
@@ -474,6 +487,8 @@
         k_s[rows, :] = kv_r[j][:, :d]
         v_s[rows, :] = jnp.concatenate([kv_r[j][:, d:], jnp.broadcast_to(ones, (px, d))], axis=1)
 
+    for k in range(1, AHEAD):
+        query_copy(k).start()
     for cp in own:
         cp.wait()
     take(at.s)
@@ -482,12 +497,6 @@
         take(lax.rem(at.s - k + n_sp, n_sp))
     blocks = [(0, T)] + [(T + j * BK, BK) for j in range(L // BK)]
     scale = d ** -0.5
-
-    def query_copy(k):
-        return pltpu.make_async_remote_copy(
-            src_ref=qin.at[lax.rem(at.s + k, n_sp)], dst_ref=q_r.at[at.s], send_sem=ssem.at[1, k],
-            recv_sem=rsem.at[1, k], device_id=(at.i, lax.rem(at.s + k, n_sp)), device_id_type=MESH,
-        )
 
     def back_copy(j, k, src, dst, o):
         return pltpu.make_async_remote_copy(
@@ -538,11 +547,8 @@
         peak = scores(query(at.s, 0), 0, st, n, peak)
     peak_s[0] = peak
 
-    for k in range(1, AHEAD):
-        query_copy(k).start()
-
     def owner(k, _):
-        o = lax.rem(at.s - k + n_sp, n_sp)
+        o = source(k)
 
         @pl.when(k + AHEAD < n_sp)
         def _():
@@ -554,7 +560,7 @@
         def _():
             query_copy(k + 1).wait_recv()
 
-        forward(o, 1, lax.rem(at.s - k - 1 + n_sp, n_sp))
+        forward(o, 1, source(lax.rem(k + 1, n_sp)))
 
         @pl.when(k > 0)
         def _():
@@ -628,7 +634,7 @@
     for cp in local:
         cp.start()
     for k in range(1, n_sp):
-        back_copy(2, k, o_s, of, lax.rem(at.s - k + n_sp, n_sp)).wait()
+        back_copy(2, k, o_s, of, source(k)).wait()
         o = lax.rem(at.s + k, n_sp)
         back_copy(4, k, dkv_s, dkv, o).wait()
         back_copy(3, k, dq_o, qf, o).wait()
@@ -847,7 +853,6 @@
     got.along(IN, far)
     got.second(IN, close[1:])
     got.third(PROJ)
-    got.near(QKV)
     got.along(OUT, close)
     got.second(IN, far)
     got.along(OUT, far)
@@ -921,7 +926,6 @@
     got.complete(IN)
     copy(weights[IN], outs[IN])
     taps(weights[IN], hidden, 0, 3, None)
-    got.second(QKV)
     got.complete(PROJ)
     g = dot(cot[...], joined(weights[PROJ], 0), 1, 0).astype(BF16)
     for h in range(HEADS):
@@ -945,6 +949,8 @@
         round3.append(mail.send(mod_s, mod_r.at[at.s], dev))
     kv_r[at.s] = kv_s[...]
     mod_r[at.s] = mod_s[...]
+    got.near(QKV)
+    got.second(QKV)
     got.fourth(OUT)
     got.third(QKV)
     for cp in round3 + stat1:

time: 274 us -> 267 us (0.974)
  Pallas kernels: 273 us -> 266 us
    pallas_call x1, Pallas kernels: 105 us -> 99.7 us  [attention_call(): pl.pallas_call(functools.partial(attention_kernel, n_sp, 1024), out_shape...]
where the time goes in v8:
time: 267 us
  Pallas kernels  266 us (100%)
    pallas_call x1, Pallas kernels, attention_call(): pl.pallas_call(functools.partial(attention_kernel, n_sp, 1024), out_shape...  99.7 us
    pallas_call x1, Pallas kernels, forward_call(): pl.pallas_call(functools.partial(forward_kernel, nz, width, dims), out_sh...  82.7 us
    pallas_call x1, Pallas kernels, backward_call(): pl.pallas_call(functools.partial(backward_kernel, nz, width), out_shape=[...  79.3 us

profile of v8, /device:TPU:0, one launch (start us, length us, event | category | flops | bytes accessed | tf_op | source)
XLA Modules:
  0.0 266.9 jit_solution(873587200884879170)
XLA Ops:
  0.6 82.7 %forward.1 = (bf16[4,1,512,128]{3,2,1,0:T(8,128)(2,1)}, bf16[4,9,512,128]{3,2,1,0:T(8,128)(2,1)}, bf16[4,9,512,128]{3,2,1,0:T(8,128)(2,1)}, bf16[4,1,1536,128]{3...) custom-call(bf16[1,64,128]{2,1,0:T(8,128)(2,1)} %bitcast.38, ...), custom_call_target="tpu_custom_call" | custom-call | tf_op jit(solution)/shard_map/forward/pallas_call | solution.py:1022
  83.3 99.7 %attention.1 = (bf16[8,256,128]{2,1,0:T(8,128)(2,1)}, bf16[8,256,128]{2,1,0:T(8,128)(2,1)}, bf16[8,512,128]{2,1,0:T(8,128)(2,1)}, bf16[8,128,128]{2,1,0:T(8,128)(2,1)}) custom-call(bf16[8,512,128]{2,1,0:T(8,128)(2,1)} %get-tuple-element.63.kv, bf16[8,256,128]{2,1,0:T(8,128)(2,1)} %get-tuple-element.64.qin, bf16[8,256,128]{2,1,0:T(8,128)(2,1)} %get-tuple-element.65.gin, ...), custom_call_target="tpu_custom_call" | custom-call | tf_op jit(solution)/shard_map/attention/pallas_call | solution.py:658
  183.0 79.3 %backward.1 = (bf16[512,512]{1,0:T(8,128)(2,1)}, f32[512,512]{1,0:T(8,128)}, f32[9,64,128]{2,1,0:T(8,128)}, f32[9,64,128]{2,1,0:T(8,128)}, f32[1,256,128]{2,1,0:...) custom-call(bf16[8,256,128]{2,1,0:T(8,128)(2,1)} %get-tuple-element., ...), custom_call_target="tpu_custom_call" | custom-call | tf_op jit(solution)/shard_map/backward/pallas_call | solution.py:1453
  262.3 4.4 %emit.1 = (bf16[512,512]{1,0:T(8,128)(2,1)}, f32[512,512]{1,0:T(8,128)}, f32[1,2048]{1,0:T(1,128)}, f32[16,2048]{1,0:T(8,128)}, f32[9,64,128]{2,1,0:T(8,128)}, /...) custom-call(bf16[512,512]{1,0:T(8,128)(2,1)} %get-tuple-element.92.r, ...), custom_call_target="tpu_custom_call" | custom-call | tf_op jit(solution)/shard_map/emit/pallas_call | solution.py:1520

commit v9 on v8

--- a/solution.py
+++ b/solution.py
@@ -587,7 +587,7 @@
         kc, vc = k_s[cols, :], v_s[cols, :]
         zero = jnp.zeros((d, n), F32)
         dk, dv = lax.fori_loop(
-            0, n_sp, lambda o, acc: block(o, cols, kc, vc, acc[0], acc[1], fresh), (zero, zero), unroll=4
+            0, n_sp, lambda o, acc: block(o, cols, kc, vc, acc[0], acc[1], fresh), (zero, zero), unroll=8
         )
         return both(dk, dv)
 
@@ -624,7 +624,7 @@
 
         return acc
 
-    grads = both(*lax.fori_loop(0, n_sp, last, (zero, zero)))
+    grads = both(*lax.fori_loop(0, n_sp, last, (zero, zero), unroll=2))
     for core in range(2):
         dkv_s[2 * at.z + core] = grads[core * px : (core + 1) * px]
     sib = at.sib[1]
@@ -772,12 +772,12 @@
     chunks, refs = refs[:na], refs[na:]
     x, cot, temb, cap, w_emb, w_cap, gains, biases = refs[:8]
     outs, refs = refs[8 : 8 + na], refs[8 + na :]
-    hidden_o, a0_o, res_o, a1_o, g_o, normed, kv, qf = refs[:8]
+    hidden_o, a0_o, res_o, a1_o, g_o, normed_o, kv_o, qf_o = refs[:8]
     st0, st1, st2, rows, ca, cb, ra, rb, ha, hb, kv_all, cap_all, emb_all = refs[8:21]
     refs = refs[21:]
     weights, refs = refs[:na], refs[na:]
     (ssem, rsem, lsem, msend, mrecv, g_s, emb, affine, mine, every, edge_s, xa, xb, ca_s, cb_s, ha_s, hb_s, ra_s, rb_s,
-     aff_s, emb_s, cap_s, part, part_r, kv_s, kv_r, mod_s, mod_r, acts, hidden, res) = refs
+     aff_s, emb_s, cap_s, part, part_r, kv_s, kv_r, mod_s, mod_r, acts, hidden, res, normed, kv, qf) = refs
     n_sp = 2 * nz
     at = Place()
     line = [at.rp(k, n_sp) for k in range(1, n_sp)]
@@ -986,7 +986,11 @@
     for h in range(HEADS):
         lanes = slice(h * d, (h + 1) * d)
         kv[h] = jnp.concatenate([k[:, lanes], v[:, lanes]], axis=1)
-        qf[h] = fold(q[:, lanes])
+    copy(kv, kv_o)
+    for h in range(HEADS):
+        qf[h] = fold(q[:, h * d : (h + 1) * d])
+    copy(qf, qf_o)
+    copy(normed, normed_o)
     restore(2, ra_s, rb_s, ra, rb)
     st0[...] = every[0]
     st1[...] = every[1]
@@ -1023,12 +1027,12 @@
         functools.partial(forward_kernel, nz, width, dims),
         out_shape=[jax.ShapeDtypeStruct(s, ty) for s, ty in outs],
         in_specs=[ANY] * na + [VM, VM, VM, ANY] + [VM] * 4,
-        out_specs=[ANY] * (na + 5) + [VM] * (len(outs) - na - 5),
+        out_specs=[ANY] * (na + 8) + [VM] * (len(outs) - na - 8),
         scratch_shapes=[vm(s, ty) for s, ty in big]
         + [
             pltpu.SemaphoreType.DMA((na, Gather.copies(nz))),
             pltpu.SemaphoreType.DMA((na, Gather.copies(nz))),
-            pltpu.SemaphoreType.DMA((2 * na + 6,)),
+            pltpu.SemaphoreType.DMA((2 * na + 9,)),
             pltpu.SemaphoreType.DMA((FORWARD_MAIL,)),
             pltpu.SemaphoreType.DMA((FORWARD_MAIL,)),
             vm((HEADS, px // 2, d2), BF16), vm((4, 8, e), F32), vm((8, 128), F32),
@@ -1040,6 +1044,7 @@
             vm((4, tokens + 8, 128), F32), vm((4, tokens + 8, 128), F32),
             vm((tokens, 128), BF16), vm((n_sp, tokens, 128), BF16), vm((8, 128), F32), vm((n_sp, 8, 128), F32),
             vm((2, 3, padded, c), BF16), vm((px, c), F32), vm((px, c), F32),
+            vm((px, c), BF16), vm((HEADS, px, d2), BF16), vm((HEADS, px // 2, d2), BF16),
         ],
         compiler_params=params(cid),
         name="forward",
@@ -1186,13 +1191,13 @@
     hbm, refs = refs[:BIG], refs[BIG:]
     w_in, w_out = refs[:2]
     (st0, st1, st2, rows, ca, cb, ra, rb, ha, hb, dt_all, cap_all, emb_all, w_emb, w_cap, temb) = refs[2:18]
-    output, image_grad, s_in, s_out, s_small, g_temb, g_cap, g_wemb, g_wcap, g_aff = refs[18:28]
+    output_o, image_o, s_in, s_out, s_small, g_temb, g_cap, g_wemb, g_wcap, g_aff = refs[18:28]
     refs = refs[28:]
     big, refs = refs[:BIG], refs[BIG:]
     bufs = [dict(zip(Reducer.NAMES, refs[8 * a : 8 * a + 8])) for a in range(3)]
     (bsem, gsend, grecv, msend, mrecv, ring, rsem, g3, gt, acc, ng, pre_grad, res_grad,
      mine, every, edge_s, na, nb, pa, pb, tg_s, tg_r, mod_s, mod_r,
-     gc_s, gc_r, pe_s, pe_r, gs_s, gs_r, ps_s, ps_r, aff_s, aff_r) = refs[24:]
+     gc_s, gc_r, pe_s, pe_r, gs_s, gs_r, ps_s, ps_r, aff_s, aff_r, output, image_grad, osem) = refs[24:]
     n_sp = 2 * nz
     at = Place()
     line = [at.rp(k, n_sp) for k in range(1, n_sp)]
@@ -1200,11 +1205,10 @@
     greet(line + grid)
     loads = []
     for j in range(BIG):
-        cp = pltpu.make_async_copy(hbm[j], big[j], bsem.at[j])
+        loads.append(pltpu.make_async_copy(hbm[j], big[j], bsem.at[j]))
+    for cp in loads[:8]:
         cp.start()
-        loads.append(cp)
     of, qf, dkv, w_qkv, w_proj, res, cot, normed, a3_out, hidden, a3_in, x = big
-    ring_start(w_out, ring, rsem)
     mail = Mail(msend, mrecv)
     red = Reducer(at, nz, [(s_out, bufs[0]), (s_small, bufs[1]), (s_in, bufs[2])], gsend, grecv)
     px, c = res.shape
@@ -1229,6 +1233,9 @@
 
     for j in range(8):
         loads[j].wait()
+    for cp in loads[8:]:
+        cp.start()
+    ring_start(w_out, ring, rsem)
     unfold = lambda v: jnp.concatenate([v[:, :d], v[:, d:]], axis=0)
     att = jnp.concatenate([unfold(of[h]) for h in range(HEADS)], axis=1)
     pg = jnp.concatenate(
@@ -1255,6 +1262,8 @@
             small[j % 2, b, 0, j // 2, cols:] = go[j * (c // n_sp) : (j + 1) * (c // n_sp), lanes]
     red.add(1, 0, 1)
     output[...] = (res[...] + dot(att, wp, 1, 1)).astype(BF16)
+    handed = [pltpu.make_async_copy(output, output_o, osem.at[0]), pltpu.make_async_copy(image_grad, image_o, osem.at[1])]
+    handed[0].start()
 
     first = 2 * lax.rem(at.s, nz)
     value = lax.div(at.s, nz)
@@ -1403,6 +1412,7 @@
     aff_r[at.i] = aff_s[at.i]
     total = group_total(t0 * gain0) / members
     image_grad[...] = res_grad[...] + inverse0 * (acc[...] * gain0 - total[0:1] - hat * total[1:2])
+    handed[1].start()
     for g in (2, 3):
         red.run(3, g)
         red.run(2, g + 3)
@@ -1431,6 +1441,8 @@
     g_cap[...] = jnp.concatenate([gs_r[j] for j in range(4)], axis=1)
     g_temb[...] = jnp.concatenate([ps_r[j] for j in range(4)], axis=1) * silu_slope(temb[...].astype(F32))
     g_aff[...] = aff_r[0] + aff_r[1] + aff_r[2] + aff_r[3]
+    for cp in handed:
+        cp.wait()
     for cp in mail.sent:
         cp.wait_send()
 
@@ -1454,7 +1466,7 @@
         functools.partial(backward_kernel, nz, width),
         out_shape=[jax.ShapeDtypeStruct(s, ty) for s, ty in outs],
         in_specs=[ANY] * (len(big) + 2) + [VM] * len(small),
-        out_specs=[VM] * len(outs),
+        out_specs=[ANY] * 2 + [VM] * (len(outs) - 2),
         scratch_shapes=[vm(v.shape, v.dtype) for v in big]
         + Reducer.buffers(nz, 9, r) + Reducer.buffers(nz, 1, rs) + Reducer.buffers(nz, 9, r)
         + [
@@ -1476,6 +1488,7 @@
             vm((4, share, e), F32), vm((4, share, e), F32),
             vm((4, 8, e), F32), vm((4, 8, e), F32),
             vm((4, 8, 128), F32), vm((4, 8, 128), F32),
+            vm((px, c), BF16), vm((px, c), F32), pltpu.SemaphoreType.DMA((2,)),
         ],
         compiler_params=params(cid),
         name="backward",

time: 267 us -> 266 us (level)
  no operation moved by 1% of the time
where the time goes in v9:
time: 266 us
  Pallas kernels  265 us (100%)
    pallas_call x1, Pallas kernels, attention_call(): pl.pallas_call(functools.partial(attention_kernel, n_sp, 1024), out_shape...  99.1 us
    pallas_call x1, Pallas kernels, forward_call(): pl.pallas_call(functools.partial(forward_kernel, nz, width, dims), out_sh...  83.1 us
    pallas_call x1, Pallas kernels, backward_call(): pl.pallas_call(functools.partial(backward_kernel, nz, width), out_shape=[...  78.6 us

profile of v9, /device:TPU:0, one launch (start us, length us, event | category | flops | bytes accessed | tf_op | source)
XLA Modules:
  0.0 266.1 jit_solution(15651353583511187257)
XLA Ops:
  0.6 83.1 %forward.1 = (bf16[4,1,512,128]{3,2,1,0:T(8,128)(2,1)}, bf16[4,9,512,128]{3,2,1,0:T(8,128)(2,1)}, bf16[4,9,512,128]{3,2,1,0:T(8,128)(2,1)}, bf16[4,1,1536,128]{3...) custom-call(bf16[1,64,128]{2,1,0:T(8,128)(2,1)} %bitcast.38, ...), custom_call_target="tpu_custom_call" | custom-call | tf_op jit(solution)/shard_map/forward/pallas_call | solution.py:1026
  83.7 99.1 %attention.1 = (bf16[8,256,128]{2,1,0:T(8,128)(2,1)}, bf16[8,256,128]{2,1,0:T(8,128)(2,1)}, bf16[8,512,128]{2,1,0:T(8,128)(2,1)}, bf16[8,128,128]{2,1,0:T(8,128)(2,1)}) custom-call(bf16[8,512,128]{2,1,0:T(8,128)(2,1)} %get-tuple-element.63.kv, bf16[8,256,128]{2,1,0:T(8,128)(2,1)} %get-tuple-element.64.qin, bf16[8,256,128]{2,1,0:T(8,128)(2,1)} %get-tuple-element.65.gin, ...), custom_call_target="tpu_custom_call" | custom-call | tf_op jit(solution)/shard_map/attention/pallas_call | solution.py:658
  182.9 78.6 %backward.1 = (bf16[512,512]{1,0:T(8,128)(2,1)}, f32[512,512]{1,0:T(8,128)}, f32[9,64,128]{2,1,0:T(8,128)}, f32[9,64,128]{2,1,0:T(8,128)}, f32[1,256,128]{2,1,0:...) custom-call(bf16[8,256,128]{2,1,0:T(8,128)(2,1)} %get-tuple-element., ...), custom_call_target="tpu_custom_call" | custom-call | tf_op jit(solution)/shard_map/backward/pallas_call | solution.py:1465
  261.5 4.4 %emit.1 = (bf16[512,512]{1,0:T(8,128)(2,1)}, f32[512,512]{1,0:T(8,128)}, f32[1,2048]{1,0:T(1,128)}, f32[16,2048]{1,0:T(8,128)}, f32[9,64,128]{2,1,0:T(8,128)}, /...) custom-call(bf16[512,512]{1,0:T(8,128)(2,1)} %get-tuple-element.92.r, ...), custom_call_target="tpu_custom_call" | custom-call | tf_op jit(solution)/shard_map/emit/pallas_call | solution.py:1533

commit v10 on v9

--- a/solution.py
+++ b/solution.py
@@ -809,7 +809,7 @@
     def publish(j, v, edges):
         pair = channel_stats(v)
         put_rows(mine.at[j], pair)
-        out = []
+        out = [mail.send(mine.at[j], every.at[j, at.s], dev) for dev in line]
         for ref, above, below in edges:
             if ref is None:
                 edge_s[j - 1, 0] = (v[px - width :] - pair[0]).astype(BF16)
@@ -819,8 +819,6 @@
             else:
                 out.append(mail.send(ref.at[px - width :], above, line[0]))
                 out.append(mail.send(ref.at[:width], below, line[-1]))
-        for dev in line:
-            out.append(mail.send(mine.at[j], every.at[j, at.s], dev))
         every[j, at.s] = mine[j]
         return out
 
@@ -945,7 +943,6 @@
     mod_s[...] = total[tokens:]
     round3 = []
     for dev in line:
-        round3.append(mail.send(kv_s, kv_r.at[at.s], dev))
         round3.append(mail.send(mod_s, mod_r.at[at.s], dev))
     kv_r[at.s] = kv_s[...]
     mod_r[at.s] = mod_s[...]
@@ -955,7 +952,7 @@
     got.third(QKV)
     for cp in round3 + stat1:
         cp.wait_recv()
-    kv_all[...] = kv_r[...]
+    round_k = [mail.send(kv_s, kv_r.at[at.s], dev) for dev in line]
     mod = jnp.concatenate([mod_r[j][0:1] for j in range(n_sp)], axis=1)
     rows[1, 2:3] = 1.0 + mod[:, :c]
     rows[1, 3:4] = mod[:, c:]
@@ -975,7 +972,7 @@
     copy(weights[QKV], outs[QKV])
     wq = joined(weights[QKV], 0)
 
-    for cp in stat2:
+    for cp in stat2[: n_sp - 1]:
         cp.wait_recv()
     center, inverse = combine_stats(every.at[2], px)
     n = ((res[...] - center) * (inverse * rows[2, 0:1]) + rows[2, 1:2]).astype(BF16)
@@ -991,6 +988,9 @@
         qf[h] = fold(q[:, h * d : (h + 1) * d])
     copy(qf, qf_o)
     copy(normed, normed_o)
+    for cp in stat2[n_sp - 1 :] + round_k:
+        cp.wait_recv()
+    kv_all[...] = kv_r[...]
     restore(2, ra_s, rb_s, ra, rb)
     st0[...] = every[0]
     st1[...] = every[1]

time: 266 us -> 265 us (level)
    pallas_call x1, Pallas kernels: 83.1 us -> 79.7 us  [forward_call(): pl.pallas_call(functools.partial(forward_kernel, nz, width, dims), out_sh...]
where the time goes in v10:
time: 265 us; the launch traced here: 264 us
  Pallas kernels  263 us (99%)
    pallas_call x1, Pallas kernels, attention_call(): pl.pallas_call(functools.partial(attention_kernel, n_sp, 1024), out_shape...  101 us
    pallas_call x1, Pallas kernels, forward_call(): pl.pallas_call(functools.partial(forward_kernel, nz, width, dims), out_sh...  79.7 us
    pallas_call x1, Pallas kernels, backward_call(): pl.pallas_call(functools.partial(backward_kernel, nz, width), out_shape=[...  78.4 us

profile of v10, /device:TPU:0, one launch (start us, length us, event | category | flops | bytes accessed | tf_op | source)
XLA Modules:
  0.0 264.3 jit_solution(2343878312582180631)
XLA Ops:
  0.6 79.7 %forward.1 = (bf16[4,1,512,128]{3,2,1,0:T(8,128)(2,1)}, bf16[4,9,512,128]{3,2,1,0:T(8,128)(2,1)}, bf16[4,9,512,128]{3,2,1,0:T(8,128)(2,1)}, bf16[4,1,1536,128]{3...) custom-call(bf16[1,64,128]{2,1,0:T(8,128)(2,1)} %bitcast.38, ...), custom_call_target="tpu_custom_call" | custom-call | tf_op jit(solution)/shard_map/forward/pallas_call | solution.py:1026
  80.3 100.9 %attention.1 = (bf16[8,256,128]{2,1,0:T(8,128)(2,1)}, bf16[8,256,128]{2,1,0:T(8,128)(2,1)}, bf16[8,512,128]{2,1,0:T(8,128)(2,1)}, bf16[8,128,128]{2,1,0:T(8,128)(2,1)}) custom-call(bf16[8,512,128]{2,1,0:T(8,128)(2,1)} %get-tuple-element.63.kv, bf16[8,256,128]{2,1,0:T(8,128)(2,1)} %get-tuple-element.64.qin, bf16[8,256,128]{2,1,0:T(8,128)(2,1)} %get-tuple-element.65.gin, ...), custom_call_target="tpu_custom_call" | custom-call | tf_op jit(solution)/shard_map/attention/pallas_call | solution.py:658
  181.2 78.4 %backward.1 = (bf16[512,512]{1,0:T(8,128)(2,1)}, f32[512,512]{1,0:T(8,128)}, f32[9,64,128]{2,1,0:T(8,128)}, f32[9,64,128]{2,1,0:T(8,128)}, f32[1,256,128]{2,1,0:...) custom-call(bf16[8,256,128]{2,1,0:T(8,128)(2,1)} %get-tuple-element., ...), custom_call_target="tpu_custom_call" | custom-call | tf_op jit(solution)/shard_map/backward/pallas_call | solution.py:1465
  259.7 4.4 %emit.1 = (bf16[512,512]{1,0:T(8,128)(2,1)}, f32[512,512]{1,0:T(8,128)}, f32[1,2048]{1,0:T(1,128)}, f32[16,2048]{1,0:T(8,128)}, f32[9,64,128]{2,1,0:T(8,128)}, /...) custom-call(bf16[512,512]{1,0:T(8,128)(2,1)} %get-tuple-element.92.r, ...), custom_call_target="tpu_custom_call" | custom-call | tf_op jit(solution)/shard_map/emit/pallas_call | solution.py:1533
